TPU v7x, 32 devices: a whole 2x2x4 slice. The times are simulated.
32 devices in a mesh: dp: 8 (over y, x, core), mp: 4 (over z).
Axes of the slice: x: 2, y: 2, z: 4, core: 2. Of those that a mesh axis runs over, the one named last changes fastest.
Arguments:
- inputs: bfloat16 [2, 10240, 1024], P(None, 'dp', 'mp'), may hold values from -6 to 6
- cotangent: bfloat16 [2, 10240, 1024], P(None, 'dp', 'mp'), may hold values from -6 to 6
- boundary_flags: int32 [2, 10240], P(None, 'dp'), may hold values from 0 to 1, as said below
- segment_ids: int32 [2, 10240], P(None, 'dp'), may hold values from 0 to 3, as said below
- mamba_norm: bfloat16 [2, 1024], replicated, may hold values from 0.5 to 1.5
- mamba_z: bfloat16 [2, 1024, 2048], P(None, 'dp', 'mp'), may hold values from -0.1875 to 0.1875
- mamba_x: bfloat16 [2, 1024, 2048], P(None, 'dp', 'mp'), may hold values from -0.1875 to 0.1875
- mamba_bc: bfloat16 [2, 1024, 256], P(None, 'dp'), may hold values from -0.1875 to 0.1875
- mamba_dt: bfloat16 [2, 1024, 32], P(None, 'dp', 'mp'), may hold values from -0.1875 to 0.1875
- mamba_conv_x: bfloat16 [2, 4, 2048], replicated, may hold values from -3 to 3
- mamba_conv_bc: bfloat16 [2, 4, 256], replicated, may hold values from -3 to 3
- mamba_dt_bias: bfloat16 [2, 32], replicated, may hold values from -5 to -2
- mamba_a_log: bfloat16 [2, 32], replicated, may hold values from 0 to 2.5
- mamba_skip: bfloat16 [2, 32], replicated, may hold values from 0.5 to 1.5
- mamba_gate_norm: bfloat16 [2, 2048], replicated, may hold values from 0.5 to 1.5
- mamba_out: bfloat16 [2, 2048, 1024], P(None, 'mp', 'dp'), may hold values from -0.125 to 0.125
- router_qk: bfloat16 [2, 1024, 1024], P(None, 'dp', 'mp'), may hold values from -0.1875 to 0.1875
- group_up: bfloat16 [1024, 1536], P('dp', 'mp'), may hold values from -0.1875 to 0.1875
- group_down: bfloat16 [1536, 1024], P('dp', 'mp'), may hold values from -0.15625 to 0.15625
- attn_norms: bfloat16 [2, 1536], replicated, may hold values from 0.5 to 1.5
- attn_qkv: bfloat16 [3, 1536, 1536], P(None, 'dp', 'mp'), may hold values from -0.15625 to 0.15625
- attn_out: bfloat16 [1536, 1536], P('mp', 'dp'), may hold values from -0.625 to 0.625
- ffn_gate_up: bfloat16 [2, 1536, 4096], P(None, 'dp', 'mp'), may hold values from -0.15625 to 0.15625
- ffn_down: bfloat16 [4096, 1536], P('mp', 'dp'), may hold values from -0.09375 to 0.09375
Outputs:
- outputs: bfloat16 [2, 10240, 1024], P(None, 'dp', 'mp')
- grad_inputs: float32 [2, 10240, 1024], P(None, 'dp', 'mp')
- grad_mamba_norm: float32 [2, 1024], replicated
- grad_mamba_z: float32 [2, 1024, 2048], P(None, 'dp', 'mp')
- grad_mamba_x: float32 [2, 1024, 2048], P(None, 'dp', 'mp')
- grad_mamba_bc: float32 [2, 1024, 256], P(None, 'dp')
- grad_mamba_dt: float32 [2, 1024, 32], P(None, 'dp', 'mp')
- grad_mamba_conv_x: float32 [2, 4, 2048], replicated
- grad_mamba_conv_bc: float32 [2, 4, 256], replicated
- grad_mamba_dt_bias: float32 [2, 32], replicated
- grad_mamba_a_log: float32 [2, 32], replicated
- grad_mamba_skip: float32 [2, 32], replicated
- grad_mamba_gate_norm: float32 [2, 2048], replicated
- grad_mamba_out: float32 [2, 2048, 1024], P(None, 'mp', 'dp')
- grad_router_qk: float32 [2, 1024, 1024], P(None, 'dp', 'mp')
- grad_group_up: float32 [1024, 1536], P('dp', 'mp')
- grad_group_down: float32 [1536, 1024], P('dp', 'mp')
- grad_attn_norms: float32 [2, 1536], replicated
- grad_attn_qkv: float32 [3, 1536, 1536], P(None, 'dp', 'mp')
- grad_attn_out: float32 [1536, 1536], P('mp', 'dp')
- grad_ffn_gate_up: float32 [2, 1536, 4096], P(None, 'dp', 'mp')
- grad_ffn_down: float32 [4096, 1536], P('mp', 'dp')
Inputs may be any that keep to these rules, and one draw needn't show every extreme that they name: `boundary_flags`: 1 at the first byte of every item; a sequence (1280 bytes of one micro-batch at one index of dp) has at most 320 ones, and in every micro-batch one sequence has exactly 320. `segment_ids`: each sequence of 1280 bytes packs 4 items numbered 0 to 3 in order, one of them 4 * 256 bytes long.
All inputs are finite; a program needn't handle non-finite values.
Results may differ from a plain program's by a relative error of at most 0.028.
Values may be sent and summed in bfloat16 or wider, within the bound.
No kernel may reach another device: no remote copies, remote signals or barrier semaphores. Data moves between devices by JAX's collectives and lax.ppermute only.
A program may use at most 448 MiB of HBM per device.

v0:
```python
import jax
import jax.numpy as jnp
from jax import lax
from jax.sharding import PartitionSpec as P

DM = 1536
AHEADS = 24
CAP = 320


EPSILON = 1e-06
HIGHEST = lax.Precision.HIGHEST


def rms_scale(values, gain):
    return values * lax.rsqrt(jnp.mean(values * values, axis=-1, keepdims=True) + EPSILON) * gain


def causal_conv(values, kernel, segment):
    tap_count = kernel.shape[0]
    length = values.shape[0]
    result = values * kernel[tap_count - 1]
    for offset in range(1, tap_count):
        shifted = jnp.concatenate(
            [jnp.zeros((offset, values.shape[1]), values.dtype), values[: length - offset]], 0
        )
        shifted_seg = jnp.concatenate(
            [jnp.full((offset,), -1, jnp.int32), segment[: length - offset]], 0
        )
        result = (
            result
            + jnp.where((shifted_seg == segment)[:, None], shifted, 0.0)
            * kernel[tap_count - 1 - offset]
        )
    return result


def state_scan(inputs, step_sizes, decays, in_map, out_map, segment):
    length, head_count, head_size = inputs.shape
    nstate = in_map.shape[1]
    blocksize = 256
    block_count = length // blocksize
    lower_mask = jnp.tril(jnp.ones((blocksize, blocksize), jnp.bool_))

    def scan_block(carry, block_in):
        states, last_seg = carry
        block_x, block_step, block_decay, block_in_map, block_out_map, block_seg = block_in
        cumlog = jnp.cumsum(block_decay, axis=0)
        visible = ((block_seg[:, None] == block_seg[None, :]) & lower_mask)[:, :, None]
        log_gaps = cumlog[:, None, :] - cumlog[None, :, :]
        factors = jnp.where(visible, jnp.exp(jnp.where(visible, log_gaps, 0.0)), 0.0)
        intersection = jnp.dot(block_out_map, block_in_map.T, precision=HIGHEST)
        weights = intersection[:, :, None] * factors * block_step[None, :, :]
        outputs = jnp.einsum("ijh,jhp->ihp", weights, block_x, precision=HIGHEST)
        carried = (block_seg == last_seg).astype(block_x.dtype)
        reach_back = jnp.exp(cumlog) * carried[:, None]
        outputs = (
            outputs
            + jnp.einsum("in,hpn->ihp", block_out_map, states, precision=HIGHEST)
            * reach_back[:, :, None]
        )
        end_seg = block_seg[-1]
        to_end = (
            jnp.where((block_seg == end_seg)[:, None], jnp.exp(cumlog[-1][None, :] - cumlog), 0.0)
            * block_step
        )
        new_terms = jnp.einsum("jh,jn,jhp->hpn", to_end, block_in_map, block_x, precision=HIGHEST)
        kept_part = jnp.exp(cumlog[-1]) * (last_seg == end_seg).astype(block_x.dtype)
        states = states * kept_part[:, None, None] + new_terms
        return ((states, end_seg), outputs)

    def by_block(array):
        return array.reshape((block_count, blocksize) + array.shape[1:])

    start_carry = (
        jnp.zeros((head_count, head_size, nstate), inputs.dtype),
        jnp.array(-1, jnp.int32),
    )
    end_carry, outputs = lax.scan(
        jax.checkpoint(scan_block),
        start_carry,
        (
            by_block(inputs),
            by_block(step_sizes),
            by_block(decays),
            by_block(in_map),
            by_block(out_map),
            by_block(segment),
        ),
    )
    return outputs.reshape(length, head_count, head_size)


def gated_mixer(
    z_proj, x_proj, bc_proj, dt_proj, conv_x, conv_bc, dt_bias, decay_log, skip_gain, segment
):
    length = x_proj.shape[0]
    head_count = dt_proj.shape[1]
    head_size = x_proj.shape[1] // head_count
    nstate = bc_proj.shape[1] // 2
    conv_out = jax.nn.silu(causal_conv(x_proj, conv_x, segment))
    maps_all = jax.nn.silu(causal_conv(bc_proj, conv_bc, segment))
    step_sizes = jax.nn.softplus(dt_proj + dt_bias)
    decays = -jnp.exp(decay_log) * step_sizes
    inputs = conv_out.reshape(length, head_count, head_size)
    outputs = (
        state_scan(inputs, step_sizes, decays, maps_all[:, :nstate], maps_all[:, nstate:], segment)
        + skip_gain[None, :, None] * inputs
    )
    return outputs.reshape(length, head_count * head_size) * jax.nn.silu(z_proj)


def rotate_pairs(values, head_count):
    length = values.shape[0]
    head_size = values.shape[1] // head_count
    half_size = head_size // 2
    frequency = 10000.0 ** (-jnp.arange(half_size, dtype=values.dtype) * (2.0 / head_size))
    angles = jnp.arange(length, dtype=values.dtype)[:, None] * frequency[None, :]
    cosines = jnp.cos(angles)[:, None, :]
    sines = jnp.sin(angles)[:, None, :]
    pairs_in = values.reshape(length, head_count, head_size)
    first_half = pairs_in[..., :half_size]
    second_half = pairs_in[..., half_size:]
    turned = jnp.concatenate(
        [first_half * cosines - second_half * sines, first_half * sines + second_half * cosines], -1
    )
    return turned.reshape(length, head_count * head_size)


def attend_forward(queries, key_proj, value_proj, group_seg, head_count):
    length = queries.shape[0]
    head_size = queries.shape[1] // head_count
    query_rot = (
        rotate_pairs(queries, head_count)
        .astype(jnp.bfloat16)
        .reshape(length, head_count, head_size)
    )
    key_rot = (
        rotate_pairs(key_proj, head_count)
        .astype(jnp.bfloat16)
        .reshape(length, head_count, head_size)
    )
    value_low = value_proj.astype(jnp.bfloat16).reshape(length, head_count, head_size)
    places = jnp.arange(length)
    visible = (places[:, None] >= places[None, :]) & (group_seg[:, None] == group_seg[None, :])
    scores = jnp.einsum(
        "ihd,jhd->hij", query_rot, key_rot, preferred_element_type=jnp.float32
    ) * head_size ** (-0.5)
    scores = jnp.where(visible[None], scores, -1e30)
    probs = jax.nn.softmax(scores, axis=-1)
    weights_low = probs.astype(jnp.bfloat16)
    mixed = jnp.einsum("hij,jhd->ihd", weights_low, value_low, preferred_element_type=jnp.float32)
    mixed_low = mixed.astype(jnp.bfloat16).reshape(length, head_count * head_size)
    return (mixed_low, (query_rot, key_rot, value_low, probs, weights_low, visible, head_count))


def attend_backward(grad_mixed, memory):
    query_rot, key_rot, value_low, probs, weights_low, visible, head_count = memory
    length, heads_here, head_size = query_rot.shape
    scale = head_size ** (-0.5)
    grad_low = grad_mixed.astype(jnp.bfloat16).reshape(length, heads_here, head_size)
    grad_weights = jnp.einsum(
        "ihd,jhd->hij", grad_low, value_low, preferred_element_type=jnp.float32
    )
    grad_value = jnp.einsum(
        "hij,ihd->jhd", weights_low, grad_low, preferred_element_type=jnp.float32
    )
    inner = jnp.sum(grad_weights * probs, axis=-1, keepdims=True)
    grad_scores = jnp.where(visible[None], probs * (grad_weights - inner), 0.0).astype(jnp.bfloat16)
    grad_qrot = (
        jnp.einsum("hij,jhd->ihd", grad_scores, key_rot, preferred_element_type=jnp.float32) * scale
    )
    grad_krot = (
        jnp.einsum("hij,ihd->jhd", grad_scores, query_rot, preferred_element_type=jnp.float32)
        * scale
    )
    width = heads_here * head_size
    zeros_in = jnp.zeros((length, width), jnp.float32)
    turned, turn_back = jax.vjp(lambda values: rotate_pairs(values, head_count), zeros_in)
    (grad_query,) = turn_back(grad_qrot.reshape(length, width))
    (grad_key,) = turn_back(grad_krot.reshape(length, width))
    return (grad_query, grad_key, grad_value.reshape(length, width))


def pair_dots(queries, key_proj):
    previous = jnp.concatenate(
        [jnp.zeros((1, key_proj.shape[1]), key_proj.dtype), key_proj[:-1]], 0
    )
    return jnp.stack(
        [
            jnp.sum(queries * previous, axis=1),
            jnp.sum(queries * queries, axis=1),
            jnp.sum(previous * previous, axis=1),
        ],
        0,
    )


def boundary_prob(all_dots, starts):
    cosine = all_dots[0] * lax.rsqrt(all_dots[1] + EPSILON) * lax.rsqrt(all_dots[2] + EPSILON)
    return jnp.where(starts, 1.0, 0.5 * (1.0 - cosine))


def group_layout(flag_row, capacity):
    group_rank = jnp.cumsum(flag_row) - 1
    slot_ids = jnp.arange(capacity, dtype=jnp.int32)
    places = jnp.arange(flag_row.shape[0], dtype=jnp.int32)
    marked = (group_rank[None, :] == slot_ids[:, None]) & (flag_row[None, :] == 1)
    positions = jnp.sum(jnp.where(marked, places[None, :], 0), axis=1)
    slot_valid = jnp.any(marked, axis=1)
    return (group_rank, positions, slot_valid)


def smooth_groups(down_rows, group_probs):

    def combine(earlier, later):
        return (earlier[0] * later[0], later[0] * earlier[1] + later[1])

    decay_part = (1.0 - group_probs)[:, None]
    scanned = lax.associative_scan(combine, (decay_part, group_probs[:, None] * down_rows))
    return scanned[1]


def spread_groups(down_rows, prob_row, flag_row, group_rank, positions, slot_valid):
    group_probs = jnp.where(slot_valid, jnp.take(prob_row, positions), 1.0)
    smooth = smooth_groups(down_rows, group_probs)
    confidence = jnp.where(flag_row == 1, prob_row, 1.0 - prob_row)
    return confidence[:, None] * jnp.take(smooth, group_rank, axis=0)


def to_low(values):
    return values.astype(jnp.bfloat16)


def matmul(left, right):
    return jnp.dot(left, right, preferred_element_type=jnp.float32)


def left_product(left, right):
    return lax.dot_general(
        left, right, (((0,), (0,)), ((), ())), preferred_element_type=jnp.float32
    )


def right_product(left, right):
    return lax.dot_general(
        left, right, (((1,), (1,)), ((), ())), preferred_element_type=jnp.float32
    )


def widen(values):
    return lax.all_gather(values, "mp", axis=1, tiled=True)


def narrow(values):
    return lax.psum_scatter(values, "mp", scatter_dimension=1, tiled=True)


def fetch(
    mamba_z,
    mamba_x,
    mamba_bc,
    mamba_dt,
    mamba_out,
    router_qk,
    group_up,
    group_down,
    attn_qkv,
    attn_out,
    ffn_gate_up,
    ffn_down,
):
    return (
        lax.all_gather(mamba_z, "dp", axis=1, tiled=True),
        lax.all_gather(mamba_x, "dp", axis=1, tiled=True),
        lax.all_gather(mamba_bc, "dp", axis=1, tiled=True),
        lax.all_gather(mamba_dt, "dp", axis=1, tiled=True),
        lax.all_gather(mamba_out, "dp", axis=2, tiled=True),
        lax.all_gather(router_qk, "dp", axis=1, tiled=True),
        lax.all_gather(group_up, "dp", axis=0, tiled=True),
        lax.all_gather(group_down, "dp", axis=0, tiled=True),
        lax.all_gather(attn_qkv, "dp", axis=1, tiled=True),
        lax.all_gather(attn_out, "dp", axis=1, tiled=True),
        lax.all_gather(ffn_gate_up, "dp", axis=1, tiled=True),
        lax.all_gather(ffn_down, "dp", axis=1, tiled=True),
    )


def settle(grads):
    return (
        lax.psum_scatter(
            grads[0].astype(jnp.bfloat16), "dp", scatter_dimension=1, tiled=True
        ).astype(jnp.float32),
        lax.psum_scatter(
            grads[1].astype(jnp.bfloat16), "dp", scatter_dimension=1, tiled=True
        ).astype(jnp.float32),
        lax.psum_scatter(
            grads[2].astype(jnp.bfloat16), "dp", scatter_dimension=1, tiled=True
        ).astype(jnp.float32),
        lax.psum_scatter(
            grads[3].astype(jnp.bfloat16), "dp", scatter_dimension=1, tiled=True
        ).astype(jnp.float32),
        lax.psum_scatter(
            grads[4].astype(jnp.bfloat16), "dp", scatter_dimension=2, tiled=True
        ).astype(jnp.float32),
        lax.psum_scatter(
            grads[5].astype(jnp.bfloat16), "dp", scatter_dimension=1, tiled=True
        ).astype(jnp.float32),
        lax.psum_scatter(
            grads[6].astype(jnp.bfloat16), "dp", scatter_dimension=0, tiled=True
        ).astype(jnp.float32),
        lax.psum_scatter(
            grads[7].astype(jnp.bfloat16), "dp", scatter_dimension=0, tiled=True
        ).astype(jnp.float32),
        lax.psum_scatter(
            grads[8].astype(jnp.bfloat16), "dp", scatter_dimension=1, tiled=True
        ).astype(jnp.float32),
        lax.psum_scatter(
            grads[9].astype(jnp.bfloat16), "dp", scatter_dimension=1, tiled=True
        ).astype(jnp.float32),
        lax.psum_scatter(
            grads[10].astype(jnp.bfloat16), "dp", scatter_dimension=1, tiled=True
        ).astype(jnp.float32),
        lax.psum_scatter(
            grads[11].astype(jnp.bfloat16), "dp", scatter_dimension=1, tiled=True
        ).astype(jnp.float32),
    )


def accumulate(running, new_terms):
    if running is None:
        return tuple(new_terms)
    return tuple((a + b for a, b in zip(running, new_terms)))


def mamba_forward(residual, layer_index, big_weights, small_params, segment):
    mamba_z, mamba_x, mamba_bc, mamba_dt, mamba_out = big_weights
    norm_full, conv_x_own, conv_bc_full, bias_own, decay_own, skip_own, gate_own = small_params
    gathered = widen(to_low(residual))
    normed, norm_back = jax.vjp(rms_scale, gathered.astype(jnp.float32), norm_full[layer_index])
    normed_low = to_low(normed)

    def local_mix(z_proj, x_proj, bc_proj, dt_proj, conv_x, conv_bc, dt_bias, decay_log, skip_gain):
        return gated_mixer(
            z_proj,
            x_proj,
            bc_proj,
            dt_proj,
            conv_x,
            conv_bc,
            dt_bias,
            decay_log,
            skip_gain,
            segment,
        )

    gated, mix_back = jax.vjp(
        local_mix,
        matmul(normed_low, mamba_z[layer_index]),
        matmul(normed_low, mamba_x[layer_index]),
        matmul(normed_low, mamba_bc[layer_index]),
        matmul(normed_low, mamba_dt[layer_index]),
        conv_x_own[layer_index],
        conv_bc_full[layer_index],
        bias_own[layer_index],
        decay_own[layer_index],
        skip_own[layer_index],
    )
    full_width = gated.shape[1] * lax.axis_size("mp")
    square_sum = lax.psum(jnp.sum(gated * gated, axis=1), "mp")
    scale = lax.rsqrt(square_sum / full_width + EPSILON)
    gain = gate_own[layer_index]
    mixed_low = to_low(gated * scale[:, None] * gain)
    result = residual + narrow(matmul(mixed_low, mamba_out[layer_index]))
    return (result, (normed_low, mixed_low, norm_back, mix_back, gated, scale, gain))


def mamba_backward(gradient, layer_index, big_weights, memory, shard_index):
    mamba_z, mamba_x, mamba_bc, mamba_dt, mamba_out = big_weights
    normed_low, mixed_low, norm_back, mix_back, gated, scale, gain = memory
    spread = widen(to_low(gradient))
    grad_out = left_product(mixed_low, spread)
    grad_mixed = right_product(spread, mamba_out[layer_index])
    grad_gain = jnp.sum(grad_mixed * gated * scale[:, None], axis=0)
    weighted = grad_mixed * gain
    full_width = gated.shape[1] * lax.axis_size("mp")
    inner = lax.psum(jnp.sum(weighted * gated, axis=1), "mp")
    grad_gated = (
        scale[:, None] * weighted - gated * (scale * scale * scale * inner / full_width)[:, None]
    )
    pulled = mix_back(grad_gated)
    grad_z = to_low(pulled[0])
    grad_x = to_low(pulled[1])
    grad_bc = to_low(lax.psum(pulled[2].astype(jnp.bfloat16), "mp").astype(jnp.float32))
    grad_dt = to_low(pulled[3])
    grad_normed = (
        right_product(grad_z, mamba_z[layer_index])
        + right_product(grad_x, mamba_x[layer_index])
        + right_product(grad_dt, mamba_dt[layer_index])
    )
    column_count = grad_normed.shape[1] // lax.axis_size("mp")
    own_rows = lax.dynamic_slice_in_dim(
        mamba_bc[layer_index], shard_index * column_count, column_count, 0
    )
    own_block = lax.dynamic_slice_in_dim(
        grad_normed, shard_index * column_count, column_count, 1
    ) + right_product(grad_bc, own_rows)
    grad_normed = lax.dynamic_update_slice_in_dim(
        grad_normed, own_block, shard_index * column_count, 1
    )
    grad_in, grad_norm = norm_back(grad_normed)
    weight_grads = (
        left_product(normed_low, grad_z),
        left_product(normed_low, grad_x),
        left_product(normed_low, grad_bc),
        left_product(normed_low, grad_dt),
        grad_out,
    )
    small_grads = (grad_norm, pulled[4], pulled[5], pulled[6], pulled[7], pulled[8], grad_gain)
    return (gradient + narrow(grad_in), weight_grads, small_grads)


def trans_forward(hidden, group_seg, weights, norm_gains):
    attn_qkv, attn_out, ffn_gate_up, ffn_down, group_down = weights
    head_count = attn_qkv.shape[2] // (DM // AHEADS)
    first_norm, first_back = jax.vjp(
        rms_scale, widen(to_low(hidden)).astype(jnp.float32), norm_gains[0]
    )
    first_low = to_low(first_norm)
    attended_low, attn_memory = attend_forward(
        matmul(first_low, attn_qkv[0]),
        matmul(first_low, attn_qkv[1]),
        matmul(first_low, attn_qkv[2]),
        group_seg,
        head_count,
    )
    hidden = hidden + narrow(matmul(attended_low, attn_out))
    second_norm, second_back = jax.vjp(
        rms_scale, widen(to_low(hidden)).astype(jnp.float32), norm_gains[1]
    )
    second_low = to_low(second_norm)
    active, active_back = jax.vjp(
        lambda a, b: jax.nn.silu(a) * b,
        matmul(second_low, ffn_gate_up[0]),
        matmul(second_low, ffn_gate_up[1]),
    )
    active_low = to_low(active)
    hidden = hidden + narrow(matmul(active_low, ffn_down))
    third_in = widen(to_low(hidden))
    memory = (
        first_low,
        first_back,
        attn_memory,
        attended_low,
        second_low,
        second_back,
        active_back,
        active_low,
        third_in,
    )
    return (matmul(third_in, group_down), memory)


def trans_backward(grad_down, memory, weights):
    attn_qkv, attn_out, ffn_gate_up, ffn_down, group_down = weights
    (
        first_low,
        first_back,
        attn_memory,
        attended_low,
        second_low,
        second_back,
        active_back,
        active_low,
        third_in,
    ) = memory
    down_low = to_low(grad_down)
    grad_group_down = left_product(third_in, down_low)
    grad_hidden = narrow(right_product(down_low, group_down))
    spread = widen(to_low(grad_hidden))
    grad_ffn_down = left_product(active_low, spread)
    grad_gate, grad_upper = active_back(right_product(spread, ffn_down))
    grad_gate = to_low(grad_gate)
    grad_upper = to_low(grad_upper)
    grad_gate_up = jnp.stack(
        [left_product(second_low, grad_gate), left_product(second_low, grad_upper)]
    )
    grad_second, grad_norm_two = second_back(
        right_product(grad_gate, ffn_gate_up[0]) + right_product(grad_upper, ffn_gate_up[1])
    )
    grad_hidden = grad_hidden + narrow(grad_second)
    spread = widen(to_low(grad_hidden))
    grad_attn_out = left_product(attended_low, spread)
    pulled = attend_backward(right_product(spread, attn_out), attn_memory)
    lowered = [to_low(member) for member in pulled]
    grad_qkv = jnp.stack([left_product(first_low, member) for member in lowered])
    grad_first, grad_norm_one = first_back(
        right_product(lowered[0], attn_qkv[0])
        + right_product(lowered[1], attn_qkv[1])
        + right_product(lowered[2], attn_qkv[2])
    )
    grad_hidden = grad_hidden + narrow(grad_first)
    return (
        grad_hidden,
        (grad_qkv, grad_attn_out, grad_gate_up, grad_ffn_down, grad_group_down),
        jnp.stack([grad_norm_one, grad_norm_two]),
    )


def one_batch(residual, cot_row, flag_row, segment, fetched, small_params, norm_gains, shard_index):
    (
        mamba_z,
        mamba_x,
        mamba_bc,
        mamba_dt,
        mamba_out,
        router_qk,
        group_up,
        group_down,
        attn_qkv,
        attn_out,
        ffn_gate_up,
        ffn_down,
    ) = fetched
    big_weights = (mamba_z, mamba_x, mamba_bc, mamba_dt, mamba_out)
    trans_weights = (attn_qkv, attn_out, ffn_gate_up, ffn_down, group_down)
    starts = jnp.concatenate([jnp.ones((1,), jnp.bool_), segment[1:] != segment[:-1]])
    group_rank, positions, slot_valid = group_layout(flag_row, CAP)
    encoded, enc_memory = mamba_forward(
        residual.astype(jnp.float32), 0, big_weights, small_params, segment
    )
    shared = widen(to_low(encoded))
    queries = matmul(shared, router_qk[0])
    key_proj = matmul(shared, router_qk[1])
    partial_dots, dots_back = jax.vjp(pair_dots, queries, key_proj)
    all_dots = lax.psum(partial_dots, "mp")
    prob_row, prob_back = jax.vjp(lambda values: boundary_prob(values, starts), all_dots)
    group_rows = jnp.take(shared, positions, axis=0) * slot_valid[:, None].astype(jnp.bfloat16)
    group_seg = jnp.where(slot_valid, jnp.take(segment, positions), -1)
    down_rows, trans_memory = trans_forward(
        matmul(group_rows, group_up), group_seg, trans_weights, norm_gains
    )
    spread_out, spread_back = jax.vjp(
        lambda a, b: spread_groups(a, b, flag_row, group_rank, positions, slot_valid),
        down_rows,
        prob_row,
    )
    decoded, dec_memory = mamba_forward(encoded + spread_out, 1, big_weights, small_params, segment)
    gradient, dec_weights, dec_smalls = mamba_backward(
        cot_row.astype(jnp.float32), 1, big_weights, dec_memory, shard_index
    )
    grad_down, grad_probs = spread_back(gradient)
    grad_hidden, trans_grads, norm_grads = trans_backward(grad_down, trans_memory, trans_weights)
    hidden_low = to_low(grad_hidden)
    grad_up = left_product(group_rows, hidden_low)
    grad_rows = right_product(hidden_low, group_up) * slot_valid[:, None].astype(jnp.float32)
    grad_shared = jax.ops.segment_sum(grad_rows, positions, num_segments=shared.shape[0])
    (grad_dots,) = prob_back(lax.psum(grad_probs, "mp"))
    grad_query, grad_key = dots_back(grad_dots)
    grad_query = to_low(grad_query)
    grad_key = to_low(grad_key)
    grad_shared = (
        grad_shared
        + right_product(grad_query, router_qk[0])
        + right_product(grad_key, router_qk[1])
    )
    gradient = gradient + narrow(grad_shared)
    gradient, enc_weights, enc_smalls = mamba_backward(
        gradient, 0, big_weights, enc_memory, shard_index
    )
    mamba_grads = tuple(
        (jnp.stack([early, later]) for early, later in zip(enc_weights, dec_weights))
    )
    big_grads = mamba_grads + (
        jnp.stack([left_product(shared, grad_query), left_product(shared, grad_key)]),
        grad_up,
        trans_grads[4],
        trans_grads[0],
        trans_grads[1],
        trans_grads[2],
        trans_grads[3],
    )
    small_grads = tuple(
        (jnp.stack([early, later]) for early, later in zip(enc_smalls, dec_smalls))
    ) + (norm_grads,)
    return (decoded, gradient, big_grads, small_grads)


def per_device(
    inputs,
    cotangent,
    boundary_flags,
    segment_ids,
    mamba_norm,
    mamba_z,
    mamba_x,
    mamba_bc,
    mamba_dt,
    mamba_conv_x,
    mamba_conv_bc,
    mamba_dt_bias,
    mamba_a_log,
    mamba_skip,
    mamba_gate_norm,
    mamba_out,
    router_qk,
    group_up,
    group_down,
    attn_norms,
    attn_qkv,
    attn_out,
    ffn_gate_up,
    ffn_down,
):
    shard_index = lax.axis_index("mp")
    own_width = mamba_z.shape[2]
    head_count = mamba_dt.shape[2]
    small_params = (
        mamba_norm.astype(jnp.float32),
        lax.dynamic_slice_in_dim(mamba_conv_x, shard_index * own_width, own_width, 2).astype(
            jnp.float32
        ),
        mamba_conv_bc.astype(jnp.float32),
        lax.dynamic_slice_in_dim(mamba_dt_bias, shard_index * head_count, head_count, 1).astype(
            jnp.float32
        ),
        lax.dynamic_slice_in_dim(mamba_a_log, shard_index * head_count, head_count, 1).astype(
            jnp.float32
        ),
        lax.dynamic_slice_in_dim(mamba_skip, shard_index * head_count, head_count, 1).astype(
            jnp.float32
        ),
        lax.dynamic_slice_in_dim(mamba_gate_norm, shard_index * own_width, own_width, 1).astype(
            jnp.float32
        ),
    )
    norm_gains = attn_norms.astype(jnp.float32)
    fetched = None
    big_total = None
    small_total = None
    results = []
    input_grads = []
    for micro_index in range(inputs.shape[0]):
        fetched = fetch(
            mamba_z,
            mamba_x,
            mamba_bc,
            mamba_dt,
            mamba_out,
            router_qk,
            group_up,
            group_down,
            attn_qkv,
            attn_out,
            ffn_gate_up,
            ffn_down,
        )
        decoded, gradient, big_grads, small_grads = one_batch(
            inputs[micro_index],
            cotangent[micro_index],
            boundary_flags[micro_index],
            segment_ids[micro_index],
            fetched,
            small_params,
            norm_gains,
            shard_index,
        )
        results.append(decoded.astype(jnp.bfloat16))
        input_grads.append(gradient)
        big_total = accumulate(big_total, settle(big_grads))
        small_total = accumulate(small_total, small_grads)
    conv_x_full = lax.dynamic_update_slice_in_dim(
        jnp.zeros(mamba_conv_x.shape, jnp.float32), small_total[1], shard_index * own_width, 2
    )
    bias_full = lax.dynamic_update_slice_in_dim(
        jnp.zeros(mamba_dt_bias.shape, jnp.float32), small_total[3], shard_index * head_count, 1
    )
    decay_full = lax.dynamic_update_slice_in_dim(
        jnp.zeros(mamba_a_log.shape, jnp.float32), small_total[4], shard_index * head_count, 1
    )
    skip_full = lax.dynamic_update_slice_in_dim(
        jnp.zeros(mamba_skip.shape, jnp.float32), small_total[5], shard_index * head_count, 1
    )
    gate_full = lax.dynamic_update_slice_in_dim(
        jnp.zeros(mamba_gate_norm.shape, jnp.float32), small_total[6], shard_index * own_width, 1
    )
    summed = lax.psum(
        (
            small_total[0],
            conv_x_full,
            small_total[2],
            bias_full,
            decay_full,
            skip_full,
            gate_full,
            small_total[7],
        ),
        ("dp", "mp"),
    )
    return (
        jnp.stack(results),
        jnp.stack(input_grads),
        summed[0],
        big_total[0],
        big_total[1],
        big_total[2],
        big_total[3],
        summed[1],
        summed[2],
        summed[3],
        summed[4],
        summed[5],
        summed[6],
        big_total[4],
        big_total[5],
        big_total[6],
        big_total[7],
        summed[7],
        big_total[8],
        big_total[9],
        big_total[10],
        big_total[11],
    )


def solution(mesh):
    in_specs = (
        P(None, "dp", "mp"),
        P(None, "dp", "mp"),
        P(None, "dp"),
        P(None, "dp"),
        P(),
        P(None, "dp", "mp"),
        P(None, "dp", "mp"),
        P(None, "dp", None),
        P(None, "dp", "mp"),
        P(),
        P(),
        P(),
        P(),
        P(),
        P(),
        P(None, "mp", "dp"),
        P(None, "dp", "mp"),
        P("dp", "mp"),
        P("dp", "mp"),
        P(),
        P(None, "dp", "mp"),
        P("mp", "dp"),
        P(None, "dp", "mp"),
        P("mp", "dp"),
    )
    out_specs = (
        P(None, "dp", "mp"),
        P(None, "dp", "mp"),
        P(),
        P(None, "dp", "mp"),
        P(None, "dp", "mp"),
        P(None, "dp", None),
        P(None, "dp", "mp"),
        P(),
        P(),
        P(),
        P(),
        P(),
        P(),
        P(None, "mp", "dp"),
        P(None, "dp", "mp"),
        P("dp", "mp"),
        P("dp", "mp"),
        P(),
        P(None, "dp", "mp"),
        P("mp", "dp"),
        P(None, "dp", "mp"),
        P("mp", "dp"),
    )
    return jax.shard_map(
        per_device, mesh=mesh, in_specs=in_specs, out_specs=out_specs, check_vma=False
    )
```

profile of v0, /device:TPU:1, one launch (start us, length us, event | category | flops | bytes accessed | tf_op | source)
XLA Modules:
  0.0 4963.1 jit_solution(1198628380140920371)
XLA Ops:
  30.2 37.0 all-gather.54.cloned.1.call-done
  69.7 52.7 %all-gather.56.cloned.1.call-done = bf16[1,1280,1024]{2,1,0:T(8,128)(2,1)} async-done(((bf16[1,1280,256]{2,1,0:T(8,128)(2,1)}), bf16[1,1280,1024]{2,1,0:T(8,128)(2,1)}) %all-gather.56.cloned.1.call-update) | async-done | bytes 2621456 | tf_op jit(solution)/shard_map/all_gather | solution.py:252
  189.4 73.7 %while.186 = (s32[]{:T(128)}, f32[8,64,128]{2,1,0:T(8,128)S(1)}, s32[]{:T(128)}, f32[5,256,8,64]{1,3,2,0:T(8,128)}, f32[5,8,64,128]{3,2,1,0:T(8,128)}, /*index=5...) while((s32[]{:T(128)}, f32[8,64,128]{2,1,0:T(8,128)S(1)}, ...), condition=%wide.region_34.40_spmd.clone, body=%wide.region_31.39_spmd.clone.sunk | while | flops 909779712 | bytes 5254555 | solution.py:79
  278.9 73.3 %while.184 = (s32[]{:T(128)}, f32[8,64,128]{2,1,0:T(8,128)S(1)}, s32[]{:T(128)}, f32[5,256,8,64]{1,3,2,0:T(8,128)}, f32[5,8,64,128]{3,2,1,0:T(8,128)}, /*index=5...) while((s32[]{:T(128)}, f32[8,64,128]{2,1,0:T(8,128)S(1)}, ...), condition=%wide.region_4.6_spmd.clone, body=%wide.region_1.0_spmd.clone.sunk | while | flops 909779712 | bytes 5254555 | solution.py:79
  413.3 86.2 %reduce-scatter.61.cloned.1.call-done = f32[1280,256]{1,0:T(8,128)} async-done(((f32[1280,1024]{1,0:T(8,128)}), f32[1280,256]{1,0:T(8,128)}) %reduce-scatter.61.cloned.1.call-update) | async-done | bytes 1310736 | tf_op jit(solution)/shard_map/reduce_scatter | solution.py:256
  499.5 96.6 %reduce-scatter.53.cloned.1.call-done = f32[1280,256]{1,0:T(8,128)} async-done(((f32[1280,1024]{1,0:T(8,128)}), f32[1280,256]{1,0:T(8,128)}) %reduce-scatter.53.cloned.1.call-update) | async-done | bytes 1310736 | tf_op jit(solution)/shard_map/reduce_scatter | solution.py:256
  639.5 20.4 all-gather.34.cloned.1.call-done
  659.9 56.6 %all-gather.32.cloned.1.call-done = bf16[1280,1024]{1,0:T(8,128)(2,1)} async-done(((bf16[1280,256]{1,0:T(8,128)(2,1)}), bf16[1280,1024]{1,0:T(8,128)(2,1)}) %all-gather.32.cloned.1.call-update) | async-done | bytes 2621456 | tf_op jit(solution)/shard_map/all_gather | solution.py:252
  721.5 49.5 all-gather.46.cloned.1.call-done
  886.9 34.0 reduce-scatter.63.cloned.1.call-done
  941.8 26.2 all-gather.40.cloned.1.call-done
  974.7 27.3 all-gather.42.cloned.1.call-done
  1006.6 38.5 reduce-scatter.55.cloned.1.call-done
  1046.3 29.5 all_gather.120
  1121.0 36.8 all_gather.130
  1162.9 29.5 all_gather.123
  1235.9 46.5 all-gather.44.cloned.1.call-done
  1284.9 52.1 %all-gather.48.cloned.1.call-done = bf16[1280,1024]{1,0:T(8,128)(2,1)} async-done(((bf16[1280,256]{1,0:T(8,128)(2,1)}), bf16[1280,1024]{1,0:T(8,128)(2,1)}) %all-gather.48.cloned.1.call-update) | async-done | bytes 2621456 | tf_op jit(solution)/shard_map/all_gather | solution.py:252
  1374.3 82.6 %while.187 = (s32[]{:T(128)}, f32[8,64,128]{2,1,0:T(8,128)S(1)}, s32[]{:T(128)}, f32[5,256,8,64]{1,3,2,0:T(8,128)}, f32[5,8,64,128]{3,2,1,0:T(8,128)}, /*index=5...) while((s32[]{:T(128)}, f32[8,64,128]{2,1,0:T(8,128)S(1)}, ...), condition=%wide.region_56.62_spmd.clone, body=%wide.region_53.61_spmd.clone.sunk | while | flops 909779712 | bytes 5254527 | solution.py:79
  1472.6 74.8 %while.185 = (s32[]{:T(128)}, f32[8,64,128]{2,1,0:T(8,128)S(1)}, s32[]{:T(128)}, f32[5,256,8,64]{1,3,2,0:T(8,128)}, f32[5,8,64,128]{3,2,1,0:T(8,128)S(1)}, /*ind...) while((s32[]{:T(128)}, f32[8,64,128]{2,1,0:T(8,128)S(1)}, ...), condition=%wide.region_26.32_spmd.clone, body=%wide.region_23.31_spmd.clone.sunk | while | flops 909779712 | bytes 5254047 | solution.py:79
  1647.5 155.0 %while.188 = (s32[]{:T(128)}, f32[8,64,128]{2,1,0:T(8,128)S(1)}, f32[5,256,8,64]{1,3,2,0:T(8,128)}, f32[5,256,8]{1,2,0:T(8,128)}, f32[5,256,8]{1,2,0:T(8,128)}, ...) while((s32[]{:T(128)}, f32[8,64,128]{2,1,0:T(8,128)S(1)}, ...), condition=%wide.region_74.80_spmd.clone, body=%wide.region_62.79_spmd.clone.sunk | while | flops 2126684928 | bytes 15858829 | solution.py:79
  1817.2 152.4 %while.190 = (s32[]{:T(128)}, f32[8,64,128]{2,1,0:T(8,128)S(1)}, f32[5,256,8,64]{1,3,2,0:T(8,128)}, f32[5,256,8]{1,2,0:T(8,128)}, f32[5,256,8]{1,2,0:T(8,128)}, ...) while((s32[]{:T(128)}, f32[8,64,128]{2,1,0:T(8,128)S(1)}, ...), condition=%wide.region_138.144_spmd.clone, body=%wide.region_126.143_spmd.clone.sunk | while | flops 2126684928 | bytes 15858829 | solution.py:79
  2033.9 43.4 all-reduce.283.cloned.1.call-done
  2096.3 93.2 %reduce-scatter.81.cloned.1.call-done = f32[1280,256]{1,0:T(8,128)} async-done(((f32[1280,1024]{1,0:T(8,128)}), f32[1280,256]{1,0:T(8,128)}) %reduce-scatter.81.cloned.1.call-update) | async-done | bytes 1310736 | tf_op jit(solution)/shard_map/reduce_scatter | solution.py:256
  2210.9 75.1 %reduce-scatter.69.cloned.1.call-done = f32[1280,256]{1,0:T(8,128)} async-done(((f32[1280,1024]{1,0:T(8,128)}), f32[1280,256]{1,0:T(8,128)}) %reduce-scatter.69.cloned.1.call-update) | async-done | bytes 1310736 | tf_op jit(solution)/shard_map/reduce_scatter | solution.py:256
  2329.2 34.5 reduce-scatter.83.cloned.1.call-done
  2364.7 28.9 all_gather.137
  2393.7 23.7 reduce-scatter.71.cloned.1.call-done
  2470.4 29.0 reduce-scatter.73.cloned.1.call-done
  2501.3 29.8 all_gather.134
  2533.7 20.2 reduce-scatter.85.cloned.1.call-done
  2554.9 31.0 all_gather.138
  2635.2 26.4 reduce-scatter.59.cloned.1.call-done
  2661.5 97.3 %reduce-scatter.67.cloned.1.call-done = f32[1280,256]{1,0:T(8,128)} async-done(((f32[1280,1024]{1,0:T(8,128)}), f32[1280,256]{1,0:T(8,128)}) %reduce-scatter.67.cloned.1.call-update) | async-done | bytes 1310736 | tf_op jit(solution)/shard_map/reduce_scatter | solution.py:256
  2822.8 23.5 reduce-scatter.75.cloned.1.call-done
  2856.8 85.0 %reduce-scatter.89.cloned.1.call-done = f32[1280,256]{1,0:T(8,128)} async-done(((f32[1280,1024]{1,0:T(8,128)}), f32[1280,256]{1,0:T(8,128)}) %reduce-scatter.89.cloned.1.call-update) | async-done | bytes 1310736 | tf_op jit(solution)/shard_map/reduce_scatter | solution.py:256
  2941.8 96.4 %reduce-scatter.77.cloned.1.call-done = f32[1280,256]{1,0:T(8,128)} async-done(((f32[1280,1024]{1,0:T(8,128)}), f32[1280,256]{1,0:T(8,128)}) %reduce-scatter.77.cloned.1.call-update) | async-done | bytes 1310736 | tf_op jit(solution)/shard_map/reduce_scatter | solution.py:256
  3042.8 54.6 %all-gather.52.cloned.1.call-done = bf16[1280,1024]{1,0:T(8,128)(2,1)} async-done(((bf16[1280,256]{1,0:T(8,128)(2,1)}), bf16[1280,1024]{1,0:T(8,128)(2,1)}) %all-gather.52.cloned.1.call-update) | async-done | bytes 2621456 | tf_op jit(solution)/shard_map/all_gather | solution.py:252
  3102.5 50.0 %all-gather.50.cloned.1.call-done = bf16[1280,1024]{1,0:T(8,128)(2,1)} async-done(((bf16[1280,256]{1,0:T(8,128)(2,1)}), bf16[1280,1024]{1,0:T(8,128)(2,1)}) %all-gather.50.cloned.1.call-update) | async-done | bytes 2621456 | tf_op jit(solution)/shard_map/all_gather | solution.py:252
  3200.4 129.9 %while.191 = (s32[]{:T(128)}, f32[8,64,128]{2,1,0:T(8,128)S(1)}, f32[5,256,8,64]{1,3,2,0:T(8,128)}, f32[5,256,8]{1,2,0:T(8,128)S(1)}, f32[5,256,8]{1,2,0:T(8,128...) while((s32[]{:T(128)}, f32[8,64,128]{2,1,0:T(8,128)S(1)}, ...), condition=%wide.region_184.190_spmd.clone, body=%wide.region_172.189_spmd.clone.sunk | while | flops 2126684928 | bytes 15494677 | solution.py:79
  3345.7 145.7 %while.189 = (s32[]{:T(128)}, f32[8,64,128]{2,1,0:T(8,128)S(1)}, f32[5,256,8,64]{1,3,2,0:T(8,128)}, f32[5,256,8]{1,2,0:T(8,128)}, f32[5,256,8]{1,2,0:T(8,128)}, ...) while((s32[]{:T(128)}, f32[8,64,128]{2,1,0:T(8,128)S(1)}, ...), condition=%wide.region_120.126_spmd.clone, body=%wide.region_108.125_spmd.clone.sunk | while | flops 2126684928 | bytes 16541701 | solution.py:79
  3726.3 47.9 reduce-scatter.131.cloned.1.call-done
  3774.3 49.9 %reduce-scatter.129.cloned.1.call-done = bf16[1024,192]{0,1:T(8,128)(2,1)} async-done(((bf16[1024,1536]{0,1:T(8,128)(2,1)}), bf16[1024,192]{0,1:T(8,128)(2,1)}) %reduce-scatter.129.cloned.1.call-update) | async-done | bytes 393232 | tf_op jit(solution)/shard_map/reduce_scatter | solution.py:324
  3826.2 37.6 reduce-scatter.123.cloned.1.call-done
  3863.9 40.2 reduce-scatter.121.cloned.1.call-done
  3905.8 36.6 reduce-scatter.111.cloned.1.call-done
  3942.5 38.0 reduce-scatter.109.cloned.1.call-done
  3982.4 50.0 %reduce-scatter.117.cloned.1.call-done = bf16[3,192,384]{2,1,0:T(8,128)(2,1)} async-done(((bf16[3,1536,384]{2,1,0:T(8,128)(2,1)}), bf16[3,192,384]{2,1,0:T(8,128)(2,1)}) %reduce-scatter.117.cloned.1.call-update) | async-done | bytes 442384 | tf_op jit(solution)/shard_map/reduce_scatter | solution.py:315
  4032.4 51.4 %reduce-scatter.119.cloned.1.call-done = bf16[3,192,384]{2,1,0:T(8,128)(2,1)} async-done(((bf16[3,1536,384]{2,1,0:T(8,128)(2,1)}), bf16[3,192,384]{2,1,0:T(8,128)(2,1)}) %reduce-scatter.119.cloned.1.call-update) | async-done | bytes 442384 | tf_op jit(solution)/shard_map/reduce_scatter | solution.py:315
  4086.0 63.0 %reduce-scatter.125.cloned.1.call-done = bf16[2,192,1024]{2,1,0:T(8,128)(2,1)} async-done(((bf16[2,1536,1024]{2,1,0:T(8,128)(2,1)}), bf16[2,192,1024]{2,1,0:T(8,128)(2,1)}) %reduce-scatter.125.cloned.1.call-update) | async-done | bytes 786448 | tf_op jit(solution)/shard_map/reduce_scatter | solution.py:321
  4149.0 65.4 %reduce-scatter.127.cloned.1.call-done = bf16[2,192,1024]{2,1,0:T(8,128)(2,1)} async-done(((bf16[2,1536,1024]{2,1,0:T(8,128)(2,1)}), bf16[2,192,1024]{2,1,0:T(8,128)(2,1)}) %reduce-scatter.127.cloned.1.call-update) | async-done | bytes 786448 | tf_op jit(solution)/shard_map/reduce_scatter | solution.py:321
  4219.3 31.9 reduce-scatter.133.cloned.1.call-done
  4252.1 36.6 reduce-scatter.135.cloned.1.call-done
  4290.2 40.8 all-reduce.266
  4331.0 36.8 reduce-scatter.103.cloned.1.call-done
  4369.5 42.8 reduce-scatter.137.cloned.1.call-done
  4413.6 43.4 reduce-scatter.139.cloned.1.call-done
  4459.2 42.3 reduce-scatter.97.cloned.1.call-done
  4501.5 44.9 reduce-scatter.99.cloned.1.call-done
  4548.3 42.6 reduce-scatter.93.cloned.1.call-done
  4590.9 45.3 reduce-scatter.95.cloned.1.call-done
  4638.1 94.1 %reduce-scatter.79.cloned.1.call-done = f32[1280,256]{1,0:T(8,128)} async-done(((f32[1280,1024]{1,0:T(8,128)}), f32[1280,256]{1,0:T(8,128)}) %reduce-scatter.79.cloned.1.call-update) | async-done | bytes 1310736 | tf_op jit(solution)/shard_map/reduce_scatter | solution.py:256
  4732.2 96.6 %reduce-scatter.91.cloned.1.call-done = f32[1280,256]{1,0:T(8,128)} async-done(((f32[1280,1024]{1,0:T(8,128)}), f32[1280,256]{1,0:T(8,128)}) %reduce-scatter.91.cloned.1.call-update) | async-done | bytes 1310736 | tf_op jit(solution)/shard_map/reduce_scatter | solution.py:256
  4834.0 120.6 %all-reduce.279.cloned.1.call-done = f32[2,4,2048]{2,1,0:T(4,128)} async-done(((f32[2,4,2048]{2,1,0:T(4,128)}), f32[2,4,2048]{2,1,0:T(4,128)}) %all-reduce.279.cloned.1.call-update) | async-done | bytes 65552 | tf_op jit(solution)/shard_map/psum | solution.py:687
  (3965 shorter events, 2119.3 us)
Async XLA Ops:
  9.8 112.7 %all-gather.56.cloned.1.call-start = ((), (), s32[]{:S(2)}) async-start(), calls=%async_computation.101 | async-start | bytes 3276800 | tf_op jit(solution)/shard_map/all_gather | solution.py:252
  10.5 140.3 %all-gather.24.cloned.1.call-start = ((), (), s32[]{:S(2)}) async-start(), calls=%async_computation.44 | async-start | bytes 2359296 | tf_op jit(solution)/shard_map/all_gather | solution.py:275
  11.2 164.9 %all-gather.26.cloned.1.call-start = ((), (), s32[]{:S(2)}) async-start(), calls=%async_computation.45 | async-start | bytes 1179648 | tf_op jit(solution)/shard_map/all_gather | solution.py:276
  11.8 360.8 %all-gather.28.cloned.1.call-start = ((), (), s32[]{:S(2)}) async-start(), calls=%async_computation.46 | async-start | bytes 2359296 | tf_op jit(solution)/shard_map/all_gather | solution.py:274
  12.4 387.3 %all-gather.30.cloned.1.call-start = ((), (), s32[]{:S(2)}) async-start(), calls=%async_computation.47 | async-start | bytes 2359296 | tf_op jit(solution)/shard_map/all_gather | solution.py:278
  13.0 486.5 %reduce-scatter.61.cloned.1.call-start = ((), (), s32[]{:S(2)}) async-start(), calls=%async_computation.59 | async-start | bytes 6553600 | tf_op jit(solution)/shard_map/reduce_scatter | solution.py:256
  404.9 191.2 %reduce-scatter.53.cloned.1.call-start = ((), (), s32[]{:S(2)}) async-start(), calls=%async_computation.48 | async-start | bytes 6553600 | tf_op jit(solution)/shard_map/reduce_scatter | solution.py:256
  411.8 222.8 %all-gather.36.cloned.1.call-start = ((), (), s32[]{:S(2)}) async-start(), calls=%async_computation.51 | async-start | bytes 3981312 | tf_op jit(solution)/shard_map/all_gather | solution.py:282
  412.6 247.3 %all-gather.34.cloned.1.call-start = ((), (), s32[]{:S(2)}) async-start(), calls=%async_computation.50 | async-start | bytes 1179648 | tf_op jit(solution)/shard_map/all_gather | solution.py:279
  413.2 303.3 %all-gather.32.cloned.1.call-start = ((), (), s32[]{:S(2)}) async-start(), calls=%async_computation.49 | async-start | bytes 3276800 | tf_op jit(solution)/shard_map/all_gather | solution.py:252
  599.2 171.7 %all-gather.46.cloned.1.call-start = ((), (), s32[]{:S(2)}) async-start(), calls=%async_computation.60 | async-start | bytes 3276800 | tf_op jit(solution)/shard_map/all_gather | solution.py:252
  599.8 267.5 %all-gather.38.cloned.1.call-start = ((), (), s32[]{:S(2)}) async-start(), calls=%async_computation.52 | async-start | bytes 1327104 | tf_op jit(solution)/shard_map/all_gather | solution.py:283
  600.6 320.2 %reduce-scatter.63.cloned.1.call-start = ((), (), s32[]{:S(2)}) async-start(), calls=%async_computation.61 | async-start | bytes 2457600 | tf_op jit(solution)/shard_map/reduce_scatter | solution.py:256
  870.7 97.3 %all-gather.40.cloned.1.call-start = ((), (), s32[]{:S(2)}) async-start(), calls=%async_computation.54 | async-start | bytes 7077888 | tf_op jit(solution)/shard_map/all_gather | solution.py:284
  871.3 130.8 %all-gather.42.cloned.1.call-start = ((), (), s32[]{:S(2)}) async-start(), calls=%async_computation.55 | async-start | bytes 3538944 | tf_op jit(solution)/shard_map/all_gather | solution.py:285
  871.9 173.2 %reduce-scatter.55.cloned.1.call-start = ((), (), s32[]{:S(2)}) async-start(), calls=%async_computation.53 | async-start | bytes 2457600 | tf_op jit(solution)/shard_map/reduce_scatter | solution.py:256
  886.8 233.1 %reduce-scatter.65.cloned.1.call-start = ((), (), s32[]{:S(2)}) async-start(), calls=%async_computation.62 | async-start | bytes 2457600 | tf_op jit(solution)/shard_map/reduce_scatter | solution.py:256
  1006.5 155.3 %reduce-scatter.57.cloned.1.call-start = ((), (), s32[]{:S(2)}) async-start(), calls=%async_computation.56 | async-start | bytes 2457600 | tf_op jit(solution)/shard_map/reduce_scatter | solution.py:256
  1084.6 146.5 %all-gather.58.cloned.1.call-start = ((), (), s32[]{:S(2)}) async-start(), calls=%async_computation.102 | async-start | bytes 3276800 | tf_op jit(solution)/shard_map/all_gather | solution.py:252
  1087.1 195.3 %all-gather.44.cloned.1.call-start = ((), (), s32[]{:S(2)}) async-start(), calls=%async_computation.57 | async-start | bytes 3276800 | tf_op jit(solution)/shard_map/all_gather | solution.py:252
  1223.0 114.0 %all-gather.48.cloned.1.call-start = ((), (), s32[]{:S(2)}) async-start(), calls=%async_computation.63 | async-start | bytes 3276800 | tf_op jit(solution)/shard_map/all_gather | solution.py:252
  1223.7 371.8 %all-gather.60.cloned.1.call-start = ((), (), s32[]{:S(2)}) async-start(), calls=%async_computation.103 | async-start | bytes 3276800 | tf_op jit(solution)/shard_map/all_gather | solution.py:252
  1224.5 852.8 %all-reduce.283.cloned.1.call-start = ((), (), s32[]{:S(2)}) async-start(), calls=%async_computation.109 | async-start | bytes 2621440 | tf_op jit(solution)/shard_map/psum | solution.py:394
  2011.2 178.4 %reduce-scatter.81.cloned.1.call-start = ((), (), s32[]{:S(2)}) async-start(), calls=%async_computation.72 | async-start | bytes 6553600 | tf_op jit(solution)/shard_map/reduce_scatter | solution.py:256
  2095.7 190.3 %reduce-scatter.69.cloned.1.call-start = ((), (), s32[]{:S(2)}) async-start(), calls=%async_computation.65 | async-start | bytes 6553600 | tf_op jit(solution)/shard_map/reduce_scatter | solution.py:256
  2096.3 267.4 %reduce-scatter.83.cloned.1.call-start = ((), (), s32[]{:S(2)}) async-start(), calls=%async_computation.73 | async-start | bytes 2457600 | tf_op jit(solution)/shard_map/reduce_scatter | solution.py:256
  2329.1 170.3 %reduce-scatter.73.cloned.1.call-start = ((), (), s32[]{:S(2)}) async-start(), calls=%async_computation.67 | async-start | bytes 2457600 | tf_op jit(solution)/shard_map/reduce_scatter | solution.py:256
  2456.3 97.5 %reduce-scatter.85.cloned.1.call-start = ((), (), s32[]{:S(2)}) async-start(), calls=%async_computation.74 | async-start | bytes 2457600 | tf_op jit(solution)/shard_map/reduce_scatter | solution.py:256
  2456.9 204.6 %reduce-scatter.59.cloned.1.call-start = ((), (), s32[]{:S(2)}) async-start(), calls=%async_computation.58 | async-start | bytes 6553600 | tf_op jit(solution)/shard_map/reduce_scatter | solution.py:256
  2463.2 295.6 %reduce-scatter.67.cloned.1.call-start = ((), (), s32[]{:S(2)}) async-start(), calls=%async_computation.64 | async-start | bytes 6553600 | tf_op jit(solution)/shard_map/reduce_scatter | solution.py:256
  2470.4 332.9 %reduce-scatter.87.cloned.1.call-start = ((), (), s32[]{:S(2)}) async-start(), calls=%async_computation.75 | async-start | bytes 2457600 | tf_op jit(solution)/shard_map/reduce_scatter | solution.py:256
  2629.7 216.6 %reduce-scatter.75.cloned.1.call-start = ((), (), s32[]{:S(2)}) async-start(), calls=%async_computation.68 | async-start | bytes 2457600 | tf_op jit(solution)/shard_map/reduce_scatter | solution.py:256
  2771.8 170.0 %reduce-scatter.89.cloned.1.call-start = ((), (), s32[]{:S(2)}) async-start(), calls=%async_computation.76 | async-start | bytes 6553600 | tf_op jit(solution)/shard_map/reduce_scatter | solution.py:256
  2813.6 224.7 %reduce-scatter.77.cloned.1.call-start = ((), (), s32[]{:S(2)}) async-start(), calls=%async_computation.69 | async-start | bytes 6553600 | tf_op jit(solution)/shard_map/reduce_scatter | solution.py:256
  2856.6 240.8 %all-gather.52.cloned.1.call-start = ((), (), s32[]{:S(2)}) async-start(), calls=%async_computation.77 | async-start | bytes 3276800 | tf_op jit(solution)/shard_map/all_gather | solution.py:252
  3041.9 110.7 %all-gather.50.cloned.1.call-start = ((), (), s32[]{:S(2)}) async-start(), calls=%async_computation.70 | async-start | bytes 3276800 | tf_op jit(solution)/shard_map/all_gather | solution.py:252
  3042.7 537.7 %all-reduce.281.cloned.1.call-start = ((), (), s32[]{:S(2)}) async-start(), calls=%async_computation.108 | async-start | bytes 2621440 | tf_op jit(solution)/shard_map/psum | solution.py:394
  3507.4 210.9 %reduce-scatter.115.cloned.1.call-start = ((), (), s32[]{:S(2)}) async-start(), calls=%async_computation.91 | async-start | bytes 884736 | tf_op jit(solution)/shard_map/reduce_scatter | solution.py:312
  3510.4 207.9 %reduce-scatter.113.cloned.1.call-start = ((), (), s32[]{:S(2)}) async-start(), calls=%async_computation.90 | async-start | bytes 884736 | tf_op jit(solution)/shard_map/reduce_scatter | solution.py:312
  3513.2 206.7 %reduce-scatter.105.cloned.1.call-start = ((), (), s32[]{:S(2)}) async-start(), calls=%async_computation.86 | async-start | bytes 1179648 | tf_op jit(solution)/shard_map/reduce_scatter | solution.py:306
  3517.4 207.1 %reduce-scatter.107.cloned.1.call-start = ((), (), s32[]{:S(2)}) async-start(), calls=%async_computation.87 | async-start | bytes 1179648 | tf_op jit(solution)/shard_map/reduce_scatter | solution.py:306
  3522.4 251.9 %reduce-scatter.131.cloned.1.call-start = ((), (), s32[]{:S(2)}) async-start(), calls=%async_computation.99 | async-start | bytes 3538944 | tf_op jit(solution)/shard_map/reduce_scatter | solution.py:324
  3526.6 297.6 %reduce-scatter.129.cloned.1.call-start = ((), (), s32[]{:S(2)}) async-start(), calls=%async_computation.98 | async-start | bytes 3538944 | tf_op jit(solution)/shard_map/reduce_scatter | solution.py:324
  3531.5 332.4 %reduce-scatter.123.cloned.1.call-start = ((), (), s32[]{:S(2)}) async-start(), calls=%async_computation.95 | async-start | bytes 1327104 | tf_op jit(solution)/shard_map/reduce_scatter | solution.py:318
  3534.7 369.4 %reduce-scatter.121.cloned.1.call-start = ((), (), s32[]{:S(2)}) async-start(), calls=%async_computation.94 | async-start | bytes 1327104 | tf_op jit(solution)/shard_map/reduce_scatter | solution.py:318
  3536.8 405.7 %reduce-scatter.111.cloned.1.call-start = ((), (), s32[]{:S(2)}) async-start(), calls=%async_computation.89 | async-start | bytes 884736 | tf_op jit(solution)/shard_map/reduce_scatter | solution.py:309
  3538.6 441.9 %reduce-scatter.109.cloned.1.call-start = ((), (), s32[]{:S(2)}) async-start(), calls=%async_computation.88 | async-start | bytes 884736 | tf_op jit(solution)/shard_map/reduce_scatter | solution.py:309
  3540.4 492.0 %reduce-scatter.117.cloned.1.call-start = ((), (), s32[]{:S(2)}) async-start(), calls=%async_computation.92 | async-start | bytes 3981312 | tf_op jit(solution)/shard_map/reduce_scatter | solution.py:315
  3545.9 538.0 %reduce-scatter.119.cloned.1.call-start = ((), (), s32[]{:S(2)}) async-start(), calls=%async_computation.93 | async-start | bytes 3981312 | tf_op jit(solution)/shard_map/reduce_scatter | solution.py:315
  3552.4 596.6 %reduce-scatter.125.cloned.1.call-start = ((), (), s32[]{:S(2)}) async-start(), calls=%async_computation.96 | async-start | bytes 7077888 | tf_op jit(solution)/shard_map/reduce_scatter | solution.py:321
  3560.9 653.4 %reduce-scatter.127.cloned.1.call-start = ((), (), s32[]{:S(2)}) async-start(), calls=%async_computation.97 | async-start | bytes 7077888 | tf_op jit(solution)/shard_map/reduce_scatter | solution.py:321
  3569.4 681.7 %reduce-scatter.133.cloned.1.call-start = ((), (), s32[]{:S(2)}) async-start(), calls=%async_computation.104 | async-start | bytes 294912
  3578.6 710.0 %reduce-scatter.135.cloned.1.call-start = ((), (), s32[]{:S(2)}) async-start(), calls=%async_computation.105 | async-start | bytes 294912
  3580.1 750.9 %reduce-scatter.101.cloned.1.call-start = ((), (), s32[]{:S(2)}) async-start(), calls=%async_computation.83 | async-start | bytes 1179648 | tf_op jit(solution)/shard_map/reduce_scatter | solution.py:297
  3584.4 783.3 %reduce-scatter.103.cloned.1.call-start = ((), (), s32[]{:S(2)}) async-start(), calls=%async_computation.84 | async-start | bytes 1179648 | tf_op jit(solution)/shard_map/reduce_scatter | solution.py:297
  3592.5 819.7 %reduce-scatter.137.cloned.1.call-start = ((), (), s32[]{:S(2)}) async-start(), calls=%async_computation.106 | async-start | bytes 2359296
  3609.5 847.5 %reduce-scatter.139.cloned.1.call-start = ((), (), s32[]{:S(2)}) async-start(), calls=%async_computation.107 | async-start | bytes 2359296
  3659.3 842.2 %reduce-scatter.97.cloned.1.call-start = ((), (), s32[]{:S(2)}) async-start(), calls=%async_computation.81 | async-start | bytes 2359296 | tf_op jit(solution)/shard_map/reduce_scatter | solution.py:294
  3671.4 875.0 %reduce-scatter.99.cloned.1.call-start = ((), (), s32[]{:S(2)}) async-start(), calls=%async_computation.82 | async-start | bytes 2359296 | tf_op jit(solution)/shard_map/reduce_scatter | solution.py:294
  3678.5 912.4 %reduce-scatter.93.cloned.1.call-start = ((), (), s32[]{:S(2)}) async-start(), calls=%async_computation.79 | async-start | bytes 2359296 | tf_op jit(solution)/shard_map/reduce_scatter | solution.py:291
  3685.5 950.7 %reduce-scatter.95.cloned.1.call-start = ((), (), s32[]{:S(2)}) async-start(), calls=%async_computation.80 | async-start | bytes 2359296 | tf_op jit(solution)/shard_map/reduce_scatter | solution.py:291
  3692.5 1039.8 %reduce-scatter.79.cloned.1.call-start = ((), (), s32[]{:S(2)}) async-start(), calls=%async_computation.71 | async-start | bytes 6553600 | tf_op jit(solution)/shard_map/reduce_scatter | solution.py:256
  3715.6 1113.2 %reduce-scatter.91.cloned.1.call-start = ((), (), s32[]{:S(2)}) async-start(), calls=%async_computation.78 | async-start | bytes 6553600 | tf_op jit(solution)/shard_map/reduce_scatter | solution.py:256
  3716.4 1238.2 %all-reduce.279.cloned.1.call-start = ((), (), s32[]{:S(2)}) async-start(), calls=%async_computation.85 | async-start | bytes 131072 | tf_op jit(solution)/shard_map/psum | solution.py:687
  (855 other events, 23436.3 us)
Sparse Core Ops, SparseCore 0:
  10.2 56.9 all-gather.53
  69.3 53.0 all-gather.55
  124.3 26.4 all-gather.23
  177.9 27.9 all-gather.27
  207.6 28.2 all-gather.29
  405.0 94.4 reduce-scatter.60
  501.8 94.2 reduce-scatter.52
  598.0 36.5 all-gather.35
  636.4 23.4 all-gather.33
  662.0 54.4 all-gather.31
  717.9 53.0 all-gather.45
  870.8 49.9 reduce-scatter.62
  922.6 45.3 all-gather.39
  969.7 32.3 all-gather.41
  1004.2 40.8 reduce-scatter.54
  1047.3 51.9 reduce-scatter.64
  1101.5 56.0 reduce-scatter.56
  1159.1 67.1 all-gather.57
  1227.8 54.4 all-gather.43
  1283.9 53.0 all-gather.47
  1338.6 53.0 all-gather.59
  2011.3 65.8 all-reduce.282
  2095.8 93.7 reduce-scatter.80
  2191.7 94.2 reduce-scatter.68
  2321.8 41.8 reduce-scatter.82
  2366.0 51.3 reduce-scatter.70
  2456.4 42.9 reduce-scatter.72
  2501.6 52.2 reduce-scatter.84
  2556.2 105.3 reduce-scatter.58
  2663.8 94.9 reduce-scatter.66
  2761.0 42.2 reduce-scatter.86
  2805.6 40.6 reduce-scatter.74
  2848.6 93.1 reduce-scatter.88
  2944.0 94.2 reduce-scatter.76
  3042.0 55.2 all-gather.51
  3099.5 53.0 all-gather.49
  3507.5 61.9 all-reduce.280
  3573.2 34.5 reduce-scatter.114
  3611.0 34.9 reduce-scatter.112
  3649.1 36.2 reduce-scatter.104
  3688.4 36.0 reduce-scatter.106
  3727.9 46.3 reduce-scatter.130
  3777.9 46.2 reduce-scatter.128
  3827.2 36.6 reduce-scatter.122
  3867.3 36.7 reduce-scatter.120
  3907.7 34.7 reduce-scatter.110
  3945.5 34.9 reduce-scatter.108
  3984.0 48.3 reduce-scatter.116
  4035.7 48.0 reduce-scatter.118
  4087.2 61.7 reduce-scatter.124
  4152.6 61.7 reduce-scatter.126
  4218.0 33.1 reduce-scatter.132
  4255.1 33.5 reduce-scatter.134
  4291.8 36.4 reduce-scatter.100
  4331.6 36.1 reduce-scatter.102
  4370.9 41.2 reduce-scatter.136
  4415.7 41.2 reduce-scatter.138
  4460.3 41.1 reduce-scatter.96
  4505.1 41.2 reduce-scatter.98
  4549.7 41.1 reduce-scatter.92
  4595.0 41.2 reduce-scatter.94
  4638.4 93.7 reduce-scatter.78
  4734.5 94.2 reduce-scatter.90
  4834.8 119.7 all-reduce.278
  (2 shorter events, 46.1 us)
where the time goes:
time: 4990 us; the launch traced here: 4960 us
  waiting for transfers between devices  2580 us (52%)
  matrix products  781 us (16%)
  other arithmetic  575 us (12%)
  local copies, waits for them, and re-layouts  517 us (10%)
  blocking collectives  420 us (8%)
  loops' own time  57.5 us (1%)
    reduce_scatter x20, waiting for transfers between devices, narrow(): return lax.psum_scatter(values, 'mp', scatter_dimension=1, tiled=True)  1050 us
    all_gather x10, waiting for transfers between devices, widen(): return lax.all_gather(values, 'mp', axis=1, tiled=True)  399 us
    all_gather x10, blocking collectives, widen(): return lax.all_gather(values, 'mp', axis=1, tiled=True)  258 us
    dot_general x60, matrix products, scan_block(): outputs = jnp.einsum('ijh,jhp->ihp', weights, block_x, precision=HIGHEST)  225 us
    unnamed x70, waiting for transfers between devices  166 us
    reduce_scatter x2, waiting for transfers between devices, settle(): lax.psum_scatter(grads[10].astype(jnp.bfloat16), 'dp', scatter_dimension=...  128 us
    unnamed x1517, local copies, waits for them, and re-layouts  121 us
    psum x1, waiting for transfers between devices, per_device(): lax.psum((small_total[0], conv_x_full, small_total[2], bias_full, decay_f...  121 us

commit v1 on v0

v1 whole, which is shorter than its diff:
```python
import functools

import jax
import jax.numpy as jnp
from jax import lax
from jax.experimental import pallas as pl
from jax.experimental.pallas import tpu as pltpu
from jax.sharding import PartitionSpec as P

DM = 1536
AHEADS = 24
CAP = 320


EPSILON = 1e-06
HIGHEST = lax.Precision.HIGHEST


def boundary_prob(all_dots, starts):
    cosine = all_dots[0] * lax.rsqrt(all_dots[1] + EPSILON) * lax.rsqrt(all_dots[2] + EPSILON)
    return jnp.where(starts, 1.0, 0.5 * (1.0 - cosine))


def to_low(values):
    return values.astype(jnp.bfloat16)


def matmul(left, right):
    return jnp.dot(left, right, preferred_element_type=jnp.float32)


def left_product(left, right):
    return lax.dot_general(
        left, right, (((0,), (0,)), ((), ())), preferred_element_type=jnp.float32
    )


def right_product(left, right):
    return lax.dot_general(
        left, right, (((1,), (1,)), ((), ())), preferred_element_type=jnp.float32
    )


BLOCK = 128
LANES = 128
HEAD_SIZE = 64


def sigmoid(values):
    return 1.0 / (1.0 + jnp.exp(-values))


def split_product(values, ones_low):
    high = to_low(values)
    rest = to_low(values - high.astype(jnp.float32))
    return matmul(high, ones_low) + matmul(rest, ones_low)


def exact_product(left, right):
    return jnp.dot(left, right, precision=HIGHEST, preferred_element_type=jnp.float32)


def shifted_down(tail, block, steps):
    joined = jnp.concatenate([tail, block], 0)
    return pltpu.roll(joined, steps, 0)[8:]


def shifted_up(block, head, steps):
    joined = jnp.concatenate([block, head], 0)
    size = joined.shape[0]
    return pltpu.roll(joined, size - steps, 0)[: size - 8]


def filtered(tail, block, taps, columns):
    result = block * taps[3:4]
    for steps in range(1, 4):
        moved = shifted_down(tail, block, steps)
        result = result + moved * columns[:, steps - 1 : steps] * taps[3 - steps : 4 - steps]
    return result


def pair_columns(values, pair, first_half):
    return jnp.where(
        first_half, values[:, 2 * pair : 2 * pair + 1], values[:, 2 * pair + 1 : 2 * pair + 2]
    )


def stacked_halves(values, first_half):
    zero = jnp.zeros_like(values)
    return jnp.concatenate(
        [jnp.where(first_half, values, zero), jnp.where(first_half, zero, values)], 0
    )


def folded_rows(values):
    return jnp.sum(values.reshape(values.shape[0] // 8, 8, values.shape[1]), axis=0)


class Decay:
    def __init__(self, dt_raw, dt_bias, rate, columns, segment_row):
        rows = lax.broadcasted_iota(jnp.int32, (BLOCK, BLOCK), 0)
        cols = lax.broadcasted_iota(jnp.int32, (BLOCK, BLOCK), 1)
        self.lower = rows >= cols
        shifted = dt_raw + dt_bias
        self.steepness = sigmoid(shifted)
        self.step = jnp.maximum(shifted, 0.0) + jnp.log(1.0 + jnp.exp(-jnp.abs(shifted)))
        self.decay = rate * self.step
        self.total = exact_product(self.lower.astype(jnp.float32), self.decay)
        self.total_rows = self.total.T
        same = self.lower & (columns[:, 3:4] == segment_row)
        self.mask = jnp.where(same, 0.0, -1e30)
        last = self.total[BLOCK - 1 : BLOCK]
        self.reach = jnp.exp(self.total) * columns[:, 4:5]
        self.to_end = jnp.exp(last - self.total) * columns[:, 5:6]
        self.kept = jnp.exp(last) * columns[BLOCK - 1 : BLOCK, 4:5]

    def factor(self, head):
        return jnp.exp(
            self.total[:, head : head + 1] - self.total_rows[head : head + 1] + self.mask
        )


def zx_lanes(pair, per_block):
    block, tile = divmod(pair, per_block)
    start = (2 * block * per_block + tile) * LANES
    shift = per_block * LANES
    return slice(start, start + LANES), slice(start + shift, start + shift + LANES)


def mix_kernel(
    per_block,
    zx_ref,
    bcdt_ref,
    columns_ref,
    segment_ref,
    taps_ref,
    map_taps_ref,
    heads_ref,
    channels_ref,
    mixed_ref,
    y_ref,
    square_ref,
    states_ref,
    state,
    tail_x,
    tail_maps,
    ends,
):
    pairs = channels_ref.shape[1] // LANES

    @pl.when(pl.program_id(0) == 0)
    def _():
        state[...] = jnp.zeros_like(state)
        tail_x[...] = jnp.zeros_like(tail_x)
        tail_maps[...] = jnp.zeros_like(tail_maps)

    columns = columns_ref[...]
    first_half = lax.broadcasted_iota(jnp.int32, (1, LANES), 1) < HEAD_SIZE
    maps_in = bcdt_ref[:, : 2 * LANES]
    maps = filtered(tail_maps[...], maps_in, map_taps_ref[...], columns)
    maps = maps * sigmoid(maps)
    in_map = to_low(maps[:, :LANES])
    out_map = to_low(maps[:, LANES:])
    heads = heads_ref[...]
    decay = Decay(
        bcdt_ref[:, 2 * LANES :], heads[0:1], heads[1:2], columns, segment_ref[0, 0:1, :]
    )
    meeting = right_product(out_map, in_map)
    low_state = to_low(state[...])
    states_ref[...] = low_state
    y_ref[...] = matmul(out_map, low_state)
    squares = jnp.zeros((BLOCK, LANES), jnp.float32)
    for pair in range(pairs):
        lanes = slice(pair * LANES, (pair + 1) * LANES)
        z_lanes, x_lanes = zx_lanes(pair, per_block)
        block = zx_ref[:, x_lanes]
        pre = filtered(tail_x[:, lanes], block, taps_ref[:, lanes], columns)
        tail_x[:, lanes] = block[BLOCK - 8 :]
        value = pre * sigmoid(pre)
        scaled = value * pair_columns(decay.step, pair, first_half)
        ends[:, lanes] = to_low(scaled * pair_columns(decay.to_end, pair, first_half))
        weights = jnp.concatenate(
            [to_low(meeting * decay.factor(2 * pair + half)) for half in range(2)], 1
        )
        y = matmul(weights, stacked_halves(to_low(scaled), first_half))
        y = y + y_ref[:, lanes] * pair_columns(decay.reach, pair, first_half)
        y_ref[:, lanes] = y
        gate_in = zx_ref[:, z_lanes]
        gated = (y + channels_ref[0:1, lanes] * value) * (gate_in * sigmoid(gate_in))
        squares = squares + gated * gated
        mixed_ref[:, lanes] = to_low(gated * channels_ref[1:2, lanes])
        state[:, lanes] = state[:, lanes] * pair_columns(decay.kept, pair, first_half)
    square_ref[...] = jnp.sum(squares, axis=1, keepdims=True)
    state[...] += left_product(in_map, ends[...])
    tail_maps[...] = bcdt_ref[BLOCK - 8 :, : 2 * LANES]


def mix_back_kernel(
    per_block,
    grad_ref,
    zx_ref,
    zx_tail_ref,
    bcdt_ref,
    maps_tail_ref,
    y_ref,
    states_ref,
    columns_ref,
    later_ref,
    segment_ref,
    taps_ref,
    map_taps_ref,
    heads_ref,
    channels_ref,
    owner_ref,
    grad_zx_ref,
    grad_maps_ref,
    grad_dt_ref,
    grad_taps_ref,
    grad_map_taps_ref,
    grad_heads_ref,
    grad_channels_ref,
    grad_state,
    head_x,
    head_maps,
    ends,
    reached,
    pulled,
    balance,
    step_part,
):
    pairs = channels_ref.shape[1] // LANES
    step = pl.program_id(0)
    first_chunk = step == pl.num_programs(0) - 1

    @pl.when(step == 0)
    def _():
        grad_state[...] = jnp.zeros_like(grad_state)
        head_x[...] = jnp.zeros_like(head_x)
        head_maps[...] = jnp.zeros_like(head_maps)
        grad_taps_ref[...] = jnp.zeros_like(grad_taps_ref)
        grad_map_taps_ref[...] = jnp.zeros_like(grad_map_taps_ref)
        grad_heads_ref[...] = jnp.zeros_like(grad_heads_ref)
        grad_channels_ref[...] = jnp.zeros_like(grad_channels_ref)

    columns = columns_ref[...]
    later = later_ref[...]
    first_half = lax.broadcasted_iota(jnp.int32, (1, LANES), 1) < HEAD_SIZE
    tail_maps = jnp.where(first_chunk, 0.0, maps_tail_ref[:, : 2 * LANES])
    maps_in = bcdt_ref[:, : 2 * LANES]
    maps_pre = filtered(tail_maps, maps_in, map_taps_ref[...], columns)
    maps_open = sigmoid(maps_pre)
    maps = maps_pre * maps_open
    in_map = to_low(maps[:, :LANES])
    out_map = to_low(maps[:, LANES:])
    heads = heads_ref[...]
    decay = Decay(
        bcdt_ref[:, 2 * LANES :], heads[0:1], heads[1:2], columns, segment_ref[0, 0:1, :]
    )
    meeting = right_product(out_map, in_map)
    low_grad_state = to_low(grad_state[...])
    pulled[...] = matmul(in_map, low_grad_state)
    scale = later[:, 3:4]
    coefficient = later[:, 4:5]
    grad_meeting = jnp.zeros((BLOCK, BLOCK), jnp.float32)
    for pair in range(pairs):
        lanes = slice(pair * LANES, (pair + 1) * LANES)
        z_lanes, x_lanes = zx_lanes(pair, per_block)
        tail = jnp.where(first_chunk, 0.0, zx_tail_ref[:, x_lanes])
        block = zx_ref[:, x_lanes]
        taps = taps_ref[:, lanes]
        pre = filtered(tail, block, taps, columns)
        opened = sigmoid(pre)
        value = pre * opened
        slope = opened + value * (1.0 - opened)
        gate_in = zx_ref[:, z_lanes]
        gate_open = sigmoid(gate_in)
        gate = gate_in * gate_open
        skip = channels_ref[0:1, lanes]
        gain = channels_ref[1:2, lanes]
        y = y_ref[:, lanes]
        whole = y + skip * value
        gated = whole * gate
        grad_mixed = grad_ref[:, lanes]
        grad_gated = scale * (grad_mixed * gain) - coefficient * gated
        grad_channels_ref[8:16, lanes] += folded_rows(grad_mixed * gated * scale)
        grad_y = grad_gated * gate
        grad_zx_ref[:, z_lanes] = to_low(
            grad_gated * whole * (gate_open + gate * (1.0 - gate_open))
        )
        grad_channels_ref[0:8, lanes] += folded_rows(grad_y * value)
        low_grad_y = to_low(grad_y)
        reached[:, lanes] = to_low(grad_y * pair_columns(decay.reach, pair, first_half))
        step_wide = pair_columns(decay.step, pair, first_half)
        scaled = value * step_wide
        low_scaled = to_low(scaled)
        end_wide = pair_columns(decay.to_end, pair, first_half)
        ends[:, lanes] = to_low(scaled * end_wide)
        stacked = stacked_halves(low_grad_y, first_half)
        grad_weights = right_product(stacked, low_scaled)
        parts = []
        for half in range(2):
            factor = decay.factor(2 * pair + half)
            grad_meeting = (
                grad_meeting + factor * grad_weights[half * BLOCK : (half + 1) * BLOCK]
            )
            parts.append(to_low(meeting * factor))
        from_end = pulled[:, lanes] * end_wide
        grad_scaled = left_product(jnp.concatenate(parts, 0), stacked) + from_end
        wide_scaled = low_scaled.astype(jnp.float32)
        balance[:BLOCK, lanes] = low_grad_y.astype(jnp.float32) * y - wide_scaled * grad_scaled
        step_part[:, lanes] = to_low(grad_scaled * value)
        kept = pair_columns(decay.kept, pair, first_half)
        kept_state = grad_state[:, lanes] * kept
        balance[BLOCK : BLOCK + 8, lanes] = folded_rows(wide_scaled * from_end) + folded_rows(
            kept_state * states_ref[:, lanes].astype(jnp.float32)
        )
        grad_state[:, lanes] = kept_state
        grad_pre = (grad_scaled * step_wide + grad_y * skip) * slope
        grad_taps_ref[24:32, lanes] += folded_rows(grad_pre * block)
        grad_x = grad_pre * taps[3:4]
        head = head_x[:, lanes]
        for steps in range(1, 4):
            moved = shifted_down(tail, block, steps)
            grad_taps_ref[24 - 8 * steps : 32 - 8 * steps, lanes] += folded_rows(
                grad_pre * columns[:, steps - 1 : steps] * moved
            )
            grad_x = grad_x + (
                shifted_up(grad_pre, head, steps)
                * later[:, steps - 1 : steps]
                * taps[3 - steps : 4 - steps]
            )
        grad_zx_ref[:, x_lanes] = to_low(grad_x)
        head_x[:, lanes] = grad_pre[:8]

    owner = owner_ref[...]
    grad_total = split_product(balance[:BLOCK, :], owner)
    end_rows = split_product(balance[BLOCK : BLOCK + 8, :], owner)
    end_total = jnp.sum(end_rows, axis=0, keepdims=True)
    rows = lax.broadcasted_iota(jnp.int32, (BLOCK, LANES), 0)
    grad_total = grad_total + jnp.where(rows == BLOCK - 1, end_total, 0.0)
    upper = jnp.where(rows <= lax.broadcasted_iota(jnp.int32, (BLOCK, LANES), 1), 1.0, 0.0)
    grad_decay = exact_product(upper, grad_total)
    grad_step = matmul(step_part[...], owner) + grad_decay * heads[1:2]
    grad_raw = grad_step * decay.steepness
    grad_dt_ref[...] = grad_raw
    grad_heads_ref[0:8, :] += folded_rows(grad_raw)
    grad_heads_ref[8:16, :] += folded_rows(grad_decay * decay.decay)

    low_meeting = to_low(grad_meeting)
    grad_out_map = matmul(low_meeting, in_map) + right_product(reached[...], states_ref[...])
    grad_in_map = left_product(low_meeting, out_map) + right_product(ends[...], low_grad_state)
    grad_state[...] += left_product(out_map, reached[...])
    grad_pre = jnp.concatenate([grad_in_map, grad_out_map], 1) * (
        maps_open + maps * (1.0 - maps_open)
    )
    map_taps = map_taps_ref[...]
    grad_map_taps_ref[24:32, :] += folded_rows(grad_pre * maps_in)
    grad_maps = grad_pre * map_taps[3:4]
    head = head_maps[...]
    for steps in range(1, 4):
        moved = shifted_down(tail_maps, maps_in, steps)
        grad_map_taps_ref[24 - 8 * steps : 32 - 8 * steps, :] += folded_rows(
            grad_pre * columns[:, steps - 1 : steps] * moved
        )
        grad_maps = grad_maps + (
            shifted_up(grad_pre, head, steps)
            * later[:, steps - 1 : steps]
            * map_taps[3 - steps : 4 - steps]
        )
    grad_maps_ref[...] = grad_maps
    head_maps[...] = grad_pre[:8]


def whole_block(*shape):
    return pl.BlockSpec(shape, lambda step: (0,) * len(shape))


def mix_settings(length, channels, work):
    return dict(
        compiler_params=pltpu.CompilerParams(
            dimension_semantics=("arbitrary",), vmem_limit_bytes=48 * 1024 * 1024
        ),
        cost_estimate=pl.CostEstimate(
            flops=work * length * channels * BLOCK,
            bytes_accessed=length * channels * 16,
            transcendentals=length * channels * 4,
        ),
    )


def mix_forward(
    per_block, zx_proj, bcdt, columns, segment_rows, taps, map_taps, heads, channels
):
    length = zx_proj.shape[0]
    width = channels.shape[1]
    chunks = length // BLOCK

    def rows(size):
        return pl.BlockSpec((BLOCK, size), lambda step: (step, 0))

    return pl.pallas_call(
        functools.partial(mix_kernel, per_block),
        grid=(chunks,),
        in_specs=[
            rows(2 * width),
            rows(3 * LANES),
            rows(8),
            pl.BlockSpec((1, 8, BLOCK), lambda step: (step, 0, 0)),
            whole_block(4, width),
            whole_block(4, 2 * LANES),
            whole_block(8, LANES),
            whole_block(8, width),
        ],
        out_specs=[rows(width), rows(width), rows(1), rows(width)],
        out_shape=[
            jax.ShapeDtypeStruct((length, width), jnp.bfloat16),
            jax.ShapeDtypeStruct((length, width), jnp.float32),
            jax.ShapeDtypeStruct((length, 1), jnp.float32),
            jax.ShapeDtypeStruct((chunks * LANES, width), jnp.bfloat16),
        ],
        scratch_shapes=[
            pltpu.VMEM((LANES, width), jnp.float32),
            pltpu.VMEM((8, width), jnp.float32),
            pltpu.VMEM((8, 2 * LANES), jnp.float32),
            pltpu.VMEM((BLOCK, width), jnp.bfloat16),
        ],
        **mix_settings(length, width, 8),
    )(zx_proj, bcdt, columns, segment_rows, taps, map_taps, heads, channels)


def mix_backward(
    per_block,
    grad_mixed,
    zx_proj,
    bcdt,
    y,
    states,
    columns,
    later,
    segment_rows,
    taps,
    map_taps,
    heads,
    channels,
    owner,
):
    length, width = grad_mixed.shape
    chunks = length // BLOCK
    eighths = BLOCK // 8

    def rows(size):
        return pl.BlockSpec((BLOCK, size), lambda step: (chunks - 1 - step, 0))

    def before(size):
        return pl.BlockSpec(
            (8, size), lambda step: (jnp.maximum((chunks - 1 - step) * eighths - 1, 0), 0)
        )

    low = jnp.bfloat16
    wide = jnp.float32
    return pl.pallas_call(
        functools.partial(mix_back_kernel, per_block),
        grid=(chunks,),
        in_specs=[
            rows(width),
            rows(2 * width),
            before(2 * width),
            rows(3 * LANES),
            before(3 * LANES),
            rows(width),
            rows(width),
            rows(8),
            rows(8),
            pl.BlockSpec((1, 8, BLOCK), lambda step: (chunks - 1 - step, 0, 0)),
            whole_block(4, width),
            whole_block(4, 2 * LANES),
            whole_block(8, LANES),
            whole_block(8, width),
            whole_block(width, LANES),
        ],
        out_specs=[
            rows(2 * width),
            rows(2 * LANES),
            rows(LANES),
            whole_block(32, width),
            whole_block(32, 2 * LANES),
            whole_block(16, LANES),
            whole_block(16, width),
        ],
        out_shape=[
            jax.ShapeDtypeStruct((length, 2 * width), low),
            jax.ShapeDtypeStruct((length, 2 * LANES), wide),
            jax.ShapeDtypeStruct((length, LANES), wide),
            jax.ShapeDtypeStruct((32, width), wide),
            jax.ShapeDtypeStruct((32, 2 * LANES), wide),
            jax.ShapeDtypeStruct((16, LANES), wide),
            jax.ShapeDtypeStruct((16, width), wide),
        ],
        scratch_shapes=[
            pltpu.VMEM((LANES, width), wide),
            pltpu.VMEM((8, width), wide),
            pltpu.VMEM((8, 2 * LANES), wide),
            pltpu.VMEM((BLOCK, width), low),
            pltpu.VMEM((BLOCK, width), low),
            pltpu.VMEM((BLOCK, width), wide),
            pltpu.VMEM((BLOCK + 8, width), wide),
            pltpu.VMEM((BLOCK, width), low),
        ],
        **mix_settings(length, width, 24),
    )(
        grad_mixed,
        zx_proj,
        zx_proj,
        bcdt,
        bcdt,
        y,
        states,
        columns,
        later,
        segment_rows,
        taps,
        map_taps,
        heads,
        channels,
        owner,
    )


def item_columns(segment):
    length = segment.shape[0]
    back = []
    ahead = []
    for steps in range(1, 4):
        same = segment[steps:] == segment[:-steps]
        none = jnp.zeros((steps,), jnp.bool_)
        back.append(jnp.concatenate([none, same]))
        ahead.append(jnp.concatenate([same, none]))
    blocks = segment.reshape(-1, BLOCK)
    last = blocks[:, BLOCK - 1]
    before = jnp.concatenate([jnp.full((1,), -1, segment.dtype), last[:-1]])
    carried = (blocks == before[:, None]).reshape(-1)
    ending = (blocks == last[:, None]).reshape(-1)
    wide = jnp.float32
    nothing = jnp.zeros((length,), wide)
    columns = jnp.stack(
        [b.astype(wide) for b in back]
        + [segment.astype(wide), carried.astype(wide), ending.astype(wide), nothing, nothing],
        1,
    )
    rows = jnp.broadcast_to(blocks.astype(wide)[:, None, :], (blocks.shape[0], 8, BLOCK))
    return columns, [a.astype(wide) for a in ahead], rows


SLOTS = 384


def smooth_kernel(probs_ref, down_ref, encoded_ref, confidence_ref, rank_ref, out_ref, smooth_ref, high, rest):
    count = down_ref.shape[0]

    @pl.when(pl.program_id(0) == 0)
    def _():
        high[count:, :] = jnp.zeros((SLOTS - count, high.shape[1]), jnp.bfloat16)
        rest[count:, :] = jnp.zeros((SLOTS - count, high.shape[1]), jnp.bfloat16)

        def tile(index, previous):
            start = pl.multiple_of(index * 8, 8)
            rows = down_ref[pl.ds(start, 8), :]
            done = []
            for r in range(8):
                prob = probs_ref[start + r]
                previous = prob * rows[r : r + 1] + (1.0 - prob) * previous
                done.append(previous)
            smooth_ref[pl.ds(start, 8), :] = jnp.concatenate(done, 0)
            return previous

        lax.fori_loop(0, count // 8, tile, jnp.zeros((1, down_ref.shape[1]), jnp.float32))
        smooth = smooth_ref[...]
        low = to_low(smooth)
        high[:count, :] = low
        rest[:count, :] = to_low(smooth - low.astype(jnp.float32))

    slots = lax.broadcasted_iota(jnp.int32, (BLOCK, SLOTS), 1)
    chosen = jnp.where(slots == rank_ref[...], 1.0, 0.0).astype(jnp.bfloat16)
    spread = matmul(chosen, high[...]) + matmul(chosen, rest[...])
    out_ref[...] = encoded_ref[...] + confidence_ref[...] * spread


def smooth_back_kernel(
    probs_ref,
    grad_ref,
    confidence_ref,
    rank_ref,
    smooth_ref,
    down_ref,
    grad_down_ref,
    grad_confidence_ref,
    grad_probs_ref,
    total,
    low,
):
    count = down_ref.shape[0]
    width = down_ref.shape[1]
    step = pl.program_id(0)

    @pl.when(step == 0)
    def _():
        total[...] = jnp.zeros_like(total)
        low[:count, :] = to_low(smooth_ref[...])
        low[count:, :] = jnp.zeros((SLOTS - count, width), jnp.bfloat16)

    slots = lax.broadcasted_iota(jnp.int32, (BLOCK, SLOTS), 1)
    chosen = jnp.where(slots == rank_ref[...], 1.0, 0.0).astype(jnp.bfloat16)
    gradient = grad_ref[...]
    total[...] += left_product(chosen, to_low(confidence_ref[...] * gradient))
    grad_confidence_ref[...] = jnp.sum(gradient * matmul(chosen, low[...]), axis=1, keepdims=True)

    @pl.when(step == pl.num_programs(0) - 1)
    def _():
        tiles = count // 16

        def tile(index, later):
            index = tiles - 1 - index
            start = pl.multiple_of(index * 16, 16)
            rows = total[pl.ds(start, 16), :]
            done = [None] * 16
            kept = [None] * 16
            for r in range(15, -1, -1):
                later = rows[r : r + 1] + (1.0 - probs_ref[start + r + 1]) * later
                kept[r] = later
                done[r] = probs_ref[start + r] * later
            grad_down_ref[pl.ds(start, 16), :] = to_low(jnp.concatenate(done, 0))
            total[pl.ds(start, 16), :] = jnp.concatenate(kept, 0)
            return later

        lax.fori_loop(0, tiles, tile, jnp.zeros((1, width), jnp.float32))
        smooth = smooth_ref[...]
        places = lax.broadcasted_iota(jnp.int32, (count, 1), 0)
        before = jnp.where(places == 0, 0.0, pltpu.roll(smooth, 1, 0))
        grad_probs_ref[...] = jnp.sum(
            total[:count, :] * (down_ref[...] - before), axis=1, keepdims=True
        )


def byte_rows(size):
    return pl.BlockSpec((BLOCK, size), lambda step: (step, 0))


def kernel_settings(flops, traffic):
    return dict(
        compiler_params=pltpu.CompilerParams(
            dimension_semantics=("arbitrary",), vmem_limit_bytes=48 * 1024 * 1024
        ),
        cost_estimate=pl.CostEstimate(flops=flops, bytes_accessed=traffic, transcendentals=0),
    )


def smooth_forward(probs, down_rows, encoded, confidence, rank):
    length, width = encoded.shape
    count = down_rows.shape[0]
    wide = jnp.float32
    return pl.pallas_call(
        smooth_kernel,
        grid=(length // BLOCK,),
        in_specs=[
            pl.BlockSpec(memory_space=pltpu.SMEM),
            whole_block(count, width),
            byte_rows(width),
            byte_rows(1),
            byte_rows(1),
        ],
        out_specs=[byte_rows(width), whole_block(count, width)],
        out_shape=[
            jax.ShapeDtypeStruct((length, width), wide),
            jax.ShapeDtypeStruct((count, width), wide),
        ],
        scratch_shapes=[pltpu.VMEM((SLOTS, width), jnp.bfloat16)] * 2,
        **kernel_settings(4 * length * SLOTS * width, length * width * 8),
    )(probs, down_rows, encoded, confidence, rank)


def smooth_backward(probs, gradient, confidence, rank, smooth, down_rows):
    length, width = gradient.shape
    count = down_rows.shape[0]
    wide = jnp.float32
    return pl.pallas_call(
        smooth_back_kernel,
        grid=(length // BLOCK,),
        in_specs=[
            pl.BlockSpec(memory_space=pltpu.SMEM),
            byte_rows(width),
            byte_rows(1),
            byte_rows(1),
            whole_block(count, width),
            whole_block(count, width),
        ],
        out_specs=[whole_block(count, width), byte_rows(1), whole_block(count, 1)],
        out_shape=[
            jax.ShapeDtypeStruct((count, width), jnp.bfloat16),
            jax.ShapeDtypeStruct((length, 1), wide),
            jax.ShapeDtypeStruct((count, 1), wide),
        ],
        scratch_shapes=[pltpu.VMEM((SLOTS, width), wide), pltpu.VMEM((SLOTS, width), jnp.bfloat16)],
        **kernel_settings(4 * length * SLOTS * width, length * width * 4),
    )(probs, gradient, confidence, rank, smooth, down_rows)


def turned(values, cosines, sines):
    lane = lax.broadcasted_iota(jnp.int32, values.shape, 1) % HEAD_SIZE
    swapped = jnp.where(
        lane < HEAD_SIZE // 2,
        pltpu.roll(values, LANES - HEAD_SIZE // 2, 1),
        pltpu.roll(values, HEAD_SIZE // 2, 1),
    )
    return values * cosines + swapped * sines


def attend_mask(items_ref, items_row_ref):
    size = items_ref.shape[0]
    rows = lax.broadcasted_iota(jnp.int32, (size, size), 0)
    cols = lax.broadcasted_iota(jnp.int32, (size, size), 1)
    return (rows >= cols) & (items_ref[...] == items_row_ref[0:1, :])


def softmaxed(queries, keys, visible):
    scores = right_product(queries, keys) * HEAD_SIZE ** (-0.5)
    scores = jnp.where(visible, scores, -1e30)
    weights = jnp.exp(scores - jnp.max(scores, axis=1, keepdims=True))
    return weights / jnp.sum(weights, axis=1, keepdims=True)


def half_lanes(values, half):
    lane = lax.broadcasted_iota(jnp.int32, (1, LANES), 1) // HEAD_SIZE
    return jnp.where(lane == half, values, jnp.zeros_like(values))


HEADS_PER_BLOCK = 3
BLOCK_WIDTH = 2 * LANES


def unpacked(block, cosines, sines):
    width = HEADS_PER_BLOCK * HEAD_SIZE
    size = block.shape[1]
    queries = block[:, :BLOCK_WIDTH]
    keys = pltpu.roll(block, size - width, 1)[:, :BLOCK_WIDTH]
    values = pltpu.roll(block, size - 2 * width, 1)[:, :BLOCK_WIDTH]
    tiles = []
    for tile in range(2):
        lanes = slice(tile * LANES, (tile + 1) * LANES)
        tiles.append(
            (
                to_low(turned(queries[:, lanes], cosines, sines)),
                to_low(turned(keys[:, lanes], cosines, sines)),
                to_low(values[:, lanes]),
            )
        )
    return tiles


def attend_kernel(qkv_ref, cos_ref, sin_ref, items_ref, items_row_ref, out_ref):
    visible = attend_mask(items_ref, items_row_ref)
    tiles = unpacked(qkv_ref[...], cos_ref[...], sin_ref[...])
    for tile, (queries, keys, values) in enumerate(tiles):
        mixed = 0.0
        for half in range(2 - tile):
            weights = softmaxed(half_lanes(queries, half), keys, visible)
            mixed = mixed + matmul(to_low(weights), half_lanes(values, half))
        out_ref[:, tile * LANES : (tile + 1) * LANES] = to_low(mixed)


def attend_back_kernel(
    qkv_ref, grad_ref, cos_ref, sin_ref, items_ref, items_row_ref, grad_qkv_ref
):
    visible = attend_mask(items_ref, items_row_ref)
    cosines = cos_ref[...]
    sines = sin_ref[...]
    scale = HEAD_SIZE ** (-0.5)
    tiles = unpacked(qkv_ref[...], cosines, sines)
    grads = ([], [], [])
    for tile, (queries, keys, values) in enumerate(tiles):
        gradient = to_low(grad_ref[:, tile * LANES : (tile + 1) * LANES])
        grad_q = 0.0
        grad_k = 0.0
        grad_v = 0.0
        for half in range(2 - tile):
            own_queries = half_lanes(queries, half)
            own_grad = half_lanes(gradient, half)
            weights = softmaxed(own_queries, keys, visible)
            grad_weights = right_product(own_grad, values)
            grad_v = grad_v + left_product(to_low(weights), own_grad)
            inner = jnp.sum(grad_weights * weights, axis=1, keepdims=True)
            grad_scores = to_low(jnp.where(visible, weights * (grad_weights - inner), 0.0))
            grad_q = grad_q + matmul(grad_scores, half_lanes(keys, half))
            grad_k = grad_k + left_product(grad_scores, own_queries)
        grads[0].append(turned(grad_q * scale, cosines, -sines))
        grads[1].append(turned(grad_k * scale, cosines, -sines))
        grads[2].append(grad_v)
    size = qkv_ref.shape[1]
    width = HEADS_PER_BLOCK * HEAD_SIZE
    filling = jnp.zeros((qkv_ref.shape[0], size - BLOCK_WIDTH), jnp.float32)
    packed = 0.0
    for kind, both in enumerate(grads):
        wide = jnp.concatenate(both + [filling], 1)
        packed = packed + (pltpu.roll(wide, kind * width, 1) if kind else wide)
    grad_qkv_ref[...] = to_low(packed)


def turn_tables(count):
    half = HEAD_SIZE // 2
    lane = jnp.arange(LANES) % HEAD_SIZE
    frequency = 10000.0 ** (-(lane % half).astype(jnp.float32) * (2.0 / HEAD_SIZE))
    angles = jnp.arange(count, dtype=jnp.float32)[:, None] * frequency[None, :]
    return jnp.cos(angles), jnp.where(lane < half, -1.0, 1.0)[None, :] * jnp.sin(angles)


def attend(qkv, gradient, tables, group_items, depths):
    count, width = qkv.shape
    size = width // depths

    def tiles(columns):
        return pl.BlockSpec((count, columns), lambda step: (0, step))

    backward = gradient is not None
    items = group_items.astype(jnp.int32)
    out = size if backward else BLOCK_WIDTH
    return pl.pallas_call(
        attend_back_kernel if backward else attend_kernel,
        grid=(depths,),
        in_specs=[tiles(size)]
        + [tiles(BLOCK_WIDTH)] * backward
        + [whole_block(count, LANES)] * 2
        + [whole_block(count, 1), whole_block(8, count)],
        out_specs=tiles(out),
        out_shape=jax.ShapeDtypeStruct((count, depths * out), jnp.bfloat16),
        **kernel_settings(8 * count * count * width, count * width * 16),
    )(
        qkv,
        *([gradient] if backward else []),
        *tables,
        items[:, None],
        jnp.broadcast_to(items[None, :], (8, count)),
    )


def active_kernel(pair_ref, out_ref):
    size = out_ref.shape[1]
    gate = pair_ref[:, :size]
    out_ref[...] = to_low(gate * sigmoid(gate) * pair_ref[:, size:])


def active_back_kernel(pair_ref, grad_ref, out_ref):
    size = grad_ref.shape[1]
    gate = pair_ref[:, :size]
    upper = pair_ref[:, size:]
    opened = sigmoid(gate)
    gradient = grad_ref[...]
    out_ref[:, :size] = to_low(
        gradient * upper * (opened + gate * opened * (1.0 - opened))
    )
    out_ref[:, size:] = to_low(gradient * gate * opened)


def activate(pairs, gradient, depths):
    count, width = pairs.shape
    size = width // depths // 2

    def tiles(columns):
        return pl.BlockSpec((count, columns), lambda step: (0, step))

    backward = gradient is not None
    out = 2 * size if backward else size
    return pl.pallas_call(
        active_back_kernel if backward else active_kernel,
        grid=(depths,),
        in_specs=[tiles(2 * size)] + [tiles(size)] * backward,
        out_specs=tiles(out),
        out_shape=jax.ShapeDtypeStruct((count, depths * out), jnp.bfloat16),
        **kernel_settings(count * width * 8, count * width * 8),
    )(pairs, *([gradient] if backward else []))


def dots_kernel(depths, qk_ref, out_ref, tail):
    size = qk_ref.shape[1] // depths // 2

    @pl.when(pl.program_id(0) == 0)
    def _():
        tail[...] = jnp.zeros_like(tail)

    sums = [0.0, 0.0, 0.0]
    for k in range(depths):
        queries = qk_ref[:, 2 * k * size : (2 * k + 1) * size]
        keys = qk_ref[:, (2 * k + 1) * size : (2 * k + 2) * size]
        lanes = slice(k * size, (k + 1) * size)
        previous = shifted_down(tail[:, lanes], keys, 1)
        tail[:, lanes] = keys[BLOCK - 8 :]
        sums[0] = sums[0] + queries * previous
        sums[1] = sums[1] + queries * queries
        sums[2] = sums[2] + previous * previous
    for kind in range(3):
        out_ref[:, kind : kind + 1] = jnp.sum(sums[kind], axis=1, keepdims=True)
    out_ref[:, 3:] = jnp.zeros((BLOCK, 5), jnp.float32)


def dots_back_kernel(depths, qk_ref, tail_ref, grad_ref, later_ref, out_ref, head):
    size = qk_ref.shape[1] // depths // 2
    step = pl.program_id(0)
    first_block = step == pl.num_programs(0) - 1

    @pl.when(step == 0)
    def _():
        head[...] = jnp.zeros_like(head)

    for k in range(depths):
        query_lanes = slice(2 * k * size, (2 * k + 1) * size)
        key_lanes = slice((2 * k + 1) * size, (2 * k + 2) * size)
        lanes = slice(k * size, (k + 1) * size)
        queries = qk_ref[:, query_lanes]
        keys = qk_ref[:, key_lanes]
        tail = jnp.where(first_block, 0.0, tail_ref[:, key_lanes])
        previous = shifted_down(tail, keys, 1)
        following = shifted_up(queries, head[:, lanes], 1)
        head[:, lanes] = queries[:8]
        out_ref[:, query_lanes] = to_low(
            grad_ref[:, 0:1] * previous + 2.0 * grad_ref[:, 1:2] * queries
        )
        out_ref[:, key_lanes] = to_low(
            later_ref[:, 0:1] * following + 2.0 * later_ref[:, 2:3] * keys
        )


def pair_dots(qk, depths):
    length, width = qk.shape
    return pl.pallas_call(
        functools.partial(dots_kernel, depths),
        grid=(length // BLOCK,),
        in_specs=[byte_rows(width)],
        out_specs=byte_rows(8),
        out_shape=jax.ShapeDtypeStruct((length, 8), jnp.float32),
        scratch_shapes=[pltpu.VMEM((8, width // 2), jnp.float32)],
        **kernel_settings(length * width * 4, length * width * 4),
    )(qk)


def pair_dots_back(qk, gradient, depths):
    length, width = qk.shape
    chunks = length // BLOCK
    eighths = BLOCK // 8
    later = jnp.concatenate([gradient[1:], jnp.zeros((1, 8), jnp.float32)], 0)

    def rows(size):
        return pl.BlockSpec((BLOCK, size), lambda step: (chunks - 1 - step, 0))

    return pl.pallas_call(
        functools.partial(dots_back_kernel, depths),
        grid=(chunks,),
        in_specs=[
            rows(width),
            pl.BlockSpec(
                (8, width), lambda step: (jnp.maximum((chunks - 1 - step) * eighths - 1, 0), 0)
            ),
            rows(8),
            rows(8),
        ],
        out_specs=rows(width),
        out_shape=jax.ShapeDtypeStruct((length, width), jnp.bfloat16),
        scratch_shapes=[pltpu.VMEM((8, width // 2), jnp.float32)],
        **kernel_settings(length * width * 4, length * width * 8),
    )(qk, qk, gradient, later)


def core_swap(values):
    size = lax.axis_size("dp")
    return lax.ppermute(values, "dp", [(d, d ^ 1) for d in range(size)])


def chip_swap(values, bit):
    size = lax.axis_size("dp")
    return lax.ppermute(values, "dp", [(d, d ^ (bit * 2)) for d in range(size)])


def depth_swap(values, offset):
    if offset == 0:
        return values
    size = lax.axis_size("mp")
    return lax.ppermute(values, "mp", [(d, d ^ offset) for d in range(size)])


class Place:
    def __init__(self):
        dp_index = lax.axis_index("dp")
        self.core = dp_index % 2
        self.chip = dp_index // 2
        self.depth = lax.axis_index("mp")
        self.chips = lax.axis_size("dp") // 2
        self.depths = lax.axis_size("mp")
        bits = []
        while 2 ** len(bits) < self.chips:
            bits.append(2 ** len(bits))
        self.bits = bits


def both_cores(place, own, other, axis):
    first = place.core == 0
    return jnp.concatenate([jnp.where(first, own, other), jnp.where(first, other, own)], axis)


def pick(values, index, size, axis):
    return lax.dynamic_slice_in_dim(values, index * size, size, axis)


def reorder(values, count, shift, axis=-1):
    axis = axis % values.ndim
    size = values.shape[axis] // count
    return jnp.concatenate([pick(values, r ^ shift, size, axis) for r in range(count)], axis)


def relative_to_chip(place, values):
    if place.chips == place.depths:
        return reorder(values, place.chips, place.chip ^ place.depth)
    return reorder(reorder(values, place.depths, place.depth), place.chips, place.chip)


def chip_to_relative(place, values):
    if place.chips == place.depths:
        return reorder(values, place.chips, place.chip ^ place.depth)
    return reorder(reorder(values, place.chips, place.chip), place.depths, place.depth)


def depth_to_chip(place, values):
    return reorder(values, place.chips, place.chip)


def split_columns(place, shards):
    axis = shards[0].ndim - 1

    def columns(core):
        return jnp.concatenate([pick(s, core, s.shape[-1] // 2, axis) for s in shards], axis)

    other = core_swap(columns(1 - place.core))
    return both_cores(place, columns(place.core), other, axis - 1)


def split_rows(place, shard):
    half = shard.shape[-2] // 2
    own = pick(shard, place.core, half, shard.ndim - 2)
    other = core_swap(pick(shard, 1 - place.core, half, shard.ndim - 2))
    return both_cores(place, own, other, shard.ndim - 1)


def join_columns(place, block):
    half = block.shape[-2] // 2
    own = pick(block, place.core, half, block.ndim - 2)
    other = core_swap(pick(block, 1 - place.core, half, block.ndim - 2))
    return both_cores(place, own, other, block.ndim - 1)


def join_rows(place, block):
    half = block.shape[-1] // 2
    own = pick(block, place.core, half, block.ndim - 1)
    other = core_swap(pick(block, 1 - place.core, half, block.ndim - 1))
    return both_cores(place, own, other, block.ndim - 2)


def padded_rows(rows):
    return -(-rows // LANES) * LANES


def assemble_kernel(places, items, size, *refs):
    sources = refs[: len(places)]
    outs = refs[len(places) :]
    rows = sources[0].shape[1]
    for (r, first, count), ref in zip(places, sources):

        @pl.when(pl.program_id(0) == r)
        def _(first=first, count=count, ref=ref):
            offset = 0
            for (kind, width), out_ref in zip(items, outs):
                if kind == "folded":
                    half = rows // 2
                    for k in range(count):
                        j = (first + k) * (width + width // 2)
                        out_ref[:, j : j + width] = ref[k, :half, offset : offset + width]
                        out_ref[:, j + width : j + width + width // 2] = ref[
                            k, half:, offset : offset + width // 2
                        ]
                    offset += width
                    continue
                for k in range(count):
                    i = (first + k) * size if kind == "rows" else 0
                    j = (first + k) * width if kind == "columns" else 0
                    out_ref[i : i + rows, j : j + width] = ref[k, :, offset : offset + width]
                    if size > rows:
                        out_ref[i + rows : i + size, j : j + width] = jnp.zeros(
                            (size - rows, width), jnp.bfloat16
                        )
                offset += width


def assemble(place, pieces, items, filled):
    chips, depths = place.chips, place.depths
    rows = pieces[0][2].shape[1]
    size = padded_rows(rows) if filled else rows
    if any(width % LANES for _, width in items):
        matrices = []
        offset = 0
        for kind, width in items:
            arrays = [
                jnp.pad(a[:, :, offset : offset + width], ((0, 0), (0, size - rows), (0, 0)))
                for _, _, a in pieces
            ]
            if kind == "rows":
                arrays = [a.reshape(depths * size, width) for a in arrays]
                matrices.append(jnp.concatenate(arrays, 1))
            else:
                arrays = [jnp.concatenate([a[k] for k in range(depths)], 1) for a in arrays]
                matrices.append(jnp.concatenate(arrays, 0))
            offset += width
        return matrices
    shapes = []
    blocks = []
    for kind, width in items:
        if kind == "rows":
            shapes.append((depths * size, chips * width))
            blocks.append(pl.BlockSpec((depths * size, width), lambda i: (0, i)))
        elif kind == "folded":
            whole = depths * (width + width // 2)
            shapes.append((chips * size // 2, whole))
            blocks.append(pl.BlockSpec((size // 2, whole), lambda i: (i, 0)))
        else:
            shapes.append((chips * size, depths * width))
            blocks.append(pl.BlockSpec((size, depths * width), lambda i: (i, 0)))
    places = [(r, first, array.shape[0]) for r, first, array in pieces]
    return pl.pallas_call(
        functools.partial(assemble_kernel, places, items, size),
        grid=(chips,),
        in_specs=[whole_block(*array.shape) for _, _, array in pieces],
        out_specs=blocks,
        out_shape=[jax.ShapeDtypeStruct(shape, jnp.bfloat16) for shape in shapes],
        **kernel_settings(0, sum(4 * a * b for a, b in shapes)),
    )(*[array for _, _, array in pieces])


def held_for(values, earlier):
    if not earlier:
        return values
    return lax.optimization_barrier((values, *earlier))[0]


class Gather:
    def __init__(self, place):
        self.place = place
        self.near = []
        self.far = []

    def hold(self, values, waits=()):
        return held_for(values, sum(self.near[-1:] + self.far[-2:-1], list(waits)))

    def pieces(self, shard, waits):
        place = self.place
        shard = self.hold(shard, waits)
        stack = lax.all_gather(shard, "mp", axis=0)
        if place.chips == 4:
            half = place.depths // 2
            along = [chip_swap(stack, bit) for bit in (1, 2)]
            across = [chip_swap(along[0][:half], 2), chip_swap(along[1][half:], 1)]
            self.near.append([stack])
            self.far.append(along)
            return [
                (0, 0, stack),
                (1, 0, along[0]),
                (2, 0, along[1]),
                (3, 0, across[0]),
                (3, half, across[1]),
            ]
        pieces = {0: stack}
        for bit in place.bits:
            for r, piece in list(pieces.items()):
                pieces[r ^ bit] = chip_swap(piece, bit)
        self.near.append([stack])
        return [(r, 0, pieces[r]) for r in range(place.chips)]

    def matrices(self, shards, waits=(), filled=False):
        rows = shards[0][1].shape[0]
        folded = [kind == "folded" for kind, _ in shards]
        for index, (kind, shard) in enumerate(shards):
            if kind == "folded":
                third = shard.shape[1] // 3
                if 2 * shard.shape[0] == rows and third % LANES == 0:
                    last = jnp.pad(shard[:, 2 * third :], ((0, 0), (0, third)))
                    shard = jnp.concatenate([shard[:, : 2 * third], last], 0)
                else:
                    kind = "columns"
                shards = shards[:index] + [(kind, shard)] + shards[index + 1 :]
        if len({shard.shape[0] for _, shard in shards}) > 1:
            return [
                self.matrices([item], waits, filled or flag)[0]
                for item, flag in zip(shards, folded)
            ]
        items = [(kind, shard.shape[1]) for kind, shard in shards]
        packed = jnp.concatenate([shard for _, shard in shards], 1)
        return assemble(self.place, self.pieces(packed, waits), items, filled)


def gather_chips(place, shard, bits):
    pieces = {0: shard}
    for bit in bits:
        for r, piece in list(pieces.items()):
            pieces[r ^ bit] = chip_swap(piece, bit)
    return jnp.concatenate([pieces[r] for r in range(place.chips)], -2)


def send_order(place, bits):
    order = [0]
    for bit in reversed(bits):
        order = order + [r ^ bit for r in order]
    return order


def chosen(step, values):
    result = 0
    for index, value in enumerate(values):
        result = result + jnp.where(step == index, value, 0)
    return result


def products_kernel(kinds, rows, *refs):
    out_ref = refs[-1]
    offset = 0
    for index, kind in enumerate(kinds):
        chip_side = refs[2 * index][...]
        depth_side = refs[2 * index + 1][...]
        if kind == "columns":
            block = left_product(chip_side, depth_side)
        else:
            block = left_product(depth_side, chip_side)
        width = block.shape[1]
        out_ref[0, :, offset : offset + width] = to_low(block[:rows])
        offset += width


class Scatter:
    def __init__(self, place):
        self.place = place
        self.near = []
        self.far = []

    def blocks(self, items, rows, chips, depths):
        place = self.place
        steps = [(r, k) for r in chips for k in depths]
        sizes = []
        aligned = True
        for kind, chip_side, depth_side in items:
            a = chip_side.shape[1] // place.chips
            b = depth_side.shape[1] // place.depths
            sizes.append((a, b, b if kind == "columns" else a))
            aligned = aligned and a % LANES == 0 and b % LANES == 0
        if not aligned:
            parts = []
            for (kind, chip_side, depth_side), (a, b, _) in zip(items, sizes):
                if kind == "columns":
                    whole = left_product(chip_side, depth_side)
                    whole = whole.reshape(place.chips, a, place.depths, b).transpose(0, 2, 1, 3)
                else:
                    whole = left_product(depth_side, chip_side)
                    whole = whole.reshape(place.depths, b, place.chips, a).transpose(2, 0, 1, 3)
                parts.append(to_low(whole[:, :, :rows]))
            whole = jnp.concatenate(parts, 3)
            return jnp.stack([jnp.stack([whole[r, k] for k in depths]) for r in chips])
        width = sum(size[2] for size in sizes)
        specs = []
        for (kind, chip_side, depth_side), (a, b, _) in zip(items, sizes):
            count = chip_side.shape[0]
            specs.append(
                pl.BlockSpec((count, a), lambda s: (0, chosen(s, [r for r, _ in steps])))
            )
            specs.append(
                pl.BlockSpec((count, b), lambda s: (0, chosen(s, [k for _, k in steps])))
            )
        count = items[0][1].shape[0]
        out = pl.pallas_call(
            functools.partial(products_kernel, [kind for kind, _, _ in items], rows),
            grid=(len(steps),),
            in_specs=specs,
            out_specs=pl.BlockSpec((1, rows, width), lambda s: (s, 0, 0)),
            out_shape=jax.ShapeDtypeStruct((len(steps), rows, width), jnp.bfloat16),
            **kernel_settings(
                2 * len(steps) * count * rows * width, len(steps) * (rows + count) * width * 2
            ),
        )(*[side for _, *sides in items for side in sides])
        return out.reshape(len(chips), len(depths), rows, width)

    def own(self, items, all_rows, waits=(), reduced=False):
        if len(set(all_rows)) > 1:
            parts = [self.own([item], [n], waits, reduced)[0] for item, n in zip(items, all_rows)]
            return parts
        place = self.place
        rows = all_rows[0]
        kind, chip_side, depth_side = items[0]
        chip_side = held_for(chip_side, sum(self.near[-2:-1] + self.far[-3:-2], list(waits)))
        items = [(kind, chip_side, depth_side)] + list(items[1:])
        half = place.depths // 2
        orders = (place.bits[::-1], place.bits)
        depth_sets = (range(half), range(half, place.depths))
        middle = place.chips // 2
        order_lists = [send_order(place, bits) for bits in orders]
        sents = [
            self.blocks(items, rows, order[middle:], ks)
            for order, ks in zip(order_lists, depth_sets)
        ]
        kepts = [
            self.blocks(items, rows, order[:middle], ks)
            for order, ks in zip(order_lists, depth_sets)
        ]
        got = []
        for step in range(len(place.bits)):
            got = [chip_swap(sent, bits[step]) for sent, bits in zip(sents, orders)]
            sums = [a.astype(jnp.float32) + b.astype(jnp.float32) for a, b in zip(kepts, got)]
            middle = middle // 2
            sents = [to_low(total[middle:]) for total in sums]
            kepts = [total[:middle] for total in sums] if middle else sums
            if step == 0:
                self.near.append(sents)
        by_depth = jnp.concatenate([total[0] for total in kepts], 0)
        if reduced:
            going = to_low(by_depth)
            self.far.append([going])
            total = lax.psum_scatter(going, "mp", scatter_dimension=0).astype(jnp.float32)
        else:
            blocks = [
                lax.dynamic_index_in_dim(by_depth, place.depth ^ k, 0, keepdims=False)
                for k in range(place.depths)
            ]
            going = [to_low(block) for block in blocks[1:]]
            arrived = [depth_swap(block, k + 1) for k, block in enumerate(going)]
            self.far.append(going)
            total = blocks[0]
            for values in arrived:
                total = total + values.astype(jnp.float32)
        parts = []
        offset = 0
        for kind, chip_side, depth_side in items:
            side = (depth_side, place.depths) if kind == "columns" else (chip_side, place.chips)
            width = side[0].shape[1] // side[1]
            parts.append(total[:, offset : offset + width])
            offset += width
        return parts


def scatter_rest(place, kept, sent, bits, chip_axis, over_depth=True):
    for step, bit in enumerate(bits):
        if step > 0:
            half = kept.shape[chip_axis] // 2
            sent = to_low(lax.slice_in_dim(kept, half, 2 * half, axis=chip_axis))
            kept = lax.slice_in_dim(kept, 0, half, axis=chip_axis)
        kept = kept + chip_swap(sent, bit).astype(jnp.float32)
    if not over_depth:
        return kept
    axis = 1 - chip_axis
    size = kept.shape[axis] // place.depths
    total = lax.slice_in_dim(kept, 0, size, axis=axis)
    for k in range(1, place.depths):
        block = to_low(lax.slice_in_dim(kept, k * size, (k + 1) * size, axis=axis))
        total = total + depth_swap(block, k).astype(jnp.float32)
    return total


def core_sum(partial):
    return partial + core_swap(to_low(partial)).astype(jnp.float32)


def core_sum_exact(partial):
    return partial + core_swap(partial)


def parity_part(place, values):
    size = values.shape[1] // (2 * place.chips)
    split = values.reshape(values.shape[0], place.chips, 2, size)
    own = lax.dynamic_index_in_dim(split, place.core, 2, keepdims=False)
    own = jnp.pad(own, ((0, 0), (0, 0), (0, padded_rows(size) - size)))
    return own.reshape(values.shape[0], -1)


def parity_join(place, own, size):
    rows = own.shape[0]
    own = own.reshape(rows, place.chips, -1)[:, :, :size]
    other = core_swap(own)
    return both_cores(place, own[:, :, None], other[:, :, None], 2).reshape(rows, -1)


def other_rows(place, values):
    micro, length, width = values.shape
    halves = values.reshape(micro, 2, length // 2, width)
    return core_swap(lax.dynamic_index_in_dim(halves, 1 - place.core, 1, keepdims=True))


def own_sequence(place, values, other):
    micro, length, width = values.shape
    halves = values.reshape(micro, 2, length // 2, width)
    own = lax.dynamic_index_in_dim(halves, place.core, 1, keepdims=True)
    half = both_cores(place, own, other, 1).reshape(micro * 2, length // 2, width)
    blocks = [
        depth_swap(lax.dynamic_index_in_dim(half, place.depth ^ k, 0, keepdims=False), k)
        for k in range(place.depths)
    ]
    rows = relative_to_chip(place, jnp.concatenate(blocks, 1))
    return both_cores(place, rows, core_swap(rows), 0)


def back_to_all(place, values, micro):
    length = values.shape[0]
    rows = chip_to_relative(place, pick(values, place.core, length // 2, 0))
    width = rows.shape[1] // place.depths
    blocks = [
        depth_swap(rows[:, k * width : (k + 1) * width], k)[None] for k in range(place.depths)
    ]
    by_sequence = reorder(jnp.concatenate(blocks, 0), place.depths, place.depth, 0)
    by_sequence = by_sequence.reshape(micro, 2, length // 2, width)
    own = lax.dynamic_index_in_dim(by_sequence, place.core, 1, keepdims=False)
    other = core_swap(lax.dynamic_index_in_dim(by_sequence, 1 - place.core, 1, keepdims=False))
    return both_cores(place, own, other, 1)


def own_row(place, values):
    both = both_cores(place, values[None], core_swap(values)[None], 0)
    both = jnp.swapaxes(both, 0, 1).reshape((-1,) + values.shape[1:])
    return lax.dynamic_index_in_dim(both, place.depth, 0, keepdims=False)


def own_channels(place, values):
    size = values.shape[-1] // (2 * place.depths)
    return jnp.concatenate(
        [
            pick(values, k * 2 + place.core, size, values.ndim - 1)
            for k in range(place.depths)
        ],
        -1,
    )


def all_channels(place, values):
    size = values.shape[-1] // place.depths
    full = jnp.zeros(values.shape[:-1] + (2 * values.shape[-1],), values.dtype)
    for k in range(place.depths):
        block = values[..., k * size : (k + 1) * size]
        full = lax.dynamic_update_slice_in_dim(
            full, block, (k * 2 + place.core) * size, values.ndim - 1
        )
    return full


def sum_everywhere(place, values):
    values = core_sum_exact(values)
    for bit in place.bits:
        values = values + chip_swap(values, bit)
    offset = 1
    while offset < place.depths:
        values = values + depth_swap(values, offset)
        offset *= 2
    return values


def norm_forward(values, gain):
    low = to_low(values)
    wide = low.astype(jnp.float32)
    scale = lax.rsqrt(jnp.mean(wide * wide, axis=-1, keepdims=True) + EPSILON)
    return to_low(wide * scale * gain), (low, scale)


def norm_backward(gradient, memory, gain):
    low, scale = memory
    wide = low.astype(jnp.float32)
    weighted = gradient * gain
    inner = jnp.mean(weighted * wide, axis=-1, keepdims=True)
    grad_gain = jnp.sum(gradient * (wide * scale), axis=0)
    return scale * weighted - wide * (scale * scale * scale * inner), grad_gain


def mamba_forward(place, residual, weights, params, items):
    w_zx, w_bcdt, w_out = weights
    norm, taps, map_taps, heads, channels, owner = params
    columns, ahead, segment_rows = items
    normed_low, norm_memory = norm_forward(residual, norm)
    zx_proj = matmul(normed_low, w_zx)
    bcdt = matmul(normed_low, w_bcdt)
    per_block = channels.shape[1] // place.depths // LANES
    mixed, y, squares, states = mix_forward(
        per_block, zx_proj, bcdt, columns, segment_rows, taps, map_taps, heads, channels
    )
    scale = lax.rsqrt(core_sum_exact(squares) / (2 * mixed.shape[1]) + EPSILON)
    result = residual + core_sum(matmul(mixed, w_out)) * scale
    return (result, (normed_low, mixed, norm_memory, scale, zx_proj, bcdt, y, states))


def mamba_backward(place, gradient, weights, params, items, memory, scatter, more, reduced):
    w_zx, w_bcdt, w_out = weights
    norm, taps, map_taps, heads, channels, owner = params
    columns, ahead, segment_rows = items
    normed_low, mixed, norm_memory, scale, zx_proj, bcdt, y, states = memory
    spread = to_low(gradient)
    grad_mixed = right_product(spread, w_out)
    width = mixed.shape[1]
    inner = core_sum_exact(
        jnp.sum(grad_mixed * mixed.astype(jnp.float32), axis=1, keepdims=True)
    )
    coefficient = scale * scale * scale * inner / (2 * width)
    nothing = jnp.zeros_like(scale[:, 0])
    later = jnp.stack(ahead + [scale[:, 0], coefficient[:, 0], nothing, nothing, nothing], 1)
    grad_zx, grad_maps, grad_dt, grad_taps, grad_map_taps, grad_heads, grad_channels = (
        mix_backward(
            width // place.depths // LANES,
            grad_mixed,
            zx_proj,
            bcdt,
            y,
            states,
            columns,
            later,
            segment_rows,
            taps,
            map_taps,
            heads,
            channels,
            owner,
        )
    )
    head_count = width // HEAD_SIZE
    grad_maps = core_sum_exact(grad_maps)
    own_maps = to_low(pick(grad_maps, place.core, LANES, 1))
    low_dt = to_low(grad_dt)
    grad_bcdt = jnp.concatenate([own_maps, low_dt], 1)
    own_bcdt = jnp.concatenate([pick(w_bcdt, place.core, LANES, 1), w_bcdt[:, 2 * LANES :]], 1)
    partial = right_product(grad_zx, w_zx) + right_product(grad_bcdt, own_bcdt)
    grad_in, grad_norm = norm_backward(core_sum(partial), norm_memory, norm)
    small_from = jnp.concatenate([own_maps, low_dt[:, :head_count]], 1)
    scaled = to_low(spread.astype(jnp.float32) * scale)
    rows = normed_low.shape[1] // place.chips
    weight_grads = scatter.own(
        [("columns", normed_low, grad_zx), ("rows", scaled, mixed)] + more,
        [rows, width // place.depths] + [rows] * len(more),
        [partial],
        reduced,
    )
    by_tap = grad_taps.reshape(4, 8, -1).sum(1)
    map_by_tap = grad_map_taps.reshape(4, 8, -1).sum(1)
    head_sums = grad_heads.reshape(2, 8, -1).sum(1)[:, :head_count]
    channel_sums = grad_channels.reshape(2, 8, -1).sum(1)
    small_grads = (
        0.5 * grad_norm,
        by_tap,
        map_by_tap,
        head_sums[0],
        head_sums[1],
        channel_sums[0].reshape(head_count, HEAD_SIZE).sum(1),
        channel_sums[1],
    )
    return (gradient + grad_in, weight_grads, small_grads, (normed_low, small_from))


def small_scatter(place, pairs, half_maps, heads):
    bits = place.bits[::-1]
    order = send_order(place, bits)
    wholes = [left_product(normed, small_from) for normed, small_from in pairs]
    whole = jnp.concatenate(wholes, 1)
    size = whole.shape[0] // place.chips
    ordered = [whole[r * size : (r + 1) * size] for r in order]
    half = place.chips // 2
    kept = jnp.concatenate(ordered[:half], 0)
    sent = to_low(jnp.concatenate(ordered[half:], 0))
    block = scatter_rest(place, kept, sent, bits, 0, over_depth=False)
    offset = 1
    while offset < place.depths:
        block = block + depth_swap(block, offset)
        offset *= 2
    width = block.shape[1] // len(pairs)
    layers = jnp.stack([block[:, n * width : (n + 1) * width] for n in range(len(pairs))])
    own_dt = pick(layers[:, :, half_maps:], place.depth, heads // place.depths, 2)
    return join_columns(place, layers[:, :, :half_maps]), join_columns(place, own_dt)


def one_device(
    inputs,
    cotangent,
    boundary_flags,
    segment_ids,
    mamba_norm,
    mamba_z,
    mamba_x,
    mamba_bc,
    mamba_dt,
    mamba_conv_x,
    mamba_conv_bc,
    mamba_dt_bias,
    mamba_a_log,
    mamba_skip,
    mamba_gate_norm,
    mamba_out,
    router_qk,
    group_up,
    group_down,
    attn_norms,
    attn_qkv,
    attn_out,
    ffn_gate_up,
    ffn_down,
):
    place = Place()
    micro = inputs.shape[0]
    wide = jnp.float32

    zx_shard = split_columns(place, [mamba_z[0], mamba_x[0]])
    gather = Gather(place)
    (enc_zx,) = gather.matrices([("columns", zx_shard)])
    residual_low = own_sequence(place, inputs, other_rows(place, inputs))
    residual = residual_low.astype(wide)

    mamba_bc, mamba_dt, mamba_out, router_qk, _ = lax.optimization_barrier(
        (mamba_bc, mamba_dt, mamba_out, router_qk, zx_shard)
    )
    out_shard = split_rows(place, mamba_out)
    router_shard = split_columns(place, [router_qk[0], router_qk[1]])
    enc_out, w_router, w_up = gather.matrices(
        [("rows", out_shard[0]), ("columns", router_shard), ("folded", group_up)]
    )
    dt_shard = split_columns(place, [mamba_dt])
    dt_shard = jnp.concatenate([depth_swap(dt_shard, k) for k in range(place.depths)], -1)
    dt_shard = reorder(dt_shard, place.depths, place.depth)
    bc_shard = both_cores(place, mamba_bc, core_swap(mamba_bc), 1)
    fill = jnp.zeros(dt_shard.shape[:2] + (LANES - dt_shard.shape[2],), jnp.bfloat16)
    w_bcdt = gather_chips(place, jnp.concatenate([bc_shard, dt_shard, fill], -1), place.bits)
    enc_weights = (enc_zx, w_bcdt[0], enc_out)
    qkv_shard = split_columns(place, [attn_qkv[0], attn_qkv[1], attn_qkv[2]])
    qkv_fill = -qkv_shard.shape[1] % LANES
    (w_qkv,) = gather.matrices([("columns", jnp.pad(qkv_shard, ((0, 0), (0, qkv_fill))))])
    w_attn_out, w_down = gather.matrices(
        [("rows", split_rows(place, attn_out)), ("columns", group_down)], filled=True
    )
    boundary_flags, segment_ids = lax.optimization_barrier(
        (boundary_flags, segment_ids, w_bcdt)
    )[:2]
    flag_row = own_row(place, boundary_flags)
    segment = own_row(place, segment_ids)

    mamba_params = []
    for layer in range(2):
        taps = own_channels(place, mamba_conv_x[layer]).astype(wide)
        width = taps.shape[1]
        bias = own_channels(place, mamba_dt_bias[layer]).astype(wide)
        rate = -jnp.exp(own_channels(place, mamba_a_log[layer]).astype(wide))
        skip = own_channels(place, mamba_skip[layer]).astype(wide)
        gain = own_channels(place, mamba_gate_norm[layer]).astype(wide)
        heads = jnp.pad(jnp.stack([bias, rate]), ((0, 6), (0, LANES - bias.shape[0])))
        channels = jnp.pad(jnp.stack([jnp.repeat(skip, HEAD_SIZE), gain]), ((0, 6), (0, 0)))
        owner = (
            jnp.arange(width)[:, None] // HEAD_SIZE == jnp.arange(LANES)[None, :]
        ).astype(jnp.bfloat16)
        mamba_params.append(
            (
                reorder(mamba_norm[layer], place.chips, place.chip).astype(wide),
                taps,
                mamba_conv_bc[layer].astype(wide),
                heads,
                channels,
                owner,
            )
        )
    items = item_columns(segment)
    norm_gains = reorder(attn_norms, place.chips, place.chip).astype(wide)

    starts = jnp.concatenate([jnp.ones((1,), jnp.bool_), segment[1:] != segment[:-1]])
    group_rank = jnp.cumsum(flag_row) - 1
    slots = jnp.arange(CAP, dtype=jnp.int32)
    marked = (group_rank[None, :] == slots[:, None]) & (flag_row[None, :] == 1)
    marked_low = marked.astype(jnp.bfloat16)
    slot_valid = jnp.any(marked, axis=1)
    encoded, enc_memory = mamba_forward(
        place, residual, enc_weights, mamba_params[0], items
    )

    ffn_shard = split_columns(place, [ffn_gate_up[0], ffn_gate_up[1]])
    (w_gate_up,) = gather.matrices([("columns", ffn_shard)], [enc_memory[4]])
    (w_ffn_down,) = gather.matrices([("rows", split_rows(place, ffn_down))], [enc_memory[1]])

    shared = to_low(encoded)
    length = shared.shape[0]
    qk = matmul(shared, w_router)
    all_dots = core_sum_exact(pair_dots(qk, place.depths))
    prob_row, prob_back = jax.vjp(lambda values: boundary_prob(values.T, starts), all_dots)


    group_rows = to_low(matmul(marked_low, shared))
    group_seg = jnp.sum(jnp.where(marked, segment[None, :] + 1, 0), axis=1) - 1
    own_rows = parity_part(place, group_rows)
    hidden = depth_to_chip(place, core_sum(matmul(own_rows, w_up)))

    dec_shard = split_columns(place, [mamba_z[1], mamba_x[1]])
    dec_zx, dec_out = gather.matrices(
        [("columns", dec_shard), ("rows", out_shard[1])], [qk]
    )
    dec_weights = (dec_zx, w_bcdt[1], dec_out)

    first_low, first_memory = norm_forward(hidden, norm_gains[0])
    qkv = matmul(first_low, w_qkv)
    tables = turn_tables(CAP)
    attended_low = attend(qkv, None, tables, group_seg, place.depths)
    hidden_one = hidden + core_sum(matmul(attended_low, w_attn_out))

    cotangent = gather.hold(cotangent, [hidden_one])
    cot_row = own_sequence(place, cotangent, other_rows(place, cotangent)).astype(wide)

    second_low, second_memory = norm_forward(hidden_one, norm_gains[1])
    gate_up = matmul(second_low, w_gate_up)
    active_low = activate(gate_up, None, place.depths)
    hidden_two = hidden_one + core_sum(matmul(active_low, w_ffn_down))
    third_low = parity_part(place, to_low(hidden_two))
    down_rows = depth_to_chip(place, core_sum(matmul(third_low, w_down)))

    group_probs = jnp.sum(jnp.where(marked, prob_row[None, :], 0.0), axis=1)
    group_probs = jnp.pad(jnp.where(slot_valid, group_probs, 1.0), (0, 8))
    confidence = jnp.where(flag_row == 1, prob_row, 1.0 - prob_row)[:, None]
    rank_column = group_rank[:, None]
    decoder_in, smooth = smooth_forward(group_probs, down_rows, encoded, confidence, rank_column)
    decoded, dec_memory = mamba_forward(
        place, decoder_in, dec_weights, mamba_params[1], items
    )
    outputs = back_to_all(place, to_low(decoded), micro)

    scatter = Scatter(place)
    gradient, dec_grads, dec_smalls, dec_maps = mamba_backward(
        place,
        cot_row,
        dec_weights,
        mamba_params[1],
        items,
        dec_memory,
        scatter,
        [],
        True,
    )
    grad_down, grad_confidence, grad_slots = smooth_backward(
        group_probs, gradient, confidence, rank_column, smooth, down_rows
    )
    grad_probs = jnp.where(flag_row == 1, grad_confidence[:, 0], -grad_confidence[:, 0])
    grad_probs = grad_probs + jnp.sum(jnp.where(marked, grad_slots, 0.0), axis=0)

    dm_rows = hidden.shape[1] // place.chips
    down_low = depth_to_chip(place, grad_down)
    grad_third = to_low(right_product(down_low, w_down))
    grad_hidden = parity_join(place, grad_third, dm_rows // 2).astype(wide)
    spread = to_low(grad_hidden)
    grad_pairs = activate(gate_up, right_product(spread, w_ffn_down), place.depths)
    (own_ffn_down,) = scatter.own(
        [("rows", spread, active_low)], [active_low.shape[1] // place.depths], [grad_pairs], True
    )
    partial = right_product(grad_pairs, w_gate_up)
    (own_gate_up,) = scatter.own(
        [("columns", second_low, grad_pairs)], [dm_rows], [partial], True
    )
    grad_second, grad_norm_two = norm_backward(core_sum(partial), second_memory, norm_gains[1])
    grad_hidden = grad_hidden + grad_second

    spread = to_low(grad_hidden)
    grad_attended = right_product(spread, w_attn_out)
    grad_qkv = attend(qkv, grad_attended, tables, group_seg, place.depths)
    own_attn_out, own_down = scatter.own(
        [("rows", spread, attended_low), ("columns", third_low, down_low)],
        [HEADS_PER_BLOCK * HEAD_SIZE, dm_rows // 2],
        [grad_qkv],
    )
    partial = right_product(grad_qkv, w_qkv)
    (own_qkv,) = scatter.own([("columns", first_low, grad_qkv)], [dm_rows], [partial])
    grad_first, grad_norm_one = norm_backward(core_sum(partial), first_memory, norm_gains[0])
    grad_hidden = grad_hidden + grad_first

    hidden_low = depth_to_chip(place, to_low(grad_hidden))
    d_rows = shared.shape[1] // place.chips
    partial = to_low(right_product(hidden_low, w_up))
    (own_up,) = scatter.own([("columns", own_rows, hidden_low)], [d_rows // 2], [partial])
    grad_rows = parity_join(place, partial, d_rows // 2)
    grad_shared = left_product(marked_low, grad_rows)
    (grad_dots,) = prob_back(grad_probs)
    grad_qk = pair_dots_back(qk, grad_dots, place.depths)
    partial = right_product(grad_qk, w_router)
    grad_shared = grad_shared + core_sum(partial)
    gradient = gradient + grad_shared

    gradient, enc_grads, enc_smalls, enc_maps = mamba_backward(
        place,
        gradient,
        enc_weights,
        mamba_params[0],
        items,
        enc_memory,
        scatter,
        [("columns", shared, grad_qk)],
        False,
    )
    grad_inputs = back_to_all(place, to_low(gradient), micro).astype(wide)

    parts = []
    for smalls in (enc_smalls, dec_smalls):
        parts += [
            reorder(smalls[0], place.chips, place.chip),
            all_channels(place, smalls[1]),
            smalls[2],
            all_channels(place, smalls[3]),
            all_channels(place, smalls[4]),
            all_channels(place, smalls[5]),
            all_channels(place, smalls[6]),
        ]
    parts.append(0.5 * reorder(grad_norm_one, place.chips, place.chip))
    parts.append(0.5 * reorder(grad_norm_two, place.chips, place.chip))
    flat = jnp.concatenate([part.reshape(-1) for part in parts])
    fill = -flat.shape[0] % 1024
    flat = jnp.pad(flat, (0, fill)).reshape(-1, 128)
    flat = sum_everywhere(place, flat).reshape(-1)
    summed = []
    offset = 0
    for part in parts:
        summed.append(flat[offset : offset + part.size].reshape(part.shape))
        offset += part.size
    smalls = [jnp.stack([summed[n], summed[7 + n]]) for n in range(7)]

    head_count = mamba_dt.shape[2] * place.depths // 2
    grad_bc, grad_dt = small_scatter(place, [enc_maps, dec_maps], LANES, head_count)

    def kinds(blocks, count):
        return join_columns(place, jnp.stack(jnp.split(blocks, count, 1)))

    enc_parts = kinds(enc_grads[0], 2)
    dec_parts = kinds(dec_grads[0], 2)
    qkv_width = qkv_shard.shape[1]
    return (
        outputs,
        grad_inputs,
        smalls[0],
        jnp.stack([enc_parts[0], dec_parts[0]]),
        jnp.stack([enc_parts[1], dec_parts[1]]),
        grad_bc,
        grad_dt,
        smalls[1],
        smalls[2],
        smalls[3],
        smalls[4],
        smalls[5],
        smalls[6],
        join_rows(place, jnp.stack([enc_grads[1], dec_grads[1]])),
        kinds(enc_grads[2], 2),
        own_up,
        own_down,
        jnp.stack([summed[14], summed[15]]),
        kinds(own_qkv[:, :qkv_width], 3),
        join_rows(place, own_attn_out),
        kinds(own_gate_up, 2),
        join_rows(place, own_ffn_down),
    )


def solution(mesh):
    in_specs = (
        P(None, "dp", "mp"),
        P(None, "dp", "mp"),
        P(None, "dp"),
        P(None, "dp"),
        P(),
        P(None, "dp", "mp"),
        P(None, "dp", "mp"),
        P(None, "dp", None),
        P(None, "dp", "mp"),
        P(),
        P(),
        P(),
        P(),
        P(),
        P(),
        P(None, "mp", "dp"),
        P(None, "dp", "mp"),
        P("dp", "mp"),
        P("dp", "mp"),
        P(),
        P(None, "dp", "mp"),
        P("mp", "dp"),
        P(None, "dp", "mp"),
        P("mp", "dp"),
    )
    out_specs = (
        P(None, "dp", "mp"),
        P(None, "dp", "mp"),
        P(),
        P(None, "dp", "mp"),
        P(None, "dp", "mp"),
        P(None, "dp", None),
        P(None, "dp", "mp"),
        P(),
        P(),
        P(),
        P(),
        P(),
        P(),
        P(None, "mp", "dp"),
        P(None, "dp", "mp"),
        P("dp", "mp"),
        P("dp", "mp"),
        P(),
        P(None, "dp", "mp"),
        P("mp", "dp"),
        P(None, "dp", "mp"),
        P("mp", "dp"),
    )
    return jax.shard_map(
        one_device, mesh=mesh, in_specs=in_specs, out_specs=out_specs, check_vma=False
    )
```

time: 4990 us -> 1650 us (0.33)
  waiting for transfers between devices: 2580 us -> 477 us
  matrix products: 781 us -> 136 us
  blocking collectives: 420 us -> 19.6 us
  other arithmetic: 575 us -> 228 us
  Pallas kernels: 0 us -> 334 us
  local copies, waits for them, and re-layouts: 517 us -> 258 us
  starting transfers between devices: 4.94 us -> 161 us
  loops' own time: 57.5 us -> 0 us
    reduce_scatter x40 -> x3, waiting for transfers between devices: 1750 us -> 0.01 us  [own(): lax.psum_scatter(going, 'mp', scatter_dimension=0).astype(jnp.float32)]
    dot_general x290 -> x0, matrix products: 487 us -> none  [the longest x60 225 us: scan_block(): outputs = jnp.einsum('ijh,jhp->ihp', weights, block_x, precision=HIGHEST)]
    all_gather x19 -> x6, waiting for transfers between devices: 505 us -> 42.7 us  [pieces(): stack = lax.all_gather(shard, 'mp', axis=0)]
    ppermute x0 -> x143, waiting for transfers between devices: none -> 434 us  [the longest x63 250 us: chip_swap(): return lax.ppermute(values, 'dp', [(d, d ^ bit * 2) for d in range(size)])]
    pallas_call x0 -> x47, Pallas kernels: none -> 334 us  [the longest x28 105 us: blocks(): pl.pallas_call(functools.partial(products_kernel, [kind for kind, _, _ in...]
    all_gather x13 -> x1, blocking collectives: 294 us -> 19.6 us  [pieces(): stack = lax.all_gather(shard, 'mp', axis=0)]
    unnamed x70 -> x9, waiting for transfers between devices: 166 us -> 0.15 us
    psum x3 -> x0, waiting for transfers between devices: 164 us -> none  [the longest x1 121 us: per_device(): lax.psum((small_total[0], conv_x_full, small_total[2], bias_full, decay_f...]
where the time goes in v1:
time: 1650 us; the launch traced here: 1630 us
  waiting for transfers between devices  477 us (29%)
  Pallas kernels  334 us (20%)
  local copies, waits for them, and re-layouts  258 us (16%)
  other arithmetic  228 us (14%)
  starting transfers between devices  161 us (10%)
  matrix products  136 us (8%)
  blocking collectives  19.6 us (1%)
  between operations  19 us (1%)
    ppermute x63, waiting for transfers between devices, chip_swap(): return lax.ppermute(values, 'dp', [(d, d ^ bit * 2) for d in range(size)])  250 us
    ppermute x31, waiting for transfers between devices, depth_swap(): return lax.ppermute(values, 'mp', [(d, d ^ offset) for d in range(size)])  179 us
    pallas_call x28, Pallas kernels, blocks(): pl.pallas_call(functools.partial(products_kernel, [kind for kind, _, _ in...  105 us
    unnamed x695, local copies, waits for them, and re-layouts  86.3 us
    pallas_call x2, Pallas kernels, mix_backward(): pl.pallas_call(functools.partial(mix_back_kernel, per_block), grid=(chunk...  84.3 us
    ppermute x49, starting transfers between devices, core_swap(): return lax.ppermute(values, 'dp', [(d, d ^ 1) for d in range(size)])  74.5 us
    dot_general x14, matrix products, matmul(): return jnp.dot(left, right, preferred_element_type=jnp.float32)  73.3 us
    dot_general x13, matrix products, right_product(): lax.dot_general(left, right, (((1,), (1,)), ((), ())), preferred_element_...  58.2 us
  transfers between devices with their start and end apart: 152, of which 41 were waited for; matrix products, arithmetic and copies ran while one was open for 32% of the time, Pallas kernels for 18%

profile of v1, /device:TPU:1, one launch (start us, length us, event | category | flops | bytes accessed | tf_op | source)
XLA Modules:
  0.0 1632.7 jit_solution(2173526790213993259)
XLA Ops:
  56.9 10.3 collective-permute-done.14
  68.6 19.3 %collective-permute-done.13 = bf16[640,256]{1,0:T(8,128)(2,1)} collective-permute-done((bf16[640,256]{1,0:T(8,128)(2,1)S(1)}, bf16[640,256]{1,0:T(8,128)(2,1)}, u32[]{:S(2)}, u32[]{:S(2)}) %collective-permute-start.13) | collective-permute-done | bytes 327712 | tf_op jit(solution)/shard_map/ppermute | solution.py:984
  114.4 19.4 %all-gather.16.cloned.1.call-done = bf16[1024,768]{0,1:T(8,128)(2,1)} async-done(((bf16[256,768]{0,1:T(8,128)(2,1)}), bf16[1024,768]{0,1:T(8,128)(2,1)}) %all-gather.16.cloned.1.call-update) | async-done | bytes 1572880 | tf_op jit(solution)/shard_map/all_gather | solution.py:1160
  150.2 34.7 %collective-permute-done.18.refs_3_ = bf16[2,256,512]{2,1,0:T(8,128)(2,1)} collective-permute-done((bf16[2,256,512]{2,1,0:T(8,128)(2,1)}, bf16[2,256,512]{2,1,0:T(8,128)(2,1)}, u32[]{:S(2)}, u32[]{:S(2)}) %collective-permute-start.18) | collective-permute-done | bytes 524320 | tf_op jit(solution)/shard_map/ppermute | solution.py:977
  194.8 10.4 fusion.295.zx_ref.zx_tail_ref
  205.2 20.1 %shard_map.400 = (bf16[1280,1024]{1,0:T(8,128)(2,1)S(1)}, f32[1280,1024]{1,0:T(8,128)}, f32[1280,1]{1,0:T(8,128)S(1)}, bf16[1280,1024]{1,0:T(8,128)(2,1)}) custom-call(f32[1280,2048]{1,0:T(8,128)} %fusion.295.zx_ref.zx_tail_ref, f32[1280,384]{1,0:T(8,128)S(1)} %fusion.249.bcdt_ref.maps_tail_ref, f32[1280,8]{1,0:T(8,128)S(1)} %stack.195.columns_ref, ...), custom_call_target="tpu_custom_call" | custom-call | flops 1342177280 | bytes 20971520 | tf_op jit(solution)/shard_map/pallas_call | solution.py:401
  226.1 5.5 shard_map.401
  231.8 7.3 fusion.284
  260.7 19.6 %all-gather.3 = bf16[768,640]{1,0:T(8,128)(2,1)} all-gather(bf16[192,640]{1,0:T(8,128)(2,1)S(1)} %copy-done.203), channel_id=5, replica_groups=mesh['dp'=8,'mp'=4] {'mp'}, dimensions={0}, use_global_device_ids=true | all-gather | bytes 1228800 | tf_op jit(solution)/shard_map/all_gather | solution.py:1160
  280.4 7.2 collective-permute-done.31.refs_1_
  289.0 6.4 fusion.258
  341.4 21.4 %collective-permute-done.38.refs_3_ = bf16[2,192,640]{2,1,0:T(8,128)(2,1)S(1)} collective-permute-done((bf16[2,192,640]{2,1,0:T(8,128)(2,1)}, bf16[2,192,640]{2,1,0:T(8,128)(2,1)S(1)}, u32[]{:S(2)}, u32[]{:S(2)}) %collective-permute-start.38) | collective-permute-done | bytes 491552 | tf_op jit(solution)/shard_map/ppermute | solution.py:977
  370.1 5.8 shard_map.403
  389.4 23.2 %all-gather.22.cloned.1.call-done = bf16[2048,384]{0,1:T(8,128)(2,1)} async-done(((bf16[512,384]{0,1:T(8,128)(2,1)}), bf16[2048,384]{0,1:T(8,128)(2,1)}) %all-gather.22.cloned.1.call-update) | async-done | bytes 1572880 | tf_op jit(solution)/shard_map/all_gather | solution.py:1160
  418.1 9.0 shard_map.404.refs_1_
  432.4 12.7 collective-permute-done.42.refs_1_
  460.8 18.0 %collective-permute-done.47.refs_1_ = bf16[4,512,384]{2,1,0:T(8,128)(2,1)} collective-permute-done((bf16[4,512,384]{2,1,0:T(8,128)(2,1)S(1)}, bf16[4,512,384]{2,1,0:T(8,128)(2,1)}, u32[]{:S(2)}, u32[]{:S(2)}) %collective-permute-start.47) | collective-permute-done | bytes 1572896 | tf_op jit(solution)/shard_map/ppermute | solution.py:977
  488.6 24.3 %collective-permute-done.44.refs_3_ = bf16[2,384,1024]{2,1,0:T(8,128)(2,1)} collective-permute-done((bf16[2,384,1024]{2,1,0:T(8,128)(2,1)}, bf16[2,384,1024]{2,1,0:T(8,128)(2,1)}, u32[]{:S(2)}, u32[]{:S(2)}) %collective-permute-start.44) | collective-permute-done | bytes 1572896 | tf_op jit(solution)/shard_map/ppermute | solution.py:977
  512.9 9.7 shard_map.406
  522.6 7.2 collective-permute-done.49.refs_3_
  529.8 5.6 shard_map.408
  535.3 10.5 fusion.298.pair_ref
  593.5 12.9 shard_map.409
  606.4 9.0 collective-permute-done.66
  626.2 11.7 collective-permute-done.56.refs_3_
  644.2 10.2 fusion.299.zx_ref.zx_tail_ref
  654.4 20.3 %shard_map.411 = (bf16[1280,1024]{1,0:T(8,128)(2,1)S(1)}, f32[1280,1024]{1,0:T(8,128)}, f32[1280,1]{1,0:T(8,128)S(1)}, bf16[1280,1024]{1,0:T(8,128)(2,1)}) custom-call(f32[1280,2048]{1,0:T(8,128)} %fusion.299.zx_ref.zx_tail_ref, f32[1280,384]{1,0:T(8,128)S(1)} %fusion.247.bcdt_ref.maps_tail_ref, f32[1280,8]{1,0:T(8,128)S(1)} %stack.195.columns_ref, ...), custom_call_target="tpu_custom_call" | custom-call | flops 1342177280 | bytes 20971520 | tf_op jit(solution)/shard_map/pallas_call | solution.py:401
  684.6 8.4 fusion.290
  714.7 42.0 %shard_map.412 = (bf16[1280,2048]{1,0:T(8,128)(2,1)}, f32[1280,256]{1,0:T(8,128)}, f32[1280,128]{1,0:T(8,128)S(1)}, f32[32,1024]{1,0:T(8,128)S(1)}, f32[32,256]{...) custom-call(f32[1280,1024]{1,0:T(8,128)} %get-tuple-element.667.grad_ref, ...), custom_call_target="tpu_custom_call" | custom-call | flops 4026531840 | bytes 20971520 | tf_op jit(solution)/shard_map/pallas_call | solution.py:461
  765.6 8.0 fusion.289
  788.2 5.4 fusion.7
  793.7 9.6 fusion.8
  803.3 5.9 shard_map.420
  810.4 6.0 shard_map.421
  823.1 12.4 shard_map.413
  849.6 7.8 shard_map.416.refs_5_
  864.1 6.2 shard_map.418
  882.8 9.1 fusion.291
  892.3 5.9 shard_map.419
  941.3 12.2 shard_map.415.refs_1_
  953.5 8.2 fusion.292
  998.8 7.3 collective-permute-done.99
  1034.7 7.2 multiply_convert_fusion
  1057.8 42.3 %shard_map.417 = (bf16[1280,2048]{1,0:T(8,128)(2,1)}, f32[1280,256]{1,0:T(8,128)S(1)}, f32[1280,128]{1,0:T(8,128)S(1)}, f32[32,1024]{1,0:T(8,128)S(1)}, f32[32,2...) custom-call(f32[1280,1024]{1,0:T(8,128)} %get-tuple-element.679.grad_ref, ...), custom_call_target="tpu_custom_call" | custom-call | flops 4026531840 | bytes 20971520 | tf_op jit(solution)/shard_map/pallas_call | solution.py:461
  1114.2 8.5 collective-permute-done.104
  1134.9 24.1 %collective-permute-done.132 = bf16[192,640]{1,0:T(8,128)(2,1)S(1)} collective-permute-done((bf16[192,640]{1,0:T(8,128)(2,1)S(1)}, bf16[192,640]{1,0:T(8,128)(2,1)S(1)}, u32[]{:S(2)}, u32[]{:S(2)}) %collective-permute-start.132) | collective-permute-done | bytes 245792 | tf_op jit(solution)/shard_map/ppermute | solution.py:984
  1161.0 10.7 collective-permute-start.140
  1177.7 8.2 fusion.294
  1189.3 14.3 collective-permute-done.115
  1237.3 12.4 collective-permute-start.119
  1294.2 6.3 collective-permute-done.98
  1303.6 7.7 shard_map.438
  1316.9 7.2 shard_map.439
  1329.4 7.2 shard_map.440
  1342.1 7.3 shard_map.441
  1360.1 5.5 fusion.5
  1366.0 9.2 collective-permute-start.84
  1375.2 6.2 fusion.16
  1391.0 30.6 %collective-permute-done.129 = bf16[128,384]{1,0:T(8,128)(2,1)S(1)} collective-permute-done((bf16[128,384]{1,0:T(8,128)(2,1)S(1)}, bf16[128,384]{1,0:T(8,128)(2,1)S(1)}, u32[]{:S(2)}, u32[]{:S(2)}) %collective-permute-start.129) | collective-permute-done | bytes 98336 | tf_op jit(solution)/shard_map/ppermute | solution.py:984
  1425.8 67.4 %collective-permute-done.86 = f32[224,128]{1,0:T(8,128)S(1)} collective-permute-done((f32[224,128]{1,0:T(8,128)S(1)}, f32[224,128]{1,0:T(8,128)S(1)}, u32[]{:S(2)}, u32[]{:S(2)}) %collective-permute-start.86) | collective-permute-done | bytes 114720 | tf_op jit(solution)/shard_map/ppermute | solution.py:977
  1524.7 6.4 collective-permute-done.138
  1531.1 28.6 %collective-permute-done.137 = bf16[384,640]{1,0:T(8,128)(2,1)S(1)} collective-permute-done((bf16[384,640]{1,0:T(8,128)(2,1)S(1)}, bf16[384,640]{1,0:T(8,128)(2,1)S(1)}, u32[]{:S(2)}, u32[]{:S(2)}) %collective-permute-start.137) | collective-permute-done | bytes 491552 | tf_op jit(solution)/shard_map/ppermute | solution.py:984
  1568.7 8.9 collective-permute-done.111
  1577.6 30.2 %collective-permute-done.110 = bf16[256,1024]{0,1:T(8,128)(2,1)S(1)} collective-permute-done((bf16[256,1024]{0,1:T(8,128)(2,1)S(1)}, bf16[256,1024]{0,1:T(8,128)(2,1)S(1)}, u32[]{:S(2)}, u32[]{:S(2)}) %collective-permute-start.110) | collective-permute-done | bytes 524320 | tf_op jit(solution)/shard_map/ppermute | solution.py:984
  (1519 shorter events, 730.8 us)
Async XLA Ops:
  7.2 91.5 %all-gather.14.cloned.1.call-start = ((), (), s32[]{:S(2)}) async-start(), calls=%async_computation.6 | async-start | bytes 1310720 | tf_op jit(solution)/shard_map/all_gather | solution.py:1160
  29.2 104.6 %all-gather.16.cloned.1.call-start = ((), (), s32[]{:S(2)}) async-start(), calls=%async_computation.7 | async-start | bytes 1966080 | tf_op jit(solution)/shard_map/all_gather | solution.py:1160
  45.7 43.8 %collective-permute-start.7 = (bf16[2,256,384]{1,2,0:T(8,128)(2,1)S(1)}, bf16[2,256,384]{1,2,0:T(8,128)(2,1)}, u32[]{:S(2)}, u32[]{:S(2)}) collective-permute-start(bf16[2,256,384]{1,2,0:T(8,128)(2,1)S(1)} %concatenate.403), channel_id=1, source_target_pairs={{0,16},{4,20},{8,24},{12,28},{16,0},{20,4},{24,8},{28,12},{1,17},{... | collective-permute-start | bytes 1179656 | tf_op jit(solution)/shard_map/ppermute | solution.py:977
  67.2 181.7 %collective-permute-start.35 = (bf16[192,192]{1,0:T(8,128)(2,1)}, bf16[192,192]{1,0:T(8,128)(2,1)}, u32[]{:S(2)}, u32[]{:S(2)}) collective-permute-start(bf16[192,192]{1,0:T(8,128)(2,1)} %copy.661), channel_id=1, source_target_pairs={{0,4},{4,0},{8,12},{12,8},{16,20},{20,16},{24,28},{28,24},{1,5},{5... | collective-permute-start | bytes 221192 | tf_op jit(solution)/shard_map/ppermute | solution.py:972
  94.0 44.4 %collective-permute-start.15 = (bf16[640,1024]{1,0:T(8,128)(2,1)}, bf16[640,1024]{1,0:T(8,128)(2,1)}, u32[]{:S(2)}, u32[]{:S(2)}) collective-permute-start(bf16[640,1024]{1,0:T(8,128)(2,1)} %pad_maximum_fusion.10), channel_id=1, source_target_pairs={{0,4},{4,0},{8,12},{12,8},{16,20},{20,16},{24,28},{28,24},{1,5},{5... | collective-permute-start | bytes 3932168 | tf_op jit(solution)/shard_map/ppermute | solution.py:972
  98.7 144.1 %all-gather.18.cloned.1.call-start = ((), (), s32[]{:S(2)}) async-start(), calls=%async_computation.8 | async-start | bytes 2457600 | tf_op jit(solution)/shard_map/all_gather | solution.py:1160
  135.5 55.3 %collective-permute-start.22 = (bf16[4,256,768]{2,1,0:T(8,128)(2,1)S(1)}, bf16[4,256,768]{2,1,0:T(8,128)(2,1)}, u32[]{:S(2)}, u32[]{:S(2)}) collective-permute-start(bf16[4,256,768]{2,1,0:T(8,128)(2,1)S(1)} %bitcast.550), channel_id=1, source_target_pairs={{0,8},{4,12},{8,0},{12,4},{16,24},{20,28},{24,16},{28,20},{1,9},{5... | collective-permute-start | bytes 4718600 | tf_op jit(solution)/shard_map/ppermute | solution.py:977
  138.4 54.9 %collective-permute-start.23 = (bf16[4,256,768]{2,1,0:T(8,128)(2,1)S(1)}, bf16[4,256,768]{2,1,0:T(8,128)(2,1)}, u32[]{:S(2)}, u32[]{:S(2)}) collective-permute-start(bf16[4,256,768]{2,1,0:T(8,128)(2,1)S(1)} %bitcast.551), channel_id=1, source_target_pairs={{0,16},{4,20},{8,24},{12,28},{16,0},{20,4},{24,8},{28,12},{1,17},{... | collective-permute-start | bytes 4718600 | tf_op jit(solution)/shard_map/ppermute | solution.py:977
  145.9 230.1 %all-gather.20.cloned.1.call-start = ((), (), s32[]{:S(2)}) async-start(), calls=%async_computation.9 | async-start | bytes 3932160 | tf_op jit(solution)/shard_map/all_gather | solution.py:1160
  184.9 67.2 %collective-permute-start.41 = (bf16[192,1024]{1,0:T(8,128)(2,1)}, bf16[192,1024]{1,0:T(8,128)(2,1)}, u32[]{:S(2)}, u32[]{:S(2)}) collective-permute-start(bf16[192,1024]{1,0:T(8,128)(2,1)} %pad_maximum_fusion.34), channel_id=1, source_target_pairs={{0,4},{4,0},{8,12},{12,8},{16,20},{20,16},{24,28},{28,24},{1,5},{5... | collective-permute-start | bytes 1179656 | tf_op jit(solution)/shard_map/ppermute | solution.py:972
  239.1 49.9 %collective-permute-start.26 = (bf16[1280,1024]{1,0:T(8,128)(2,1)}, bf16[1280,1024]{1,0:T(8,128)(2,1)}, u32[]{:S(2)}, u32[]{:S(2)}) collective-permute-start(bf16[1280,1024]{1,0:T(8,128)(2,1)} %get-tuple-element.656), channel_id=1, source_target_pairs={{0,4},{4,0},{8,12},{12,8},{16,20},{20,16},{24,28},{28,24},{1,5},{5... | collective-permute-start | bytes 7864328 | tf_op jit(solution)/shard_map/ppermute | solution.py:972
  242.8 44.8 %collective-permute-start.31 = (bf16[4,384,640]{2,1,0:T(8,128)(2,1)}, bf16[4,384,640]{2,1,0:T(8,128)(2,1)S(1)}, u32[]{:S(2)}, u32[]{:S(2)}) collective-permute-start(bf16[4,384,640]{2,1,0:T(8,128)(2,1)} %bitcast.562), channel_id=1, source_target_pairs={{0,8},{4,12},{8,0},{12,4},{16,24},{20,28},{24,16},{28,20},{1,9},{5... | collective-permute-start | bytes 5898248 | tf_op jit(solution)/shard_map/ppermute | solution.py:977
  244.0 44.4 %collective-permute-start.32 = (bf16[4,384,640]{2,1,0:T(8,128)(2,1)}, bf16[4,384,640]{2,1,0:T(8,128)(2,1)}, u32[]{:S(2)}, u32[]{:S(2)}) collective-permute-start(bf16[4,384,640]{2,1,0:T(8,128)(2,1)} %bitcast.563), channel_id=1, source_target_pairs={{0,16},{4,20},{8,24},{12,28},{16,0},{20,4},{24,8},{28,12},{1,17},{... | collective-permute-start | bytes 5898248 | tf_op jit(solution)/shard_map/ppermute | solution.py:977
  248.9 89.3 %collective-permute-start.46 = (bf16[512,192]{0,1:T(8,128)(2,1)}, bf16[512,192]{0,1:T(8,128)(2,1)}, u32[]{:S(2)}, u32[]{:S(2)}) collective-permute-start(bf16[512,192]{0,1:T(8,128)(2,1)} %constant_dynamic-slice_fusion.58), channel_id=1, source_target_pairs={{0,4},{4,0},{8,12},{12,8},{16,20},{20,16},{24,28},{28,24},{1,5},{5... | collective-permute-start | bytes 589832 | tf_op jit(solution)/shard_map/ppermute | solution.py:972
  288.5 124.1 %all-gather.22.cloned.1.call-start = ((), (), s32[]{:S(2)}) async-start(), calls=%async_computation.10 | async-start | bytes 1966080 | tf_op jit(solution)/shard_map/all_gather | solution.py:1160
  308.6 61.5 %collective-permute-start.33 = (bf16[2,384,640]{2,1,0:T(8,128)(2,1)}, bf16[2,384,640]{2,1,0:T(8,128)(2,1)}, u32[]{:S(2)}, u32[]{:S(2)}) collective-permute-start(bf16[2,384,640]{2,1,0:T(8,128)(2,1)} %slice.871), channel_id=1, source_target_pairs={{0,16},{4,20},{8,24},{12,28},{16,0},{20,4},{24,8},{28,12},{1,17},{... | collective-permute-start | bytes 2949128 | tf_op jit(solution)/shard_map/ppermute | solution.py:977
  312.4 57.7 %collective-permute-start.34 = (bf16[2,384,640]{2,1,0:T(8,128)(2,1)}, bf16[2,384,640]{2,1,0:T(8,128)(2,1)}, u32[]{:S(2)}, u32[]{:S(2)}) collective-permute-start(bf16[2,384,640]{2,1,0:T(8,128)(2,1)} %slice.872), channel_id=1, source_target_pairs={{0,8},{4,12},{8,0},{12,4},{16,24},{20,28},{24,16},{28,20},{1,9},{5... | collective-permute-start | bytes 2949128 | tf_op jit(solution)/shard_map/ppermute | solution.py:977
  332.7 44.7 %collective-permute-start.29 = (bf16[320,1536]{1,0:T(8,128)(2,1)}, bf16[320,1536]{1,0:T(8,128)(2,1)}, u32[]{:S(2)}, u32[]{:S(2)}) collective-permute-start(bf16[320,1536]{1,0:T(8,128)(2,1)} %get-tuple-element.658), channel_id=1, source_target_pairs={{0,4},{4,0},{8,12},{12,8},{16,20},{20,16},{24,28},{28,24},{1,5},{5... | collective-permute-start | bytes 2949128 | tf_op jit(solution)/shard_map/ppermute | solution.py:972
  375.9 69.2 %collective-permute-start.42 = (bf16[4,384,1024]{2,1,0:T(8,128)(2,1)}, bf16[4,384,1024]{2,1,0:T(8,128)(2,1)}, u32[]{:S(2)}, u32[]{:S(2)}) collective-permute-start(bf16[4,384,1024]{2,1,0:T(8,128)(2,1)} %bitcast.595), channel_id=1, source_target_pairs={{0,8},{4,12},{8,0},{12,4},{16,24},{20,28},{24,16},{28,20},{1,9},{5... | collective-permute-start | bytes 9437192 | tf_op jit(solution)/shard_map/ppermute | solution.py:977
  377.0 74.7 %collective-permute-start.43 = (bf16[4,384,1024]{2,1,0:T(8,128)(2,1)}, bf16[4,384,1024]{2,1,0:T(8,128)(2,1)}, u32[]{:S(2)}, u32[]{:S(2)}) collective-permute-start(bf16[4,384,1024]{2,1,0:T(8,128)(2,1)} %bitcast.596), channel_id=1, source_target_pairs={{0,16},{4,20},{8,24},{12,28},{16,0},{20,4},{24,8},{28,12},{1,17},{... | collective-permute-start | bytes 9437192 | tf_op jit(solution)/shard_map/ppermute | solution.py:977
  377.3 193.6 %all-gather.24.cloned.1.call-start = ((), (), s32[]{:S(2)}) async-start(), calls=%async_computation.11 | async-start | bytes 1966080 | tf_op jit(solution)/shard_map/all_gather | solution.py:1160
  414.5 64.3 %collective-permute-start.47 = (bf16[4,512,384]{2,1,0:T(8,128)(2,1)S(1)}, bf16[4,512,384]{2,1,0:T(8,128)(2,1)}, u32[]{:S(2)}, u32[]{:S(2)}) collective-permute-start(bf16[4,512,384]{2,1,0:T(8,128)(2,1)S(1)} %bitcast.543), channel_id=1, source_target_pairs={{0,8},{4,12},{8,0},{12,4},{16,24},{20,28},{24,16},{28,20},{1,9},{5... | collective-permute-start | bytes 4718600 | tf_op jit(solution)/shard_map/ppermute | solution.py:977
  415.7 65.4 %collective-permute-start.48 = (bf16[4,512,384]{2,1,0:T(8,128)(2,1)S(1)}, bf16[4,512,384]{2,1,0:T(8,128)(2,1)}, u32[]{:S(2)}, u32[]{:S(2)}) collective-permute-start(bf16[4,512,384]{2,1,0:T(8,128)(2,1)S(1)} %bitcast.544), channel_id=1, source_target_pairs={{0,16},{4,20},{8,24},{12,28},{16,0},{20,4},{24,8},{28,12},{1,17},{... | collective-permute-start | bytes 4718600 | tf_op jit(solution)/shard_map/ppermute | solution.py:977
  430.0 54.4 %collective-permute-start.40 = (bf16[320,1536]{1,0:T(8,128)(2,1)}, bf16[320,1536]{1,0:T(8,128)(2,1)}, u32[]{:S(2)}, u32[]{:S(2)}) collective-permute-start(bf16[320,1536]{1,0:T(8,128)(2,1)} %get-tuple-element.660), channel_id=1, source_target_pairs={{0,4},{4,0},{8,12},{12,8},{16,20},{20,16},{24,28},{28,24},{1,5},{5... | collective-permute-start | bytes 2949128 | tf_op jit(solution)/shard_map/ppermute | solution.py:972
  451.7 61.2 %collective-permute-start.44 = (bf16[2,384,1024]{2,1,0:T(8,128)(2,1)}, bf16[2,384,1024]{2,1,0:T(8,128)(2,1)}, u32[]{:S(2)}, u32[]{:S(2)}) collective-permute-start(bf16[2,384,1024]{2,1,0:T(8,128)(2,1)} %slice.876), channel_id=1, source_target_pairs={{0,16},{4,20},{8,24},{12,28},{16,0},{20,4},{24,8},{28,12},{1,17},{... | collective-permute-start | bytes 4718600 | tf_op jit(solution)/shard_map/ppermute | solution.py:977
  454.4 58.5 %collective-permute-start.45 = (bf16[2,384,1024]{2,1,0:T(8,128)(2,1)}, bf16[2,384,1024]{2,1,0:T(8,128)(2,1)}, u32[]{:S(2)}, u32[]{:S(2)}) collective-permute-start(bf16[2,384,1024]{2,1,0:T(8,128)(2,1)} %slice.877), channel_id=1, source_target_pairs={{0,8},{4,12},{8,0},{12,4},{16,24},{20,28},{24,16},{28,20},{1,9},{5... | collective-permute-start | bytes 4718600 | tf_op jit(solution)/shard_map/ppermute | solution.py:977
  480.9 48.9 %collective-permute-start.49 = (bf16[2,512,384]{2,1,0:T(8,128)(2,1)}, bf16[2,512,384]{2,1,0:T(8,128)(2,1)}, u32[]{:S(2)}, u32[]{:S(2)}) collective-permute-start(bf16[2,512,384]{2,1,0:T(8,128)(2,1)} %slice.878), channel_id=1, source_target_pairs={{0,16},{4,20},{8,24},{12,28},{16,0},{20,4},{24,8},{28,12},{1,17},{... | collective-permute-start | bytes 2359304 | tf_op jit(solution)/shard_map/ppermute | solution.py:977
  483.2 46.6 %collective-permute-start.50 = (bf16[2,512,384]{2,1,0:T(8,128)(2,1)}, bf16[2,512,384]{2,1,0:T(8,128)(2,1)}, u32[]{:S(2)}, u32[]{:S(2)}) collective-permute-start(bf16[2,512,384]{2,1,0:T(8,128)(2,1)} %slice.879), channel_id=1, source_target_pairs={{0,8},{4,12},{8,0},{12,4},{16,24},{20,28},{24,16},{28,20},{1,9},{5... | collective-permute-start | bytes 2359304 | tf_op jit(solution)/shard_map/ppermute | solution.py:977
  488.6 763.0 %reduce-scatter.4.cloned.1.call-start = ((), (), s32[]{:S(2)}) async-start(), calls=%async_computation.3 | async-start | bytes 1966080 | tf_op jit(solution)/shard_map/reduce_scatter | solution.py:1326
  694.8 98.9 %collective-permute-start.58 = (bf16[1280,1024]{1,0:T(8,128)(2,1)}, bf16[1280,1024]{1,0:T(8,128)(2,1)}, u32[]{:S(2)}, u32[]{:S(2)}) collective-permute-start(bf16[1280,1024]{1,0:T(8,128)(2,1)} %get-tuple-element.670), channel_id=1, source_target_pairs={{0,4},{4,0},{8,12},{12,8},{16,20},{20,16},{24,28},{28,24},{1,5},{5... | collective-permute-start | bytes 7864328 | tf_op jit(solution)/shard_map/ppermute | solution.py:972
  819.6 50.8 %collective-permute-start.62 = (bf16[640,256]{1,0:T(8,128)(2,1)}, bf16[640,256]{1,0:T(8,128)(2,1)}, u32[]{:S(2)}, u32[]{:S(2)}) collective-permute-start(bf16[640,256]{1,0:T(8,128)(2,1)} %get-tuple-element.359), channel_id=1, source_target_pairs={{0,3},{1,2},{2,1},{3,0},{4,7},{5,6},{6,5},{7,4},{8,11},{9,10},{10,... | collective-permute-start | bytes 983048 | tf_op jit(solution)/shard_map/ppermute | solution.py:984
  821.6 48.8 %collective-permute-start.61 = (bf16[640,256]{1,0:T(8,128)(2,1)}, bf16[640,256]{1,0:T(8,128)(2,1)}, u32[]{:S(2)}, u32[]{:S(2)}) collective-permute-start(bf16[640,256]{1,0:T(8,128)(2,1)} %get-tuple-element.360), channel_id=1, source_target_pairs={{0,2},{1,3},{2,0},{3,1},{4,6},{5,7},{6,4},{7,5},{8,10},{9,11},{10,... | collective-permute-start | bytes 983048 | tf_op jit(solution)/shard_map/ppermute | solution.py:984
  821.6 48.8 %collective-permute-start.60 = (bf16[640,256]{1,0:T(8,128)(2,1)}, bf16[640,256]{1,0:T(8,128)(2,1)}, u32[]{:S(2)}, u32[]{:S(2)}) collective-permute-start(bf16[640,256]{1,0:T(8,128)(2,1)} %get-tuple-element.361), channel_id=1, source_target_pairs={{0,1},{1,0},{2,3},{3,2},{4,5},{5,4},{6,7},{7,6},{8,9},{9,8},{10,11... | collective-permute-start | bytes 983048 | tf_op jit(solution)/shard_map/ppermute | solution.py:984
  873.5 57.6 %collective-permute-start.63 = (bf16[2,640,256]{2,1,0:T(8,128)(2,1)}, bf16[2,640,256]{2,1,0:T(8,128)(2,1)}, u32[]{:S(2)}, u32[]{:S(2)}) collective-permute-start(bf16[2,640,256]{2,1,0:T(8,128)(2,1)} %dynamic-slice_bitcast_fusion.1), channel_id=1, source_target_pairs={{0,4},{4,0},{8,12},{12,8},{16,20},{20,16},{24,28},{28,24},{1,5},{5... | collective-permute-start | bytes 1966088 | tf_op jit(solution)/shard_map/ppermute | solution.py:972
  891.9 42.5 %collective-permute-start.73 = (bf16[320,1536]{1,0:T(8,128)(2,1)}, bf16[320,1536]{1,0:T(8,128)(2,1)}, u32[]{:S(2)}, u32[]{:S(2)}) collective-permute-start(bf16[320,1536]{1,0:T(8,128)(2,1)} %get-tuple-element.672), channel_id=1, source_target_pairs={{0,4},{4,0},{8,12},{12,8},{16,20},{20,16},{24,28},{28,24},{1,5},{5... | collective-permute-start | bytes 2949128 | tf_op jit(solution)/shard_map/ppermute | solution.py:972
  899.4 135.3 %collective-permute-start.76 = (bf16[1280,1024]{1,0:T(8,128)(2,1)}, bf16[1280,1024]{1,0:T(8,128)(2,1)}, u32[]{:S(2)}, u32[]{:S(2)}) collective-permute-start(bf16[1280,1024]{1,0:T(8,128)(2,1)} %get-tuple-element.676), channel_id=1, source_target_pairs={{0,4},{4,0},{8,12},{12,8},{16,20},{20,16},{24,28},{28,24},{1,5},{5... | collective-permute-start | bytes 7864328 | tf_op jit(solution)/shard_map/ppermute | solution.py:972
  905.1 57.3 %collective-permute-start.90 = (bf16[2,2,256,768]{2,3,1,0:T(8,128)(2,1)}, bf16[2,2,256,768]{2,3,1,0:T(8,128)(2,1)}, u32[]{:S(2)}, u32[]{:S(2)}) collective-permute-start(bf16[2,2,256,768]{2,3,1,0:T(8,128)(2,1)} %copy.633), channel_id=1, source_target_pairs={{0,8},{4,12},{8,0},{12,4},{16,24},{20,28},{24,16},{28,20},{1,9},{5... | collective-permute-start | bytes 4718600 | tf_op jit(solution)/shard_map/ppermute | solution.py:977
  911.8 54.0 %collective-permute-start.89 = (bf16[2,2,256,768]{2,3,1,0:T(8,128)(2,1)}, bf16[2,2,256,768]{2,3,1,0:T(8,128)(2,1)}, u32[]{:S(2)}, u32[]{:S(2)}) collective-permute-start(bf16[2,2,256,768]{2,3,1,0:T(8,128)(2,1)} %copy.631), channel_id=1, source_target_pairs={{0,16},{4,20},{8,24},{12,28},{16,0},{20,4},{24,8},{28,12},{1,17},{... | collective-permute-start | bytes 4718600 | tf_op jit(solution)/shard_map/ppermute | solution.py:977
  931.1 56.0 %collective-permute-start.95 = (bf16[2,2,512,384]{3,2,1,0:T(8,128)(2,1)S(1)}, bf16[2,2,512,384]{3,2,1,0:T(8,128)(2,1)}, u32[]{:S(2)}, u32[]{:S(2)}) collective-permute-start(bf16[2,2,512,384]{3,2,1,0:T(8,128)(2,1)S(1)} %bitcast.567), channel_id=1, source_target_pairs={{0,8},{4,12},{8,0},{12,4},{16,24},{20,28},{24,16},{28,20},{1,9},{5... | collective-permute-start | bytes 4718600 | tf_op jit(solution)/shard_map/ppermute | solution.py:977
  934.5 55.1 %collective-permute-start.93 = (bf16[2,2,512,384]{3,2,1,0:T(8,128)(2,1)S(1)}, bf16[2,2,512,384]{3,2,1,0:T(8,128)(2,1)}, u32[]{:S(2)}, u32[]{:S(2)}) collective-permute-start(bf16[2,2,512,384]{3,2,1,0:T(8,128)(2,1)S(1)} %bitcast.566), channel_id=1, source_target_pairs={{0,16},{4,20},{8,24},{12,28},{16,0},{20,4},{24,8},{28,12},{1,17},{... | collective-permute-start | bytes 4718600 | tf_op jit(solution)/shard_map/ppermute | solution.py:977
  962.4 59.9 %collective-permute-start.74 = (bf16[320,1536]{1,0:T(8,128)(2,1)}, bf16[320,1536]{1,0:T(8,128)(2,1)}, u32[]{:S(2)}, u32[]{:S(2)}) collective-permute-start(bf16[320,1536]{1,0:T(8,128)(2,1)} %get-tuple-element.674), channel_id=1, source_target_pairs={{0,4},{4,0},{8,12},{12,8},{16,20},{20,16},{24,28},{28,24},{1,5},{5... | collective-permute-start | bytes 2949128 | tf_op jit(solution)/shard_map/ppermute | solution.py:972
  989.6 215.4 %collective-permute-start.91 = (bf16[2,2,384,1024]{3,2,1,0:T(8,128)(2,1)}, bf16[2,2,384,1024]{3,2,1,0:T(8,128)(2,1)}, u32[]{:S(2)}, u32[]{:S(2)}) collective-permute-start(bf16[2,2,384,1024]{3,2,1,0:T(8,128)(2,1)} %bitcast.145), channel_id=1, source_target_pairs={{0,16},{4,20},{8,24},{12,28},{16,0},{20,4},{24,8},{28,12},{1,17},{... | collective-permute-start | bytes 9437192 | tf_op jit(solution)/shard_map/ppermute | solution.py:977
  997.8 114.3 %collective-permute-start.96 = (bf16[1,2,512,384]{3,2,1,0:T(8,128)(2,1)}, bf16[1,2,512,384]{3,2,1,0:T(8,128)(2,1)}, u32[]{:S(2)}, u32[]{:S(2)}) collective-permute-start(bf16[1,2,512,384]{3,2,1,0:T(8,128)(2,1)} %slice.1176), channel_id=1, source_target_pairs={{0,16},{4,20},{8,24},{12,28},{16,0},{20,4},{24,8},{28,12},{1,17},{... | collective-permute-start | bytes 2359304 | tf_op jit(solution)/shard_map/ppermute | solution.py:977
  1006.1 121.5 %collective-permute-start.94 = (bf16[1,2,512,384]{3,2,1,0:T(8,128)(2,1)}, bf16[1,2,512,384]{3,2,1,0:T(8,128)(2,1)}, u32[]{:S(2)}, u32[]{:S(2)}) collective-permute-start(bf16[1,2,512,384]{3,2,1,0:T(8,128)(2,1)} %slice.1177), channel_id=1, source_target_pairs={{0,8},{4,12},{8,0},{12,4},{16,24},{20,28},{24,16},{28,20},{1,9},{5... | collective-permute-start | bytes 2359304 | tf_op jit(solution)/shard_map/ppermute | solution.py:977
  1008.5 250.9 %reduce-scatter.8.cloned.1.call-start = ((), (), s32[]{:S(2)}) async-start(), calls=%async_computation.5 | async-start | bytes 1966080 | tf_op jit(solution)/shard_map/reduce_scatter | solution.py:1326
  1030.9 76.8 %collective-permute-start.103 = (bf16[2,2,192,640]{3,2,1,0:T(8,128)(2,1)}, bf16[2,2,192,640]{3,2,1,0:T(8,128)(2,1)}, u32[]{:S(2)}, u32[]{:S(2)}) collective-permute-start(bf16[2,2,192,640]{3,2,1,0:T(8,128)(2,1)} %bitcast.164), channel_id=1, source_target_pairs={{0,8},{4,12},{8,0},{12,4},{16,24},{20,28},{24,16},{28,20},{1,9},{5... | collective-permute-start | bytes 2949128 | tf_op jit(solution)/shard_map/ppermute | solution.py:977
  1048.4 61.5 %collective-permute-start.101 = (bf16[2,2,192,640]{3,2,1,0:T(8,128)(2,1)}, bf16[2,2,192,640]{3,2,1,0:T(8,128)(2,1)}, u32[]{:S(2)}, u32[]{:S(2)}) collective-permute-start(bf16[2,2,192,640]{3,2,1,0:T(8,128)(2,1)} %bitcast.161), channel_id=1, source_target_pairs={{0,16},{4,20},{8,24},{12,28},{16,0},{20,4},{24,8},{28,12},{1,17},{... | collective-permute-start | bytes 2949128 | tf_op jit(solution)/shard_map/ppermute | solution.py:977
  1107.7 64.0 %collective-permute-start.78 = (f32[1280,256]{1,0:T(8,128)}, f32[1280,256]{1,0:T(8,128)}, u32[]{:S(2)}, u32[]{:S(2)}) collective-permute-start(f32[1280,256]{1,0:T(8,128)} %copy-done.76), channel_id=1, source_target_pairs={{0,4},{4,0},{8,12},{12,8},{16,20},{20,16},{24,28},{28,24},{1,5},{5... | collective-permute-start | bytes 3932168 | tf_op jit(solution)/shard_map/ppermute | solution.py:972
  1132.0 480.0 %reduce-scatter.6.cloned.1.call-start = ((), (), s32[]{:S(2)}) async-start(), calls=%async_computation.4 | async-start | bytes 3932160 | tf_op jit(solution)/shard_map/reduce_scatter | solution.py:1326
  1134.2 77.3 %collective-permute-start.92 = (bf16[2,2,384,1024]{3,2,1,0:T(8,128)(2,1)}, bf16[2,2,384,1024]{3,2,1,0:T(8,128)(2,1)}, u32[]{:S(2)}, u32[]{:S(2)}) collective-permute-start(bf16[2,2,384,1024]{3,2,1,0:T(8,128)(2,1)} %bitcast.598), channel_id=1, source_target_pairs={{0,8},{4,12},{8,0},{12,4},{16,24},{20,28},{24,16},{28,20},{1,9},{5... | collective-permute-start | bytes 9437192 | tf_op jit(solution)/shard_map/ppermute | solution.py:977
  1185.9 174.1 %collective-permute-start.79 = (bf16[1280,1024]{1,0:T(8,128)(2,1)}, bf16[1280,1024]{1,0:T(8,128)(2,1)}, u32[]{:S(2)}, u32[]{:S(2)}) collective-permute-start(bf16[1280,1024]{1,0:T(8,128)(2,1)} %get-tuple-element.680), channel_id=1, source_target_pairs={{0,4},{4,0},{8,12},{12,8},{16,20},{20,16},{24,28},{28,24},{1,5},{5... | collective-permute-start | bytes 7864328 | tf_op jit(solution)/shard_map/ppermute | solution.py:972
  1219.3 45.2 %collective-permute-start.123 = (bf16[1,2,384,1024]{3,2,1,0:T(8,128)(2,1)}, bf16[1,2,384,1024]{3,2,1,0:T(8,128)(2,1)}, u32[]{:S(2)}, u32[]{:S(2)}) collective-permute-start(bf16[1,2,384,1024]{3,2,1,0:T(8,128)(2,1)} %slice.1170), channel_id=1, source_target_pairs={{0,16},{4,20},{8,24},{12,28},{16,0},{20,4},{24,8},{28,12},{1,17},{... | collective-permute-start | bytes 4718600 | tf_op jit(solution)/shard_map/ppermute | solution.py:977
  1221.0 51.3 %collective-permute-start.122 = (bf16[1,2,384,1024]{3,2,1,0:T(8,128)(2,1)}, bf16[1,2,384,1024]{3,2,1,0:T(8,128)(2,1)}, u32[]{:S(2)}, u32[]{:S(2)}) collective-permute-start(bf16[1,2,384,1024]{3,2,1,0:T(8,128)(2,1)} %slice.1171), channel_id=1, source_target_pairs={{0,8},{4,12},{8,0},{12,4},{16,24},{20,28},{24,16},{28,20},{1,9},{5... | collective-permute-start | bytes 4718600 | tf_op jit(solution)/shard_map/ppermute | solution.py:977
  1225.6 65.6 %collective-permute-start.97 = (bf16[2,2,384,640]{3,2,1,0:T(8,128)(2,1)}, bf16[2,2,384,640]{3,2,1,0:T(8,128)(2,1)}, u32[]{:S(2)}, u32[]{:S(2)}) collective-permute-start(bf16[2,2,384,640]{3,2,1,0:T(8,128)(2,1)} %bitcast.155), channel_id=1, source_target_pairs={{0,16},{4,20},{8,24},{12,28},{16,0},{20,4},{24,8},{28,12},{1,17},{... | collective-permute-start | bytes 5898248 | tf_op jit(solution)/shard_map/ppermute | solution.py:977
  1256.1 44.4 %collective-permute-start.98 = (bf16[2,2,384,640]{3,2,1,0:T(8,128)(2,1)}, bf16[2,2,384,640]{3,2,1,0:T(8,128)(2,1)}, u32[]{:S(2)}, u32[]{:S(2)}) collective-permute-start(bf16[2,2,384,640]{3,2,1,0:T(8,128)(2,1)} %bitcast.565), channel_id=1, source_target_pairs={{0,8},{4,12},{8,0},{12,4},{16,24},{20,28},{24,16},{28,20},{1,9},{5... | collective-permute-start | bytes 5898248 | tf_op jit(solution)/shard_map/ppermute | solution.py:977
  1281.5 73.2 %collective-permute-start.124 = (bf16[2,2,128,384]{3,2,1,0:T(8,128)(2,1)}, bf16[2,2,128,384]{3,2,1,0:T(8,128)(2,1)}, u32[]{:S(2)}, u32[]{:S(2)}) collective-permute-start(bf16[2,2,128,384]{3,2,1,0:T(8,128)(2,1)} %bitcast.202), channel_id=1, source_target_pairs={{0,16},{4,20},{8,24},{12,28},{16,0},{20,4},{24,8},{28,12},{1,17},{... | collective-permute-start | bytes 1179656 | tf_op jit(solution)/shard_map/ppermute | solution.py:977
  1288.1 68.9 %collective-permute-start.126 = (bf16[2,2,128,384]{3,2,1,0:T(8,128)(2,1)}, bf16[2,2,128,384]{3,2,1,0:T(8,128)(2,1)}, u32[]{:S(2)}, u32[]{:S(2)}) collective-permute-start(bf16[2,2,128,384]{3,2,1,0:T(8,128)(2,1)} %bitcast.205), channel_id=1, source_target_pairs={{0,8},{4,12},{8,0},{12,4},{16,24},{20,28},{24,16},{28,20},{1,9},{5... | collective-permute-start | bytes 1179656 | tf_op jit(solution)/shard_map/ppermute | solution.py:977
  1421.7 89.7 %collective-permute-start.134 = (bf16[1,2,384,640]{3,2,1,0:T(8,128)(2,1)}, bf16[1,2,384,640]{3,2,1,0:T(8,128)(2,1)}, u32[]{:S(2)}, u32[]{:S(2)}) collective-permute-start(bf16[1,2,384,640]{3,2,1,0:T(8,128)(2,1)} %slice.1175), channel_id=1, source_target_pairs={{0,8},{4,12},{8,0},{12,4},{16,24},{20,28},{24,16},{28,20},{1,9},{5... | collective-permute-start | bytes 2949128 | tf_op jit(solution)/shard_map/ppermute | solution.py:977
  1423.0 90.5 %collective-permute-start.135 = (bf16[1,2,384,640]{3,2,1,0:T(8,128)(2,1)}, bf16[1,2,384,640]{3,2,1,0:T(8,128)(2,1)}, u32[]{:S(2)}, u32[]{:S(2)}) collective-permute-start(bf16[1,2,384,640]{3,2,1,0:T(8,128)(2,1)} %slice.1174), channel_id=1, source_target_pairs={{0,16},{4,20},{8,24},{12,28},{16,0},{20,4},{24,8},{28,12},{1,17},{... | collective-permute-start | bytes 2949128 | tf_op jit(solution)/shard_map/ppermute | solution.py:977
  1423.8 97.3 %collective-permute-start.105 = (bf16[2,2,256,1024]{2,3,1,0:T(8,128)(2,1)}, bf16[2,2,256,1024]{2,3,1,0:T(8,128)(2,1)}, u32[]{:S(2)}, u32[]{:S(2)}) collective-permute-start(bf16[2,2,256,1024]{2,3,1,0:T(8,128)(2,1)} %copy.639), channel_id=1, source_target_pairs={{0,16},{4,20},{8,24},{12,28},{16,0},{20,4},{24,8},{28,12},{1,17},{... | collective-permute-start | bytes 6291464 | tf_op jit(solution)/shard_map/ppermute | solution.py:977
  1425.2 98.5 %collective-permute-start.107 = (bf16[2,2,256,1024]{2,3,1,0:T(8,128)(2,1)}, bf16[2,2,256,1024]{2,3,1,0:T(8,128)(2,1)S(1)}, u32[]{:S(2)}, u32[]{:S(2)}) collective-permute-start(bf16[2,2,256,1024]{2,3,1,0:T(8,128)(2,1)} %copy.641), channel_id=1, source_target_pairs={{0,8},{4,12},{8,0},{12,4},{16,24},{20,28},{24,16},{28,20},{1,9},{5... | collective-permute-start | bytes 6291464 | tf_op jit(solution)/shard_map/ppermute | solution.py:977
  1425.4 67.8 %collective-permute-start.86 = (f32[224,128]{1,0:T(8,128)S(1)}, f32[224,128]{1,0:T(8,128)S(1)}, u32[]{:S(2)}, u32[]{:S(2)}) collective-permute-start(f32[224,128]{1,0:T(8,128)S(1)} %fusion.347), channel_id=1, source_target_pairs={{0,16},{4,20},{8,24},{12,28},{16,0},{20,4},{24,8},{28,12},{1,17},{... | collective-permute-start | bytes 344072 | tf_op jit(solution)/shard_map/ppermute | solution.py:977
  1563.6 44.2 %collective-permute-start.110 = (bf16[256,1024]{0,1:T(8,128)(2,1)S(1)}, bf16[256,1024]{0,1:T(8,128)(2,1)S(1)}, u32[]{:S(2)}, u32[]{:S(2)}) collective-permute-start(bf16[256,1024]{0,1:T(8,128)(2,1)S(1)} %get-tuple-element.347), channel_id=1, source_target_pairs={{0,2},{1,3},{2,0},{3,1},{4,6},{5,7},{6,4},{7,5},{8,10},{9,11},{10,... | collective-permute-start | bytes 1572872 | tf_op jit(solution)/shard_map/ppermute | solution.py:984
  1563.6 44.2 %collective-permute-start.109 = (bf16[256,1024]{0,1:T(8,128)(2,1)S(1)}, bf16[256,1024]{0,1:T(8,128)(2,1)S(1)}, u32[]{:S(2)}, u32[]{:S(2)}) collective-permute-start(bf16[256,1024]{0,1:T(8,128)(2,1)S(1)} %get-tuple-element.346), channel_id=1, source_target_pairs={{0,1},{1,0},{2,3},{3,2},{4,5},{5,4},{6,7},{7,6},{8,9},{9,8},{10,11... | collective-permute-start | bytes 1572872 | tf_op jit(solution)/shard_map/ppermute | solution.py:984
  (425 other events, 5302.7 us)
Sparse Core Ops, SparseCore 0:
  29.3 48.4 all-gather.13
  98.9 34.9 all-gather.15
  146.0 42.8 all-gather.17
  288.6 60.9 all-gather.19
  377.5 35.0 all-gather.21
  488.7 37.3 all-gather.23
  1008.6 34.4 reduce-scatter.3
  1132.1 40.5 reduce-scatter.7
  1277.3 58.7 reduce-scatter.5

commit v2 on v1

--- a/solution.py
+++ b/solution.py
@@ -1345,24 +1345,6 @@
         return parts
 
 
-def scatter_rest(place, kept, sent, bits, chip_axis, over_depth=True):
-    for step, bit in enumerate(bits):
-        if step > 0:
-            half = kept.shape[chip_axis] // 2
-            sent = to_low(lax.slice_in_dim(kept, half, 2 * half, axis=chip_axis))
-            kept = lax.slice_in_dim(kept, 0, half, axis=chip_axis)
-        kept = kept + chip_swap(sent, bit).astype(jnp.float32)
-    if not over_depth:
-        return kept
-    axis = 1 - chip_axis
-    size = kept.shape[axis] // place.depths
-    total = lax.slice_in_dim(kept, 0, size, axis=axis)
-    for k in range(1, place.depths):
-        block = to_low(lax.slice_in_dim(kept, k * size, (k + 1) * size, axis=axis))
-        total = total + depth_swap(block, k).astype(jnp.float32)
-    return total
-
-
 def core_sum(partial):
     return partial + core_swap(to_low(partial)).astype(jnp.float32)
 
@@ -1445,17 +1427,6 @@
             full, block, (k * 2 + place.core) * size, values.ndim - 1
         )
     return full
-
-
-def sum_everywhere(place, values):
-    values = core_sum_exact(values)
-    for bit in place.bits:
-        values = values + chip_swap(values, bit)
-    offset = 1
-    while offset < place.depths:
-        values = values + depth_swap(values, offset)
-        offset *= 2
-    return values
 
 
 def norm_forward(values, gain):
@@ -1555,25 +1526,24 @@
     return (gradient + grad_in, weight_grads, small_grads, (normed_low, small_from))
 
 
-def small_scatter(place, pairs, half_maps, heads):
-    bits = place.bits[::-1]
-    order = send_order(place, bits)
-    wholes = [left_product(normed, small_from) for normed, small_from in pairs]
-    whole = jnp.concatenate(wholes, 1)
-    size = whole.shape[0] // place.chips
-    ordered = [whole[r * size : (r + 1) * size] for r in order]
-    half = place.chips // 2
-    kept = jnp.concatenate(ordered[:half], 0)
-    sent = to_low(jnp.concatenate(ordered[half:], 0))
-    block = scatter_rest(place, kept, sent, bits, 0, over_depth=False)
-    offset = 1
-    while offset < place.depths:
-        block = block + depth_swap(block, offset)
-        offset *= 2
-    width = block.shape[1] // len(pairs)
-    layers = jnp.stack([block[:, n * width : (n + 1) * width] for n in range(len(pairs))])
-    own_dt = pick(layers[:, :, half_maps:], place.depth, heads // place.depths, 2)
-    return join_columns(place, layers[:, :, :half_maps]), join_columns(place, own_dt)
+def small_scatter(place, pairs, half_maps, waits):
+    wholes = []
+    for normed, small_from in pairs:
+        whole = left_product(normed, small_from)
+        maps = jnp.zeros((whole.shape[0], 2 * half_maps), jnp.float32)
+        maps = lax.dynamic_update_slice_in_dim(
+            maps, whole[:, :half_maps], place.core * half_maps, 1
+        )
+        wholes += [maps, all_channels(place, whole[:, half_maps:])]
+    rows = reorder(jnp.concatenate(wholes, 1), place.chips, place.chip, 0)
+    rows = lax.psum(lax.psum_scatter(rows, "dp", scatter_dimension=0, tiled=True), "mp")
+    rows = held_for(rows, waits)
+    width = rows.shape[1] // 2
+    layers = jnp.stack([rows[:, :width], rows[:, width:]])
+    steps = layers[:, :, 2 * half_maps :]
+    return layers[:, :, : 2 * half_maps], pick(
+        steps, place.depth, steps.shape[2] // place.depths, 2
+    )
 
 
 def one_device(
@@ -1617,6 +1587,17 @@
     )
     out_shard = split_rows(place, mamba_out)
     router_shard = split_columns(place, [router_qk[0], router_qk[1]])
+    qkv_shard = split_columns(place, [attn_qkv[0], attn_qkv[1], attn_qkv[2]])
+    qkv_packed = jnp.pad(qkv_shard, ((0, 0), (0, -qkv_shard.shape[1] % LANES)))
+    router_shard, qkv_packed, attn_out_shard, ffn_shard, ffn_down_shard = lax.optimization_barrier(
+        (
+            router_shard,
+            qkv_packed,
+            split_rows(place, attn_out),
+            split_columns(place, [ffn_gate_up[0], ffn_gate_up[1]]),
+            split_rows(place, ffn_down),
+        )
+    )
     enc_out, w_router, w_up = gather.matrices(
         [("rows", out_shard[0]), ("columns", router_shard), ("folded", group_up)]
     )
@@ -1627,11 +1608,9 @@
     fill = jnp.zeros(dt_shard.shape[:2] + (LANES - dt_shard.shape[2],), jnp.bfloat16)
     w_bcdt = gather_chips(place, jnp.concatenate([bc_shard, dt_shard, fill], -1), place.bits)
     enc_weights = (enc_zx, w_bcdt[0], enc_out)
-    qkv_shard = split_columns(place, [attn_qkv[0], attn_qkv[1], attn_qkv[2]])
-    qkv_fill = -qkv_shard.shape[1] % LANES
-    (w_qkv,) = gather.matrices([("columns", jnp.pad(qkv_shard, ((0, 0), (0, qkv_fill))))])
+    (w_qkv,) = gather.matrices([("columns", qkv_packed)])
     w_attn_out, w_down = gather.matrices(
-        [("rows", split_rows(place, attn_out)), ("columns", group_down)], filled=True
+        [("rows", attn_out_shard), ("columns", group_down)], filled=True
     )
     boundary_flags, segment_ids = lax.optimization_barrier(
         (boundary_flags, segment_ids, w_bcdt)
@@ -1675,9 +1654,8 @@
         place, residual, enc_weights, mamba_params[0], items
     )
 
-    ffn_shard = split_columns(place, [ffn_gate_up[0], ffn_gate_up[1]])
     (w_gate_up,) = gather.matrices([("columns", ffn_shard)], [enc_memory[4]])
-    (w_ffn_down,) = gather.matrices([("rows", split_rows(place, ffn_down))], [enc_memory[1]])
+    (w_ffn_down,) = gather.matrices([("rows", ffn_down_shard)], [enc_memory[1]])
 
     shared = to_low(encoded)
     length = shared.shape[0]
@@ -1811,7 +1789,7 @@
     flat = jnp.concatenate([part.reshape(-1) for part in parts])
     fill = -flat.shape[0] % 1024
     flat = jnp.pad(flat, (0, fill)).reshape(-1, 128)
-    flat = sum_everywhere(place, flat).reshape(-1)
+    flat = held_for(lax.psum(flat, ("dp", "mp")), scatter.far[-1]).reshape(-1)
     summed = []
     offset = 0
     for part in parts:
@@ -1819,8 +1797,7 @@
         offset += part.size
     smalls = [jnp.stack([summed[n], summed[7 + n]]) for n in range(7)]
 
-    head_count = mamba_dt.shape[2] * place.depths // 2
-    grad_bc, grad_dt = small_scatter(place, [enc_maps, dec_maps], LANES, head_count)
+    grad_bc, grad_dt = small_scatter(place, [enc_maps, dec_maps], LANES, scatter.far[-1])
 
     def kinds(blocks, count):
         return join_columns(place, jnp.stack(jnp.split(blocks, count, 1)))

time: 1650 us -> 1540 us (0.933)
  local copies, waits for them, and re-layouts: 258 us -> 220 us
  waiting for transfers between devices: 477 us -> 440 us
  starting transfers between devices: 161 us -> 144 us
    ppermute x63 -> x59, waiting for transfers between devices: 250 us -> 202 us  [chip_swap(): return lax.ppermute(values, 'dp', [(d, d ^ bit * 2) for d in range(size)])]
    unnamed x695 -> x655, local copies, waits for them, and re-layouts: 86.3 us -> 61.6 us
    ppermute x49 -> x46, starting transfers between devices: 74.5 us -> 60.3 us  [core_swap(): return lax.ppermute(values, 'dp', [(d, d ^ 1) for d in range(size)])]
    ppermute x31 -> x27, waiting for transfers between devices: 179 us -> 189 us  [depth_swap(): return lax.ppermute(values, 'mp', [(d, d ^ offset) for d in range(size)])]
    ppermute x31 -> x27, starting transfers between devices: 37 us -> 33 us  [depth_swap(): return lax.ppermute(values, 'mp', [(d, d ^ offset) for d in range(size)])]
    ppermute x63 -> x59, starting transfers between devices: 48.6 us -> 48.8 us  [chip_swap(): return lax.ppermute(values, 'dp', [(d, d ^ bit * 2) for d in range(size)])]
  transfers between devices with their start and end apart: 152 -> 144, of which waited for: 41 -> 41; matrix products, arithmetic and copies ran while one was open for 32% -> 32% of each run, Pallas kernels for 18% -> 19%
where the time goes in v2:
time: 1540 us; the launch traced here: 1530 us
  waiting for transfers between devices  440 us (29%)
  Pallas kernels  335 us (22%)
  local copies, waits for them, and re-layouts  220 us (14%)
  other arithmetic  217 us (14%)
  starting transfers between devices  144 us (9%)
  matrix products  135 us (9%)
  between operations  19.8 us (1%)
  blocking collectives  19 us (1%)
    ppermute x59, waiting for transfers between devices, chip_swap(): return lax.ppermute(values, 'dp', [(d, d ^ bit * 2) for d in range(size)])  202 us
    ppermute x27, waiting for transfers between devices, depth_swap(): return lax.ppermute(values, 'mp', [(d, d ^ offset) for d in range(size)])  189 us
    pallas_call x28, Pallas kernels, blocks(): pl.pallas_call(functools.partial(products_kernel, [kind for kind, _, _ in...  106 us
    pallas_call x2, Pallas kernels, mix_backward(): pl.pallas_call(functools.partial(mix_back_kernel, per_block), grid=(chunk...  84.5 us
    dot_general x14, matrix products, matmul(): return jnp.dot(left, right, preferred_element_type=jnp.float32)  72.2 us
    unnamed x655, local copies, waits for them, and re-layouts  61.6 us
    ppermute x46, starting transfers between devices, core_swap(): return lax.ppermute(values, 'dp', [(d, d ^ 1) for d in range(size)])  60.3 us
    dot_general x13, matrix products, right_product(): lax.dot_general(left, right, (((1,), (1,)), ((), ())), preferred_element_...  58.4 us
  transfers between devices with their start and end apart: 144, of which 41 were waited for; matrix products, arithmetic and copies ran while one was open for 32% of the time, Pallas kernels for 19%

profile of v2, /device:TPU:1, one launch (start us, length us, event | category | flops | bytes accessed | tf_op | source)
XLA Modules:
  0.0 1528.1 jit_solution(15066010477281890283)
XLA Ops:
  60.9 5.7 collective-permute-done.14
  66.6 20.5 %collective-permute-done.13 = bf16[640,256]{1,0:T(8,128)(2,1)} collective-permute-done((bf16[640,256]{1,0:T(8,128)(2,1)}, bf16[640,256]{1,0:T(8,128)(2,1)}, u32[]{:S(2)}, u32[]{:S(2)}) %collective-permute-start.13) | collective-permute-done | bytes 327712 | tf_op jit(solution)/shard_map/ppermute | solution.py:984
  114.3 18.6 %all-gather.16.cloned.1.call-done = bf16[1024,768]{1,0:T(8,128)(2,1)} async-done(((bf16[256,768]{1,0:T(8,128)(2,1)}), bf16[1024,768]{1,0:T(8,128)(2,1)}) %all-gather.16.cloned.1.call-update) | async-done | bytes 1572880 | tf_op jit(solution)/shard_map/all_gather | solution.py:1160
  145.9 33.2 %collective-permute-done.18.refs_3_ = bf16[2,256,512]{2,1,0:T(8,128)(2,1)S(1)} collective-permute-done((bf16[2,256,512]{2,1,0:T(8,128)(2,1)}, bf16[2,256,512]{2,1,0:T(8,128)(2,1)S(1)}, u32[]{:S(2)}, u32[]{:S(2)}) %collective-permute-start.18) | collective-permute-done | bytes 524320 | tf_op jit(solution)/shard_map/ppermute | solution.py:977
  187.3 10.3 fusion.294.zx_ref.zx_tail_ref
  197.7 20.2 %shard_map.400 = (bf16[1280,1024]{1,0:T(8,128)(2,1)S(1)}, f32[1280,1024]{1,0:T(8,128)}, f32[1280,1]{1,0:T(8,128)S(1)}, bf16[1280,1024]{1,0:T(8,128)(2,1)}) custom-call(f32[1280,2048]{1,0:T(8,128)} %fusion.294.zx_ref.zx_tail_ref, f32[1280,384]{1,0:T(8,128)S(1)} %fusion.249.bcdt_ref.maps_tail_ref, f32[1280,8]{1,0:T(8,128)S(1)} %stack.195.columns_ref, ...), custom_call_target="tpu_custom_call" | custom-call | flops 1342177280 | bytes 20971520 | tf_op jit(solution)/shard_map/pallas_call | solution.py:401
  218.0 5.6 shard_map.401
  223.7 7.1 fusion.283
  245.3 19.0 %all-gather.3 = bf16[768,640]{1,0:T(8,128)(2,1)} all-gather(bf16[192,640]{1,0:T(8,128)(2,1)S(1)} %copy-done.189), channel_id=5, replica_groups=mesh['dp'=8,'mp'=4] {'mp'}, dimensions={0}, use_global_device_ids=true | all-gather | bytes 1228800 | tf_op jit(solution)/shard_map/all_gather | solution.py:1160
  265.9 12.6 collective-permute-done.34.refs_1_
  279.9 6.4 fusion.257
  328.2 12.7 collective-permute-done.41.refs_4_
  347.2 5.7 shard_map.403
  366.4 26.2 %all-gather.22.cloned.1.call-done = bf16[2048,384]{0,1:T(8,128)(2,1)} async-done(((bf16[512,384]{0,1:T(8,128)(2,1)}), bf16[2048,384]{0,1:T(8,128)(2,1)}) %all-gather.22.cloned.1.call-update) | async-done | bytes 1572880 | tf_op jit(solution)/shard_map/all_gather | solution.py:1160
  398.8 9.0 shard_map.404.refs_1_
  412.4 8.3 collective-permute-done.43.refs_1_
  420.7 5.8 collective-permute-start.53
  435.8 18.6 %collective-permute-done.47.refs_1_ = bf16[4,512,384]{2,1,0:T(8,128)(2,1)} collective-permute-done((bf16[4,512,384]{2,1,0:T(8,128)(2,1)S(1)}, bf16[4,512,384]{2,1,0:T(8,128)(2,1)}, u32[]{:S(2)}, u32[]{:S(2)}) %collective-permute-start.47) | collective-permute-done | bytes 1572896 | tf_op jit(solution)/shard_map/ppermute | solution.py:977
  464.5 24.5 %collective-permute-done.45.refs_3_ = bf16[2,384,1024]{2,1,0:T(8,128)(2,1)} collective-permute-done((bf16[2,384,1024]{2,1,0:T(8,128)(2,1)}, bf16[2,384,1024]{2,1,0:T(8,128)(2,1)}, u32[]{:S(2)}, u32[]{:S(2)}) %collective-permute-start.45) | collective-permute-done | bytes 1572896 | tf_op jit(solution)/shard_map/ppermute | solution.py:977
  489.0 9.5 shard_map.406
  498.5 7.4 collective-permute-done.49.refs_3_
  505.8 5.6 shard_map.408
  511.5 10.5 fusion.297.pair_ref
  571.5 13.0 shard_map.409
  584.5 10.6 collective-permute-done.66
  605.8 10.2 collective-permute-done.56.refs_3_
  623.3 10.3 fusion.298.zx_ref.zx_tail_ref
  633.6 20.3 %shard_map.411 = (bf16[1280,1024]{1,0:T(8,128)(2,1)S(1)}, f32[1280,1024]{1,0:T(8,128)}, f32[1280,1]{1,0:T(8,128)S(1)}, bf16[1280,1024]{1,0:T(8,128)(2,1)}) custom-call(f32[1280,2048]{1,0:T(8,128)} %fusion.298.zx_ref.zx_tail_ref, f32[1280,384]{1,0:T(8,128)S(1)} %fusion.247.bcdt_ref.maps_tail_ref, f32[1280,8]{1,0:T(8,128)S(1)} %stack.195.columns_ref, ...), custom_call_target="tpu_custom_call" | custom-call | flops 1342177280 | bytes 20971520 | tf_op jit(solution)/shard_map/pallas_call | solution.py:401
  664.0 8.3 fusion.289
  692.1 42.0 %shard_map.412 = (bf16[1280,2048]{1,0:T(8,128)(2,1)}, f32[1280,256]{1,0:T(8,128)}, f32[1280,128]{1,0:T(8,128)S(1)}, f32[32,1024]{1,0:T(8,128)S(1)}, f32[32,256]{...) custom-call(f32[1280,1024]{1,0:T(8,128)} %get-tuple-element.681.grad_ref, ...), custom_call_target="tpu_custom_call" | custom-call | flops 4026531840 | bytes 20971520 | tf_op jit(solution)/shard_map/pallas_call | solution.py:461
  752.7 8.3 fusion.288
  781.4 9.6 fusion.8
  791.0 5.9 shard_map.418
  798.1 6.7 shard_map.419
  804.8 6.9 shard_map.421
  817.3 12.9 shard_map.413
  838.0 7.8 shard_map.416.refs_5_
  863.3 9.2 fusion.290
  875.4 5.9 shard_map.420
  908.2 12.2 shard_map.415.refs_1_
  920.4 8.3 fusion.291
  964.0 10.6 collective-permute-done.94
  1002.9 7.2 multiply_convert_fusion
  1025.6 42.5 %shard_map.417 = (bf16[1280,2048]{1,0:T(8,128)(2,1)}, f32[1280,256]{1,0:T(8,128)S(1)}, f32[1280,128]{1,0:T(8,128)S(1)}, f32[32,1024]{1,0:T(8,128)S(1)}, f32[32,2...) custom-call(f32[1280,1024]{1,0:T(8,128)} %get-tuple-element.693.grad_ref, ...), custom_call_target="tpu_custom_call" | custom-call | flops 4026531840 | bytes 20971520 | tf_op jit(solution)/shard_map/pallas_call | solution.py:461
  1082.1 8.0 collective-permute-done.99
  1102.7 25.2 %collective-permute-done.121 = bf16[192,640]{1,0:T(8,128)(2,1)S(1)} collective-permute-done((bf16[192,640]{1,0:T(8,128)(2,1)S(1)}, bf16[192,640]{1,0:T(8,128)(2,1)S(1)}, u32[]{:S(2)}, u32[]{:S(2)}) %collective-permute-start.121) | collective-permute-done | bytes 245792 | tf_op jit(solution)/shard_map/ppermute | solution.py:984
  1130.0 9.7 collective-permute-start.129
  1143.9 8.2 fusion.293
  1159.2 7.2 convert_add_fusion.3
  1172.3 5.5 slice.1214
  1214.2 6.6 collective-permute-done.112
  1242.4 21.0 %collective-permute-done.92 = bf16[2,2,384,640]{3,2,1,0:T(8,128)(2,1)} collective-permute-done((bf16[2,2,384,640]{3,2,1,0:T(8,128)(2,1)}, bf16[2,2,384,640]{3,2,1,0:T(8,128)(2,1)}, u32[]{:S(2)}, u32[]{:S(2)}) %collective-permute-start.92) | collective-permute-done | bytes 1966112 | tf_op jit(solution)/shard_map/ppermute | solution.py:977
  1272.6 7.3 shard_map.440
  1279.9 7.3 shard_map.441
  1288.7 7.3 shard_map.438
  1296.0 7.4 shard_map.439
  1306.1 6.4 fusion.16
  1322.6 16.6 %collective-permute-done.81 = bf16[640,256]{1,0:T(8,128)(2,1)S(1)} collective-permute-done((bf16[640,256]{1,0:T(8,128)(2,1)S(1)}, bf16[640,256]{1,0:T(8,128)(2,1)S(1)}, u32[]{:S(2)}, u32[]{:S(2)}) %collective-permute-start.81) | collective-permute-done | bytes 327712 | tf_op jit(solution)/shard_map/ppermute | solution.py:984
  1341.7 7.4 collective-permute-start.83
  1362.2 9.5 collective-permute-done.127
  1371.7 35.9 %collective-permute-done.126 = bf16[384,640]{1,0:T(8,128)(2,1)S(1)} collective-permute-done((bf16[384,640]{1,0:T(8,128)(2,1)S(1)}, bf16[384,640]{1,0:T(8,128)(2,1)S(1)}, u32[]{:S(2)}, u32[]{:S(2)}) %collective-permute-start.126) | collective-permute-done | bytes 491552 | tf_op jit(solution)/shard_map/ppermute | solution.py:984
  1418.1 18.5 %collective-permute-done.103 = bf16[1,2,256,1024]{3,2,1,0:T(8,128)(2,1)S(1)} collective-permute-done((bf16[1,2,256,1024]{3,2,1,0:T(8,128)(2,1)S(1)}, bf16[1,2,256,1024]{3,2,1,0:T(8,128)(2,1)S(1)}, u32[]{:S(2)}, u32[]{:S(2)}) %collective-permute-start.103) | collective-permute-done | bytes 1048608 | tf_op jit(solution)/shard_map/ppermute | solution.py:977
  1457.2 10.5 collective-permute-done.106
  1467.7 42.0 %collective-permute-done.105 = bf16[256,1024]{1,0:T(8,128)(2,1)} collective-permute-done((bf16[256,1024]{1,0:T(8,128)(2,1)}, bf16[256,1024]{1,0:T(8,128)(2,1)}, u32[]{:S(2)}, u32[]{:S(2)}) %collective-permute-start.105) | collective-permute-done | bytes 524320 | tf_op jit(solution)/shard_map/ppermute | solution.py:984
  (1457 shorter events, 669.6 us)
Async XLA Ops:
  7.2 90.0 %all-gather.14.cloned.1.call-start = ((), (), s32[]{:S(2)}) async-start(), calls=%async_computation.10 | async-start | bytes 1310720 | tf_op jit(solution)/shard_map/all_gather | solution.py:1160
  13.0 38.9 %collective-permute-start.11 = (bf16[2,1,640,256]{3,2,1,0:T(8,128)(2,1)}, bf16[2,1,640,256]{3,2,1,0:T(8,128)(2,1)}, u32[]{:S(2)}, u32[]{:S(2)}) collective-permute-start(bf16[2,1,640,256]{3,2,1,0:T(8,128)(2,1)} %constant_dynamic-slice_fusion.103), channel_id=1, source_target_pairs={{0,4},{4,0},{8,12},{12,8},{16,20},{20,16},{24,28},{28,24},{1,5},{5... | collective-permute-start | bytes 1966088 | tf_op jit(solution)/shard_map/ppermute | solution.py:972
  28.5 104.5 %all-gather.16.cloned.1.call-start = ((), (), s32[]{:S(2)}) async-start(), calls=%async_computation.11 | async-start | bytes 1966080 | tf_op jit(solution)/shard_map/all_gather | solution.py:1160
  48.9 39.8 %collective-permute-start.7 = (bf16[2,256,384]{2,1,0:T(8,128)(2,1)S(1)}, bf16[2,256,384]{2,1,0:T(8,128)(2,1)}, u32[]{:S(2)}, u32[]{:S(2)}) collective-permute-start(bf16[2,256,384]{2,1,0:T(8,128)(2,1)S(1)} %concatenate.397), channel_id=1, source_target_pairs={{0,16},{4,20},{8,24},{12,28},{16,0},{20,4},{24,8},{28,12},{1,17},{... | collective-permute-start | bytes 1179656 | tf_op jit(solution)/shard_map/ppermute | solution.py:977
  93.2 41.5 %collective-permute-start.15 = (bf16[640,1024]{1,0:T(8,128)(2,1)}, bf16[640,1024]{1,0:T(8,128)(2,1)}, u32[]{:S(2)}, u32[]{:S(2)}) collective-permute-start(bf16[640,1024]{1,0:T(8,128)(2,1)} %pad_maximum_fusion.12), channel_id=1, source_target_pairs={{0,4},{4,0},{8,12},{12,8},{16,20},{20,16},{24,28},{28,24},{1,5},{5... | collective-permute-start | bytes 3932168 | tf_op jit(solution)/shard_map/ppermute | solution.py:972
  97.2 136.5 %all-gather.18.cloned.1.call-start = ((), (), s32[]{:S(2)}) async-start(), calls=%async_computation.12 | async-start | bytes 2457600 | tf_op jit(solution)/shard_map/all_gather | solution.py:1160
  133.0 50.6 %collective-permute-start.26 = (bf16[4,256,768]{2,1,0:T(8,128)(2,1)}, bf16[4,256,768]{2,1,0:T(8,128)(2,1)}, u32[]{:S(2)}, u32[]{:S(2)}) collective-permute-start(bf16[4,256,768]{2,1,0:T(8,128)(2,1)} %bitcast.557), channel_id=1, source_target_pairs={{0,8},{4,12},{8,0},{12,4},{16,24},{20,28},{24,16},{28,20},{1,9},{5... | collective-permute-start | bytes 4718600 | tf_op jit(solution)/shard_map/ppermute | solution.py:977
  133.4 52.0 %collective-permute-start.27 = (bf16[4,256,768]{2,1,0:T(8,128)(2,1)}, bf16[4,256,768]{2,1,0:T(8,128)(2,1)}, u32[]{:S(2)}, u32[]{:S(2)}) collective-permute-start(bf16[4,256,768]{2,1,0:T(8,128)(2,1)} %bitcast.558), channel_id=1, source_target_pairs={{0,16},{4,20},{8,24},{12,28},{16,0},{20,4},{24,8},{28,12},{1,17},{... | collective-permute-start | bytes 4718600 | tf_op jit(solution)/shard_map/ppermute | solution.py:977
  139.3 39.8 %collective-permute-start.18 = (bf16[2,256,512]{2,1,0:T(8,128)(2,1)}, bf16[2,256,512]{2,1,0:T(8,128)(2,1)S(1)}, u32[]{:S(2)}, u32[]{:S(2)}) collective-permute-start(bf16[2,256,512]{2,1,0:T(8,128)(2,1)} %slice.888), channel_id=1, source_target_pairs={{0,16},{4,20},{8,24},{12,28},{16,0},{20,4},{24,8},{28,12},{1,17},{... | collective-permute-start | bytes 1572872 | tf_op jit(solution)/shard_map/ppermute | solution.py:977
  140.5 39.2 %collective-permute-start.19 = (bf16[2,256,512]{2,1,0:T(8,128)(2,1)}, bf16[2,256,512]{2,1,0:T(8,128)(2,1)}, u32[]{:S(2)}, u32[]{:S(2)}) collective-permute-start(bf16[2,256,512]{2,1,0:T(8,128)(2,1)} %slice.889), channel_id=1, source_target_pairs={{0,8},{4,12},{8,0},{12,4},{16,24},{20,28},{24,16},{28,20},{1,9},{5... | collective-permute-start | bytes 1572872 | tf_op jit(solution)/shard_map/ppermute | solution.py:977
  141.5 211.4 %all-gather.20.cloned.1.call-start = ((), (), s32[]{:S(2)}) async-start(), calls=%async_computation.13 | async-start | bytes 3932160 | tf_op jit(solution)/shard_map/all_gather | solution.py:1160
  230.8 49.1 %collective-permute-start.30 = (bf16[1280,1024]{1,0:T(8,128)(2,1)}, bf16[1280,1024]{1,0:T(8,128)(2,1)}, u32[]{:S(2)}, u32[]{:S(2)}) collective-permute-start(bf16[1280,1024]{1,0:T(8,128)(2,1)} %get-tuple-element.670), channel_id=1, source_target_pairs={{0,4},{4,0},{8,12},{12,8},{16,20},{20,16},{24,28},{28,24},{1,5},{5... | collective-permute-start | bytes 7864328 | tf_op jit(solution)/shard_map/ppermute | solution.py:972
  233.7 44.8 %collective-permute-start.34 = (bf16[4,384,640]{2,1,0:T(8,128)(2,1)}, bf16[4,384,640]{2,1,0:T(8,128)(2,1)S(1)}, u32[]{:S(2)}, u32[]{:S(2)}) collective-permute-start(bf16[4,384,640]{2,1,0:T(8,128)(2,1)} %bitcast.554), channel_id=1, source_target_pairs={{0,8},{4,12},{8,0},{12,4},{16,24},{20,28},{24,16},{28,20},{1,9},{5... | collective-permute-start | bytes 5898248 | tf_op jit(solution)/shard_map/ppermute | solution.py:977
  234.9 44.4 %collective-permute-start.35 = (bf16[4,384,640]{2,1,0:T(8,128)(2,1)}, bf16[4,384,640]{2,1,0:T(8,128)(2,1)}, u32[]{:S(2)}, u32[]{:S(2)}) collective-permute-start(bf16[4,384,640]{2,1,0:T(8,128)(2,1)} %bitcast.555), channel_id=1, source_target_pairs={{0,16},{4,20},{8,24},{12,28},{16,0},{20,4},{24,8},{28,12},{1,17},{... | collective-permute-start | bytes 5898248 | tf_op jit(solution)/shard_map/ppermute | solution.py:977
  279.4 113.2 %all-gather.22.cloned.1.call-start = ((), (), s32[]{:S(2)}) async-start(), calls=%async_computation.14 | async-start | bytes 1966080 | tf_op jit(solution)/shard_map/all_gather | solution.py:1160
  305.4 41.8 %collective-permute-start.36 = (bf16[2,384,640]{2,1,0:T(8,128)(2,1)}, bf16[2,384,640]{2,1,0:T(8,128)(2,1)}, u32[]{:S(2)}, u32[]{:S(2)}) collective-permute-start(bf16[2,384,640]{2,1,0:T(8,128)(2,1)} %slice.905), channel_id=1, source_target_pairs={{0,16},{4,20},{8,24},{12,28},{16,0},{20,4},{24,8},{28,12},{1,17},{... | collective-permute-start | bytes 2949128 | tf_op jit(solution)/shard_map/ppermute | solution.py:977
  308.1 39.0 %collective-permute-start.37 = (bf16[2,384,640]{2,1,0:T(8,128)(2,1)}, bf16[2,384,640]{2,1,0:T(8,128)(2,1)}, u32[]{:S(2)}, u32[]{:S(2)}) collective-permute-start(bf16[2,384,640]{2,1,0:T(8,128)(2,1)} %slice.906), channel_id=1, source_target_pairs={{0,8},{4,12},{8,0},{12,4},{16,24},{20,28},{24,16},{28,20},{1,9},{5... | collective-permute-start | bytes 2949128 | tf_op jit(solution)/shard_map/ppermute | solution.py:977
  352.9 67.7 %collective-permute-start.43 = (bf16[4,384,1024]{2,1,0:T(8,128)(2,1)}, bf16[4,384,1024]{2,1,0:T(8,128)(2,1)}, u32[]{:S(2)}, u32[]{:S(2)}) collective-permute-start(bf16[4,384,1024]{2,1,0:T(8,128)(2,1)} %bitcast.590), channel_id=1, source_target_pairs={{0,8},{4,12},{8,0},{12,4},{16,24},{20,28},{24,16},{28,20},{1,9},{5... | collective-permute-start | bytes 9437192 | tf_op jit(solution)/shard_map/ppermute | solution.py:977
  354.1 76.0 %collective-permute-start.44 = (bf16[4,384,1024]{2,1,0:T(8,128)(2,1)}, bf16[4,384,1024]{2,1,0:T(8,128)(2,1)}, u32[]{:S(2)}, u32[]{:S(2)}) collective-permute-start(bf16[4,384,1024]{2,1,0:T(8,128)(2,1)} %bitcast.591), channel_id=1, source_target_pairs={{0,16},{4,20},{8,24},{12,28},{16,0},{20,4},{24,8},{28,12},{1,17},{... | collective-permute-start | bytes 9437192 | tf_op jit(solution)/shard_map/ppermute | solution.py:977
  354.4 193.7 %all-gather.24.cloned.1.call-start = ((), (), s32[]{:S(2)}) async-start(), calls=%async_computation.15 | async-start | bytes 1966080 | tf_op jit(solution)/shard_map/all_gather | solution.py:1160
  394.4 59.9 %collective-permute-start.47 = (bf16[4,512,384]{2,1,0:T(8,128)(2,1)S(1)}, bf16[4,512,384]{2,1,0:T(8,128)(2,1)}, u32[]{:S(2)}, u32[]{:S(2)}) collective-permute-start(bf16[4,512,384]{2,1,0:T(8,128)(2,1)S(1)} %bitcast.542), channel_id=1, source_target_pairs={{0,8},{4,12},{8,0},{12,4},{16,24},{20,28},{24,16},{28,20},{1,9},{5... | collective-permute-start | bytes 4718600 | tf_op jit(solution)/shard_map/ppermute | solution.py:977
  395.7 61.8 %collective-permute-start.48 = (bf16[4,512,384]{2,1,0:T(8,128)(2,1)S(1)}, bf16[4,512,384]{2,1,0:T(8,128)(2,1)}, u32[]{:S(2)}, u32[]{:S(2)}) collective-permute-start(bf16[4,512,384]{2,1,0:T(8,128)(2,1)S(1)} %bitcast.543), channel_id=1, source_target_pairs={{0,16},{4,20},{8,24},{12,28},{16,0},{20,4},{24,8},{28,12},{1,17},{... | collective-permute-start | bytes 4718600 | tf_op jit(solution)/shard_map/ppermute | solution.py:977
  410.7 49.3 %collective-permute-start.42 = (bf16[320,1536]{1,0:T(8,128)(2,1)}, bf16[320,1536]{1,0:T(8,128)(2,1)}, u32[]{:S(2)}, u32[]{:S(2)}) collective-permute-start(bf16[320,1536]{1,0:T(8,128)(2,1)} %get-tuple-element.674), channel_id=1, source_target_pairs={{0,4},{4,0},{8,12},{12,8},{16,20},{20,16},{24,28},{28,24},{1,5},{5... | collective-permute-start | bytes 2949128 | tf_op jit(solution)/shard_map/ppermute | solution.py:972
  430.1 58.9 %collective-permute-start.45 = (bf16[2,384,1024]{2,1,0:T(8,128)(2,1)}, bf16[2,384,1024]{2,1,0:T(8,128)(2,1)}, u32[]{:S(2)}, u32[]{:S(2)}) collective-permute-start(bf16[2,384,1024]{2,1,0:T(8,128)(2,1)} %slice.910), channel_id=1, source_target_pairs={{0,16},{4,20},{8,24},{12,28},{16,0},{20,4},{24,8},{28,12},{1,17},{... | collective-permute-start | bytes 4718600 | tf_op jit(solution)/shard_map/ppermute | solution.py:977
  433.9 55.1 %collective-permute-start.46 = (bf16[2,384,1024]{2,1,0:T(8,128)(2,1)}, bf16[2,384,1024]{2,1,0:T(8,128)(2,1)}, u32[]{:S(2)}, u32[]{:S(2)}) collective-permute-start(bf16[2,384,1024]{2,1,0:T(8,128)(2,1)} %slice.911), channel_id=1, source_target_pairs={{0,8},{4,12},{8,0},{12,4},{16,24},{20,28},{24,16},{28,20},{1,9},{5... | collective-permute-start | bytes 4718600 | tf_op jit(solution)/shard_map/ppermute | solution.py:977
  456.5 49.4 %collective-permute-start.49 = (bf16[2,512,384]{2,1,0:T(8,128)(2,1)}, bf16[2,512,384]{2,1,0:T(8,128)(2,1)}, u32[]{:S(2)}, u32[]{:S(2)}) collective-permute-start(bf16[2,512,384]{2,1,0:T(8,128)(2,1)} %slice.912), channel_id=1, source_target_pairs={{0,16},{4,20},{8,24},{12,28},{16,0},{20,4},{24,8},{28,12},{1,17},{... | collective-permute-start | bytes 2359304 | tf_op jit(solution)/shard_map/ppermute | solution.py:977
  459.6 46.3 %collective-permute-start.50 = (bf16[2,512,384]{2,1,0:T(8,128)(2,1)}, bf16[2,512,384]{2,1,0:T(8,128)(2,1)}, u32[]{:S(2)}, u32[]{:S(2)}) collective-permute-start(bf16[2,512,384]{2,1,0:T(8,128)(2,1)} %slice.913), channel_id=1, source_target_pairs={{0,8},{4,12},{8,0},{12,4},{16,24},{20,28},{24,16},{28,20},{1,9},{5... | collective-permute-start | bytes 2359304 | tf_op jit(solution)/shard_map/ppermute | solution.py:977
  464.2 702.2 %reduce-scatter.5.cloned.1.call-start = ((), (), s32[]{:S(2)}) async-start(), calls=%async_computation.5 | async-start | bytes 1966080 | tf_op jit(solution)/shard_map/reduce_scatter | solution.py:1326
  560.6 38.9 %collective-permute-start.55 = (bf16[4,256,768]{2,1,0:T(8,128)(2,1)}, bf16[4,256,768]{2,1,0:T(8,128)(2,1)}, u32[]{:S(2)}, u32[]{:S(2)}) collective-permute-start(bf16[4,256,768]{2,1,0:T(8,128)(2,1)} %bitcast.61.refs_0_), channel_id=1, source_target_pairs={{0,16},{4,20},{8,24},{12,28},{16,0},{20,4},{24,8},{28,12},{1,17},{... | collective-permute-start | bytes 4718600 | tf_op jit(solution)/shard_map/ppermute | solution.py:977
  674.1 107.3 %collective-permute-start.58 = (bf16[1280,1024]{1,0:T(8,128)(2,1)}, bf16[1280,1024]{1,0:T(8,128)(2,1)}, u32[]{:S(2)}, u32[]{:S(2)}) collective-permute-start(bf16[1280,1024]{1,0:T(8,128)(2,1)} %get-tuple-element.684), channel_id=1, source_target_pairs={{0,4},{4,0},{8,12},{12,8},{16,20},{20,16},{24,28},{28,24},{1,5},{5... | collective-permute-start | bytes 7864328 | tf_op jit(solution)/shard_map/ppermute | solution.py:972
  850.9 151.9 %collective-permute-start.76 = (bf16[1280,1024]{1,0:T(8,128)(2,1)}, bf16[1280,1024]{1,0:T(8,128)(2,1)}, u32[]{:S(2)}, u32[]{:S(2)}) collective-permute-start(bf16[1280,1024]{1,0:T(8,128)(2,1)} %get-tuple-element.690), channel_id=1, source_target_pairs={{0,4},{4,0},{8,12},{12,8},{16,20},{20,16},{24,28},{28,24},{1,5},{5... | collective-permute-start | bytes 7864328 | tf_op jit(solution)/shard_map/ppermute | solution.py:972
  854.6 43.7 %collective-permute-start.63 = (bf16[2,640,256]{2,1,0:T(8,128)(2,1)}, bf16[2,640,256]{2,1,0:T(8,128)(2,1)}, u32[]{:S(2)}, u32[]{:S(2)}) collective-permute-start(bf16[2,640,256]{2,1,0:T(8,128)(2,1)} %dynamic-slice_bitcast_fusion.1), channel_id=1, source_target_pairs={{0,4},{4,0},{8,12},{12,8},{16,20},{20,16},{24,28},{28,24},{1,5},{5... | collective-permute-start | bytes 1966088 | tf_op jit(solution)/shard_map/ppermute | solution.py:972
  873.4 56.0 %collective-permute-start.84 = (bf16[2,2,256,768]{3,2,1,0:T(8,128)(2,1)}, bf16[2,2,256,768]{3,2,1,0:T(8,128)(2,1)}, u32[]{:S(2)}, u32[]{:S(2)}) collective-permute-start(bf16[2,2,256,768]{3,2,1,0:T(8,128)(2,1)} %bitcast.138), channel_id=1, source_target_pairs={{0,16},{4,20},{8,24},{12,28},{16,0},{20,4},{24,8},{28,12},{1,17},{... | collective-permute-start | bytes 4718600 | tf_op jit(solution)/shard_map/ppermute | solution.py:977
  874.2 59.4 %collective-permute-start.85 = (bf16[2,2,256,768]{3,2,1,0:T(8,128)(2,1)}, bf16[2,2,256,768]{3,2,1,0:T(8,128)(2,1)}, u32[]{:S(2)}, u32[]{:S(2)}) collective-permute-start(bf16[2,2,256,768]{3,2,1,0:T(8,128)(2,1)} %bitcast.140), channel_id=1, source_target_pairs={{0,8},{4,12},{8,0},{12,4},{16,24},{20,28},{24,16},{28,20},{1,9},{5... | collective-permute-start | bytes 4718600 | tf_op jit(solution)/shard_map/ppermute | solution.py:977
  898.4 57.1 %collective-permute-start.90 = (bf16[2,2,512,384]{3,2,1,0:T(8,128)(2,1)S(1)}, bf16[2,2,512,384]{3,2,1,0:T(8,128)(2,1)}, u32[]{:S(2)}, u32[]{:S(2)}) collective-permute-start(bf16[2,2,512,384]{3,2,1,0:T(8,128)(2,1)S(1)} %bitcast.561), channel_id=1, source_target_pairs={{0,8},{4,12},{8,0},{12,4},{16,24},{20,28},{24,16},{28,20},{1,9},{5... | collective-permute-start | bytes 4718600 | tf_op jit(solution)/shard_map/ppermute | solution.py:977
  901.1 57.0 %collective-permute-start.88 = (bf16[2,2,512,384]{3,2,1,0:T(8,128)(2,1)S(1)}, bf16[2,2,512,384]{3,2,1,0:T(8,128)(2,1)}, u32[]{:S(2)}, u32[]{:S(2)}) collective-permute-start(bf16[2,2,512,384]{3,2,1,0:T(8,128)(2,1)S(1)} %bitcast.560), channel_id=1, source_target_pairs={{0,16},{4,20},{8,24},{12,28},{16,0},{20,4},{24,8},{28,12},{1,17},{... | collective-permute-start | bytes 4718600 | tf_op jit(solution)/shard_map/ppermute | solution.py:977
  929.4 61.2 %collective-permute-start.74 = (bf16[320,1536]{1,0:T(8,128)(2,1)}, bf16[320,1536]{1,0:T(8,128)(2,1)}, u32[]{:S(2)}, u32[]{:S(2)}) collective-permute-start(bf16[320,1536]{1,0:T(8,128)(2,1)} %get-tuple-element.688), channel_id=1, source_target_pairs={{0,4},{4,0},{8,12},{12,8},{16,20},{20,16},{24,28},{28,24},{1,5},{5... | collective-permute-start | bytes 2949128 | tf_op jit(solution)/shard_map/ppermute | solution.py:972
  958.1 201.1 %collective-permute-start.86 = (bf16[2,2,384,1024]{3,2,1,0:T(8,128)(2,1)}, bf16[2,2,384,1024]{3,2,1,0:T(8,128)(2,1)}, u32[]{:S(2)}, u32[]{:S(2)}) collective-permute-start(bf16[2,2,384,1024]{3,2,1,0:T(8,128)(2,1)} %bitcast.142), channel_id=1, source_target_pairs={{0,16},{4,20},{8,24},{12,28},{16,0},{20,4},{24,8},{28,12},{1,17},{... | collective-permute-start | bytes 9437192 | tf_op jit(solution)/shard_map/ppermute | solution.py:977
  963.1 116.6 %collective-permute-start.91 = (bf16[1,2,512,384]{3,2,1,0:T(8,128)(2,1)}, bf16[1,2,512,384]{3,2,1,0:T(8,128)(2,1)}, u32[]{:S(2)}, u32[]{:S(2)}) collective-permute-start(bf16[1,2,512,384]{3,2,1,0:T(8,128)(2,1)} %slice.1219), channel_id=1, source_target_pairs={{0,16},{4,20},{8,24},{12,28},{16,0},{20,4},{24,8},{28,12},{1,17},{... | collective-permute-start | bytes 2359304 | tf_op jit(solution)/shard_map/ppermute | solution.py:977
  974.6 121.0 %collective-permute-start.89 = (bf16[1,2,512,384]{3,2,1,0:T(8,128)(2,1)}, bf16[1,2,512,384]{3,2,1,0:T(8,128)(2,1)}, u32[]{:S(2)}, u32[]{:S(2)}) collective-permute-start(bf16[1,2,512,384]{3,2,1,0:T(8,128)(2,1)} %slice.1220), channel_id=1, source_target_pairs={{0,8},{4,12},{8,0},{12,4},{16,24},{20,28},{24,16},{28,20},{1,9},{5... | collective-permute-start | bytes 2359304 | tf_op jit(solution)/shard_map/ppermute | solution.py:977
  977.1 220.9 %reduce-scatter.11.cloned.1.call-start = ((), (), s32[]{:S(2)}) async-start(), calls=%async_computation.9 | async-start | bytes 1966080 | tf_op jit(solution)/shard_map/reduce_scatter | solution.py:1326
  999.3 75.8 %collective-permute-start.98 = (bf16[2,2,192,640]{3,2,1,0:T(8,128)(2,1)}, bf16[2,2,192,640]{3,2,1,0:T(8,128)(2,1)}, u32[]{:S(2)}, u32[]{:S(2)}) collective-permute-start(bf16[2,2,192,640]{3,2,1,0:T(8,128)(2,1)} %bitcast.161), channel_id=1, source_target_pairs={{0,8},{4,12},{8,0},{12,4},{16,24},{20,28},{24,16},{28,20},{1,9},{5... | collective-permute-start | bytes 2949128 | tf_op jit(solution)/shard_map/ppermute | solution.py:977
  1016.6 60.6 %collective-permute-start.96 = (bf16[2,2,192,640]{3,2,1,0:T(8,128)(2,1)}, bf16[2,2,192,640]{3,2,1,0:T(8,128)(2,1)}, u32[]{:S(2)}, u32[]{:S(2)}) collective-permute-start(bf16[2,2,192,640]{3,2,1,0:T(8,128)(2,1)} %bitcast.158), channel_id=1, source_target_pairs={{0,16},{4,20},{8,24},{12,28},{16,0},{20,4},{24,8},{28,12},{1,17},{... | collective-permute-start | bytes 2949128 | tf_op jit(solution)/shard_map/ppermute | solution.py:977
  1075.2 64.5 %collective-permute-start.78 = (f32[1280,256]{1,0:T(8,128)}, f32[1280,256]{1,0:T(8,128)}, u32[]{:S(2)}, u32[]{:S(2)}) collective-permute-start(f32[1280,256]{1,0:T(8,128)} %copy-done.71), channel_id=1, source_target_pairs={{0,4},{4,0},{8,12},{12,8},{16,20},{20,16},{24,28},{28,24},{1,5},{5... | collective-permute-start | bytes 3932168 | tf_op jit(solution)/shard_map/ppermute | solution.py:972
  1099.6 125.3 %reduce-scatter.7.cloned.1.call-start = ((), (), s32[]{:S(2)}) async-start(), calls=%async_computation.6 | async-start | bytes 2654208 | tf_op jit(solution)/shard_map/reduce_scatter | solution.py:1539
  1101.8 67.2 %collective-permute-start.87 = (bf16[2,2,384,1024]{3,2,1,0:T(8,128)(2,1)}, bf16[2,2,384,1024]{3,2,1,0:T(8,128)(2,1)}, u32[]{:S(2)}, u32[]{:S(2)}) collective-permute-start(bf16[2,2,384,1024]{3,2,1,0:T(8,128)(2,1)} %bitcast.593), channel_id=1, source_target_pairs={{0,8},{4,12},{8,0},{12,4},{16,24},{20,28},{24,16},{28,20},{1,9},{5... | collective-permute-start | bytes 9437192 | tf_op jit(solution)/shard_map/ppermute | solution.py:977
  1152.0 51.1 %collective-permute-start.79 = (bf16[1280,1024]{1,0:T(8,128)(2,1)}, bf16[1280,1024]{1,0:T(8,128)(2,1)}, u32[]{:S(2)}, u32[]{:S(2)}) collective-permute-start(bf16[1280,1024]{1,0:T(8,128)(2,1)} %get-tuple-element.694), channel_id=1, source_target_pairs={{0,4},{4,0},{8,12},{12,8},{16,20},{20,16},{24,28},{28,24},{1,5},{5... | collective-permute-start | bytes 7864328 | tf_op jit(solution)/shard_map/ppermute | solution.py:972
  1157.2 287.0 %all-reduce.20.cloned.1.call-start = ((), (), s32[]{:S(2)}) async-start(), calls=%async_computation.4 | async-start | bytes 229376 | tf_op jit(solution)/shard_map/psum | solution.py:1792
  1179.3 41.5 %collective-permute-start.112 = (bf16[1,2,384,1024]{3,2,1,0:T(8,128)(2,1)}, bf16[1,2,384,1024]{3,2,1,0:T(8,128)(2,1)}, u32[]{:S(2)}, u32[]{:S(2)}) collective-permute-start(bf16[1,2,384,1024]{3,2,1,0:T(8,128)(2,1)} %slice.1213), channel_id=1, source_target_pairs={{0,16},{4,20},{8,24},{12,28},{16,0},{20,4},{24,8},{28,12},{1,17},{... | collective-permute-start | bytes 4718600 | tf_op jit(solution)/shard_map/ppermute | solution.py:977
  1179.4 45.6 %collective-permute-start.111 = (bf16[1,2,384,1024]{3,2,1,0:T(8,128)(2,1)}, bf16[1,2,384,1024]{3,2,1,0:T(8,128)(2,1)}, u32[]{:S(2)}, u32[]{:S(2)}) collective-permute-start(bf16[1,2,384,1024]{3,2,1,0:T(8,128)(2,1)} %slice.1214), channel_id=1, source_target_pairs={{0,8},{4,12},{8,0},{12,4},{16,24},{20,28},{24,16},{28,20},{1,9},{5... | collective-permute-start | bytes 4718600 | tf_op jit(solution)/shard_map/ppermute | solution.py:977
  1183.9 79.5 %collective-permute-start.92 = (bf16[2,2,384,640]{3,2,1,0:T(8,128)(2,1)}, bf16[2,2,384,640]{3,2,1,0:T(8,128)(2,1)}, u32[]{:S(2)}, u32[]{:S(2)}) collective-permute-start(bf16[2,2,384,640]{3,2,1,0:T(8,128)(2,1)} %bitcast.152), channel_id=1, source_target_pairs={{0,16},{4,20},{8,24},{12,28},{16,0},{20,4},{24,8},{28,12},{1,17},{... | collective-permute-start | bytes 5898248 | tf_op jit(solution)/shard_map/ppermute | solution.py:977
  1195.7 70.7 %collective-permute-start.93 = (bf16[2,2,384,640]{3,2,1,0:T(8,128)(2,1)}, bf16[2,2,384,640]{3,2,1,0:T(8,128)(2,1)}, u32[]{:S(2)}, u32[]{:S(2)}) collective-permute-start(bf16[2,2,384,640]{3,2,1,0:T(8,128)(2,1)} %bitcast.154), channel_id=1, source_target_pairs={{0,8},{4,12},{8,0},{12,4},{16,24},{20,28},{24,16},{28,20},{1,9},{5... | collective-permute-start | bytes 5898248 | tf_op jit(solution)/shard_map/ppermute | solution.py:977
  1214.2 230.0 %all-reduce.22.cloned.1.call-start = ((), (), s32[]{:S(2)}) async-start(), calls=%async_computation.7 | async-start | bytes 589824 | tf_op jit(solution)/shard_map/psum | solution.py:1539
  1224.9 289.3 %reduce-scatter.9.cloned.1.call-start = ((), (), s32[]{:S(2)}) async-start(), calls=%async_computation.8 | async-start | bytes 3932160 | tf_op jit(solution)/shard_map/reduce_scatter | solution.py:1326
  1233.8 53.4 %collective-permute-start.113 = (bf16[2,2,128,384]{3,2,1,0:T(8,128)(2,1)}, bf16[2,2,128,384]{3,2,1,0:T(8,128)(2,1)}, u32[]{:S(2)}, u32[]{:S(2)}) collective-permute-start(bf16[2,2,128,384]{3,2,1,0:T(8,128)(2,1)} %bitcast.202), channel_id=1, source_target_pairs={{0,16},{4,20},{8,24},{12,28},{16,0},{20,4},{24,8},{28,12},{1,17},{... | collective-permute-start | bytes 1179656 | tf_op jit(solution)/shard_map/ppermute | solution.py:977
  1235.1 68.3 %collective-permute-start.115 = (bf16[2,2,128,384]{3,2,1,0:T(8,128)(2,1)S(1)}, bf16[2,2,128,384]{3,2,1,0:T(8,128)(2,1)}, u32[]{:S(2)}, u32[]{:S(2)}) collective-permute-start(bf16[2,2,128,384]{3,2,1,0:T(8,128)(2,1)S(1)} %bitcast.564), channel_id=1, source_target_pairs={{0,8},{4,12},{8,0},{12,4},{16,24},{20,28},{24,16},{28,20},{1,9},{5... | collective-permute-start | bytes 1179656 | tf_op jit(solution)/shard_map/ppermute | solution.py:977
  1271.5 70.2 %collective-permute-start.123 = (bf16[1,2,384,640]{3,2,1,0:T(8,128)(2,1)}, bf16[1,2,384,640]{3,2,1,0:T(8,128)(2,1)}, u32[]{:S(2)}, u32[]{:S(2)}) collective-permute-start(bf16[1,2,384,640]{3,2,1,0:T(8,128)(2,1)} %slice.1218), channel_id=1, source_target_pairs={{0,8},{4,12},{8,0},{12,4},{16,24},{20,28},{24,16},{28,20},{1,9},{5... | collective-permute-start | bytes 2949128 | tf_op jit(solution)/shard_map/ppermute | solution.py:977
  1272.6 77.9 %collective-permute-start.124 = (bf16[1,2,384,640]{3,2,1,0:T(8,128)(2,1)}, bf16[1,2,384,640]{3,2,1,0:T(8,128)(2,1)}, u32[]{:S(2)}, u32[]{:S(2)}) collective-permute-start(bf16[1,2,384,640]{3,2,1,0:T(8,128)(2,1)} %slice.1217), channel_id=1, source_target_pairs={{0,16},{4,20},{8,24},{12,28},{16,0},{20,4},{24,8},{28,12},{1,17},{... | collective-permute-start | bytes 2949128 | tf_op jit(solution)/shard_map/ppermute | solution.py:977
  1321.5 88.6 %collective-permute-start.102 = (bf16[2,2,256,1024]{3,2,1,0:T(8,128)(2,1)S(1)}, bf16[2,2,256,1024]{3,2,1,0:T(8,128)(2,1)S(1)}, u32[]{:S(2)}, u32[]{:S(2)}) collective-permute-start(bf16[2,2,256,1024]{3,2,1,0:T(8,128)(2,1)S(1)} %bitcast.552), channel_id=1, source_target_pairs={{0,8},{4,12},{8,0},{12,4},{16,24},{20,28},{24,16},{28,20},{1,9},{5... | collective-permute-start | bytes 6291464 | tf_op jit(solution)/shard_map/ppermute | solution.py:977
  1339.2 73.7 %collective-permute-start.100 = (bf16[2,2,256,1024]{3,2,1,0:T(8,128)(2,1)S(1)}, bf16[2,2,256,1024]{3,2,1,0:T(8,128)(2,1)S(1)}, u32[]{:S(2)}, u32[]{:S(2)}) collective-permute-start(bf16[2,2,256,1024]{3,2,1,0:T(8,128)(2,1)S(1)} %bitcast.553), channel_id=1, source_target_pairs={{0,16},{4,20},{8,24},{12,28},{16,0},{20,4},{24,8},{28,12},{1,17},{... | collective-permute-start | bytes 6291464 | tf_op jit(solution)/shard_map/ppermute | solution.py:977
  1358.9 48.7 %collective-permute-start.126 = (bf16[384,640]{1,0:T(8,128)(2,1)S(1)}, bf16[384,640]{1,0:T(8,128)(2,1)S(1)}, u32[]{:S(2)}, u32[]{:S(2)}) collective-permute-start(bf16[384,640]{1,0:T(8,128)(2,1)S(1)} %get-tuple-element.364), channel_id=1, source_target_pairs={{0,2},{1,3},{2,0},{3,1},{4,6},{5,7},{6,4},{7,5},{8,10},{9,11},{10,... | collective-permute-start | bytes 1474568 | tf_op jit(solution)/shard_map/ppermute | solution.py:984
  1359.7 47.9 %collective-permute-start.125 = (bf16[384,640]{1,0:T(8,128)(2,1)S(1)}, bf16[384,640]{1,0:T(8,128)(2,1)S(1)}, u32[]{:S(2)}, u32[]{:S(2)}) collective-permute-start(bf16[384,640]{1,0:T(8,128)(2,1)S(1)} %get-tuple-element.363), channel_id=1, source_target_pairs={{0,1},{1,0},{2,3},{3,2},{4,5},{5,4},{6,7},{7,6},{8,9},{9,8},{10,11... | collective-permute-start | bytes 1474568 | tf_op jit(solution)/shard_map/ppermute | solution.py:984
  1442.6 67.1 %collective-permute-start.105 = (bf16[256,1024]{1,0:T(8,128)(2,1)}, bf16[256,1024]{1,0:T(8,128)(2,1)}, u32[]{:S(2)}, u32[]{:S(2)}) collective-permute-start(bf16[256,1024]{1,0:T(8,128)(2,1)} %get-tuple-element.362), channel_id=1, source_target_pairs={{0,2},{1,3},{2,0},{3,1},{4,6},{5,7},{6,4},{7,5},{8,10},{9,11},{10,... | collective-permute-start | bytes 1572872 | tf_op jit(solution)/shard_map/ppermute | solution.py:984
  1442.6 67.1 %collective-permute-start.104 = (bf16[256,1024]{1,0:T(8,128)(2,1)S(1)}, bf16[256,1024]{1,0:T(8,128)(2,1)}, u32[]{:S(2)}, u32[]{:S(2)}) collective-permute-start(bf16[256,1024]{1,0:T(8,128)(2,1)S(1)} %get-tuple-element.361), channel_id=1, source_target_pairs={{0,1},{1,0},{2,3},{3,2},{4,5},{5,4},{6,7},{7,6},{8,9},{9,8},{10,11... | collective-permute-start | bytes 1572872 | tf_op jit(solution)/shard_map/ppermute | solution.py:984
  (402 other events, 5434.1 us)
Sparse Core Ops, SparseCore 0:
  28.6 30.8 all-gather.13
  97.4 35.5 all-gather.15
  141.7 43.6 all-gather.17
  279.5 62.7 all-gather.19
  354.5 37.9 all-gather.21
  464.3 41.6 all-gather.23
  977.2 34.6 reduce-scatter.4
  1099.7 40.5 reduce-scatter.10
  1157.3 47.4 reduce-scatter.6
  1214.3 130.8 all-reduce.19
  1347.7 55.2 all-reduce.21
  1405.3 78.7 reduce-scatter.8

commit v3 on v2

--- a/solution.py
+++ b/solution.py
@@ -1757,6 +1757,7 @@
     (grad_dots,) = prob_back(grad_probs)
     grad_qk = pair_dots_back(qk, grad_dots, place.depths)
     partial = right_product(grad_qk, w_router)
+    (own_router,) = scatter.own([("columns", shared, grad_qk)], [d_rows], [partial])
     grad_shared = grad_shared + core_sum(partial)
     gradient = gradient + grad_shared
 
@@ -1768,7 +1769,7 @@
         items,
         enc_memory,
         scatter,
-        [("columns", shared, grad_qk)],
+        [],
         False,
     )
     grad_inputs = back_to_all(place, to_low(gradient), micro).astype(wide)
@@ -1820,7 +1821,7 @@
         smalls[5],
         smalls[6],
         join_rows(place, jnp.stack([enc_grads[1], dec_grads[1]])),
-        kinds(enc_grads[2], 2),
+        kinds(own_router, 2),
         own_up,
         own_down,
         jnp.stack([summed[14], summed[15]]),

time: 1540 us -> 1560 us (1.013)
    ppermute x59 -> x63, waiting for transfers between devices: 202 us -> 238 us  [chip_swap(): return lax.ppermute(values, 'dp', [(d, d ^ bit * 2) for d in range(size)])]
    ppermute x27 -> x30, waiting for transfers between devices: 189 us -> 155 us  [depth_swap(): return lax.ppermute(values, 'mp', [(d, d ^ offset) for d in range(size)])]
    unnamed x655 -> x657, local copies, waits for them, and re-layouts: 61.6 us -> 72 us
    pallas_call x28 -> x32, Pallas kernels: 106 us -> 109 us  [blocks(): pl.pallas_call(functools.partial(products_kernel, [kind for kind, _, _ in...]
    ppermute x27 -> x30, starting transfers between devices: 33 us -> 35 us  [depth_swap(): return lax.ppermute(values, 'mp', [(d, d ^ offset) for d in range(size)])]
    ppermute x59 -> x63, starting transfers between devices: 48.8 us -> 47.5 us  [chip_swap(): return lax.ppermute(values, 'dp', [(d, d ^ bit * 2) for d in range(size)])]
    convert_element_type x19 -> x20, other arithmetic: 49.1 us -> 49.4 us  [to_low(): return values.astype(jnp.bfloat16)]
  transfers between devices with their start and end apart: 144 -> 151, of which waited for: 41 -> 42; matrix products, arithmetic and copies ran while one was open for 32% -> 31% of each run, Pallas kernels for 19% -> 19%
where the time goes in v3:
time: 1560 us; the launch traced here: 1540 us
  waiting for transfers between devices  442 us (28%)
  Pallas kernels  338 us (22%)
  local copies, waits for them, and re-layouts  228 us (15%)
  other arithmetic  215 us (14%)
  starting transfers between devices  148 us (9%)
  matrix products  132 us (8%)
  between operations  19.9 us (1%)
  blocking collectives  19.1 us (1%)
    ppermute x63, waiting for transfers between devices, chip_swap(): return lax.ppermute(values, 'dp', [(d, d ^ bit * 2) for d in range(size)])  238 us
    ppermute x30, waiting for transfers between devices, depth_swap(): return lax.ppermute(values, 'mp', [(d, d ^ offset) for d in range(size)])  155 us
    pallas_call x32, Pallas kernels, blocks(): pl.pallas_call(functools.partial(products_kernel, [kind for kind, _, _ in...  109 us
    pallas_call x2, Pallas kernels, mix_backward(): pl.pallas_call(functools.partial(mix_back_kernel, per_block), grid=(chunk...  84.6 us
    unnamed x657, local copies, waits for them, and re-layouts  72 us
    dot_general x14, matrix products, matmul(): return jnp.dot(left, right, preferred_element_type=jnp.float32)  69.7 us
    ppermute x46, starting transfers between devices, core_swap(): return lax.ppermute(values, 'dp', [(d, d ^ 1) for d in range(size)])  64.7 us
    dot_general x13, matrix products, right_product(): lax.dot_general(left, right, (((1,), (1,)), ((), ())), preferred_element_...  58.4 us
  transfers between devices with their start and end apart: 151, of which 42 were waited for; matrix products, arithmetic and copies ran while one was open for 31% of the time, Pallas kernels for 19%

profile of v3, /device:TPU:1, one launch (start us, length us, event | category | flops | bytes accessed | tf_op | source)
XLA Modules:
  0.0 1543.0 jit_solution(2918520600662535659)
XLA Ops:
  60.9 5.7 collective-permute-done.14
  66.6 20.5 %collective-permute-done.13 = bf16[640,256]{1,0:T(8,128)(2,1)} collective-permute-done((bf16[640,256]{1,0:T(8,128)(2,1)}, bf16[640,256]{1,0:T(8,128)(2,1)}, u32[]{:S(2)}, u32[]{:S(2)}) %collective-permute-start.13) | collective-permute-done | bytes 327712 | tf_op jit(solution)/shard_map/ppermute | solution.py:984
  113.7 18.7 %all-gather.16.cloned.1.call-done = bf16[1024,768]{1,0:T(8,128)(2,1)} async-done(((bf16[256,768]{1,0:T(8,128)(2,1)}), bf16[1024,768]{1,0:T(8,128)(2,1)}) %all-gather.16.cloned.1.call-update) | async-done | bytes 1572880 | tf_op jit(solution)/shard_map/all_gather | solution.py:1160
  144.5 34.0 %collective-permute-done.18.refs_3_ = bf16[2,256,512]{2,1,0:T(8,128)(2,1)S(1)} collective-permute-done((bf16[2,256,512]{2,1,0:T(8,128)(2,1)}, bf16[2,256,512]{2,1,0:T(8,128)(2,1)S(1)}, u32[]{:S(2)}, u32[]{:S(2)}) %collective-permute-start.18) | collective-permute-done | bytes 524320 | tf_op jit(solution)/shard_map/ppermute | solution.py:977
  186.6 10.4 fusion.310.zx_ref.zx_tail_ref
  197.1 20.2 %shard_map.400 = (bf16[1280,1024]{1,0:T(8,128)(2,1)S(1)}, f32[1280,1024]{1,0:T(8,128)}, f32[1280,1]{1,0:T(8,128)S(1)}, bf16[1280,1024]{1,0:T(8,128)(2,1)}) custom-call(f32[1280,2048]{1,0:T(8,128)} %fusion.310.zx_ref.zx_tail_ref, f32[1280,384]{1,0:T(8,128)S(1)} %fusion.265.bcdt_ref.maps_tail_ref, f32[1280,8]{1,0:T(8,128)S(1)} %stack.195.columns_ref, ...), custom_call_target="tpu_custom_call" | custom-call | flops 1342177280 | bytes 20971520 | tf_op jit(solution)/shard_map/pallas_call | solution.py:401
  217.3 5.6 shard_map.401
  223.0 7.1 fusion.299
  245.2 19.1 %all-gather.3 = bf16[768,640]{1,0:T(8,128)(2,1)} all-gather(bf16[192,640]{1,0:T(8,128)(2,1)S(1)} %copy-done.190), channel_id=5, replica_groups=mesh['dp'=8,'mp'=4] {'mp'}, dimensions={0}, use_global_device_ids=true | all-gather | bytes 1228800 | tf_op jit(solution)/shard_map/all_gather | solution.py:1160
  265.8 12.0 collective-permute-done.34.refs_1_
  279.2 6.4 fusion.273
  327.5 14.0 collective-permute-done.41.refs_4_
  347.7 5.9 shard_map.403
  366.4 26.8 %all-gather.22.cloned.1.call-done = bf16[2048,384]{0,1:T(8,128)(2,1)} async-done(((bf16[512,384]{0,1:T(8,128)(2,1)}), bf16[2048,384]{0,1:T(8,128)(2,1)}) %all-gather.22.cloned.1.call-update) | async-done | bytes 1572880 | tf_op jit(solution)/shard_map/all_gather | solution.py:1160
  399.5 9.0 shard_map.404.refs_1_
  413.0 8.3 collective-permute-done.43.refs_1_
  421.3 5.7 collective-permute-start.53
  436.4 18.7 %collective-permute-done.47.refs_1_ = bf16[4,512,384]{2,1,0:T(8,128)(2,1)} collective-permute-done((bf16[4,512,384]{2,1,0:T(8,128)(2,1)S(1)}, bf16[4,512,384]{2,1,0:T(8,128)(2,1)}, u32[]{:S(2)}, u32[]{:S(2)}) %collective-permute-start.47) | collective-permute-done | bytes 1572896 | tf_op jit(solution)/shard_map/ppermute | solution.py:977
  464.8 24.7 %collective-permute-done.45.refs_3_ = bf16[2,384,1024]{2,1,0:T(8,128)(2,1)} collective-permute-done((bf16[2,384,1024]{2,1,0:T(8,128)(2,1)}, bf16[2,384,1024]{2,1,0:T(8,128)(2,1)}, u32[]{:S(2)}, u32[]{:S(2)}) %collective-permute-start.45) | collective-permute-done | bytes 1572896 | tf_op jit(solution)/shard_map/ppermute | solution.py:977
  489.5 9.7 shard_map.406
  499.3 7.1 collective-permute-done.49.refs_3_
  506.4 5.6 shard_map.408
  512.0 10.5 fusion.313.pair_ref
  572.2 12.9 shard_map.409
  585.2 10.5 collective-permute-done.66
  606.2 10.4 collective-permute-done.56.refs_3_
  623.9 10.2 fusion.314.zx_ref.zx_tail_ref
  634.2 20.3 %shard_map.411 = (bf16[1280,1024]{1,0:T(8,128)(2,1)S(1)}, f32[1280,1024]{1,0:T(8,128)}, f32[1280,1]{1,0:T(8,128)S(1)}, bf16[1280,1024]{1,0:T(8,128)(2,1)}) custom-call(f32[1280,2048]{1,0:T(8,128)} %fusion.314.zx_ref.zx_tail_ref, f32[1280,384]{1,0:T(8,128)S(1)} %fusion.263.bcdt_ref.maps_tail_ref, f32[1280,8]{1,0:T(8,128)S(1)} %stack.195.columns_ref, ...), custom_call_target="tpu_custom_call" | custom-call | flops 1342177280 | bytes 20971520 | tf_op jit(solution)/shard_map/pallas_call | solution.py:401
  664.6 8.3 fusion.305
  692.7 42.0 %shard_map.412 = (bf16[1280,2048]{1,0:T(8,128)(2,1)}, f32[1280,256]{1,0:T(8,128)}, f32[1280,128]{1,0:T(8,128)S(1)}, f32[32,1024]{1,0:T(8,128)S(1)}, f32[32,256]{...) custom-call(f32[1280,1024]{1,0:T(8,128)} %get-tuple-element.686.grad_ref, ...), custom_call_target="tpu_custom_call" | custom-call | flops 4026531840 | bytes 20971520 | tf_op jit(solution)/shard_map/pallas_call | solution.py:461
  753.1 8.3 fusion.304
  776.5 5.3 fusion.7
  781.8 9.6 fusion.8
  791.4 5.9 shard_map.424
  798.4 6.7 shard_map.425
  805.2 6.9 shard_map.423
  817.7 12.9 shard_map.413
  839.2 7.8 shard_map.416.refs_1_
  847.1 5.2 fusion.308
  865.6 9.1 fusion.306
  877.6 6.0 shard_map.422
  910.7 12.2 shard_map.415.refs_1_
  922.9 8.2 fusion.307
  966.9 9.4 collective-permute-done.87
  1006.8 7.2 multiply_convert_fusion
  1029.2 42.6 %shard_map.417 = (bf16[1280,2048]{1,0:T(8,128)(2,1)}, f32[1280,256]{1,0:T(8,128)S(1)}, f32[1280,128]{1,0:T(8,128)S(1)}, f32[32,1024]{1,0:T(8,128)S(1)}, f32[32,2...) custom-call(f32[1280,1024]{1,0:T(8,128)} %get-tuple-element.698.grad_ref, ...), custom_call_target="tpu_custom_call" | custom-call | flops 4026531840 | bytes 20971520 | tf_op jit(solution)/shard_map/pallas_call | solution.py:461
  1089.3 8.0 collective-permute-done.115
  1109.7 24.4 %collective-permute-done.130 = bf16[192,640]{1,0:T(8,128)(2,1)S(1)} collective-permute-done((bf16[192,640]{1,0:T(8,128)(2,1)S(1)}, bf16[192,640]{1,0:T(8,128)(2,1)S(1)}, u32[]{:S(2)}, u32[]{:S(2)}) %collective-permute-start.130) | collective-permute-done | bytes 245792 | tf_op jit(solution)/shard_map/ppermute | solution.py:984
  1136.0 10.5 collective-permute-start.136
  1150.8 8.2 fusion.309
  1212.9 5.2 fusion.5
  1245.6 26.2 %collective-permute-done.96 = bf16[2,2,128,384]{3,2,1,0:T(8,128)(2,1)} collective-permute-done((bf16[2,2,128,384]{3,2,1,0:T(8,128)(2,1)}, bf16[2,2,128,384]{3,2,1,0:T(8,128)(2,1)}, u32[]{:S(2)}, u32[]{:S(2)}) %collective-permute-start.96) | collective-permute-done | bytes 393248 | tf_op jit(solution)/shard_map/ppermute | solution.py:977
  1291.3 6.1 fusion.16
  1297.5 7.4 collective-permute-done.125
  1310.9 13.3 collective-permute-done.127
  1332.6 10.2 collective-permute-done.81
  1345.3 26.9 %collective-permute-done.117 = bf16[1,2,256,256]{3,2,1,0:T(8,128)(2,1)S(1)} collective-permute-done((bf16[1,2,256,256]{3,2,1,0:T(8,128)(2,1)S(1)}, bf16[1,2,256,256]{3,2,1,0:T(8,128)(2,1)S(1)}, u32[]{:S(2)}, u32[]{:S(2)}) %collective-permute-start.117) | collective-permute-done | bytes 262176 | tf_op jit(solution)/shard_map/ppermute | solution.py:977
  1396.8 5.9 shard_map.444
  1402.7 6.2 shard_map.445
  1408.9 5.9 shard_map.442
  1414.8 6.0 shard_map.443
  1423.9 29.9 %collective-permute-done.133 = bf16[384,640]{1,0:T(8,128)(2,1)} collective-permute-done((bf16[384,640]{1,0:T(8,128)(2,1)}, bf16[384,640]{1,0:T(8,128)(2,1)}, u32[]{:S(2)}, u32[]{:S(2)}) %collective-permute-start.133) | collective-permute-done | bytes 491552 | tf_op jit(solution)/shard_map/ppermute | solution.py:984
  1463.4 16.8 %collective-permute-done.107 = bf16[1,2,256,768]{3,2,1,0:T(8,128)(2,1)S(1)} collective-permute-done((bf16[1,2,256,768]{3,2,1,0:T(8,128)(2,1)S(1)}, bf16[1,2,256,768]{3,2,1,0:T(8,128)(2,1)S(1)}, u32[]{:S(2)}, u32[]{:S(2)}) %collective-permute-start.107) | collective-permute-done | bytes 786464 | tf_op jit(solution)/shard_map/ppermute | solution.py:977
  1498.5 27.6 %collective-permute-done.109 = bf16[256,768]{1,0:T(8,128)(2,1)} collective-permute-done((bf16[256,768]{1,0:T(8,128)(2,1)}, bf16[256,768]{1,0:T(8,128)(2,1)}, u32[]{:S(2)}, u32[]{:S(2)}) %collective-permute-start.109) | collective-permute-done | bytes 393248 | tf_op jit(solution)/shard_map/ppermute | solution.py:984
  (1485 shorter events, 695.1 us)
Async XLA Ops:
  7.2 89.4 %all-gather.14.cloned.1.call-start = ((), (), s32[]{:S(2)}) async-start(), calls=%async_computation.10 | async-start | bytes 1310720 | tf_op jit(solution)/shard_map/all_gather | solution.py:1160
  13.0 39.0 %collective-permute-start.11 = (bf16[2,1,640,256]{3,2,1,0:T(8,128)(2,1)}, bf16[2,1,640,256]{3,2,1,0:T(8,128)(2,1)}, u32[]{:S(2)}, u32[]{:S(2)}) collective-permute-start(bf16[2,1,640,256]{3,2,1,0:T(8,128)(2,1)} %constant_dynamic-slice_fusion.103), channel_id=1, source_target_pairs={{0,4},{4,0},{8,12},{12,8},{16,20},{20,16},{24,28},{28,24},{1,5},{5... | collective-permute-start | bytes 1966088 | tf_op jit(solution)/shard_map/ppermute | solution.py:972
  28.5 103.9 %all-gather.16.cloned.1.call-start = ((), (), s32[]{:S(2)}) async-start(), calls=%async_computation.11 | async-start | bytes 1966080 | tf_op jit(solution)/shard_map/all_gather | solution.py:1160
  49.0 39.7 %collective-permute-start.7 = (bf16[2,256,384]{2,1,0:T(8,128)(2,1)S(1)}, bf16[2,256,384]{2,1,0:T(8,128)(2,1)}, u32[]{:S(2)}, u32[]{:S(2)}) collective-permute-start(bf16[2,256,384]{2,1,0:T(8,128)(2,1)S(1)} %concatenate.400), channel_id=1, source_target_pairs={{0,16},{4,20},{8,24},{12,28},{16,0},{20,4},{24,8},{28,12},{1,17},{... | collective-permute-start | bytes 1179656 | tf_op jit(solution)/shard_map/ppermute | solution.py:977
  93.2 40.9 %collective-permute-start.15 = (bf16[640,1024]{1,0:T(8,128)(2,1)}, bf16[640,1024]{1,0:T(8,128)(2,1)}, u32[]{:S(2)}, u32[]{:S(2)}) collective-permute-start(bf16[640,1024]{1,0:T(8,128)(2,1)} %pad_maximum_fusion.12), channel_id=1, source_target_pairs={{0,4},{4,0},{8,12},{12,8},{16,20},{20,16},{24,28},{28,24},{1,5},{5... | collective-permute-start | bytes 3932168 | tf_op jit(solution)/shard_map/ppermute | solution.py:972
  96.7 136.4 %all-gather.18.cloned.1.call-start = ((), (), s32[]{:S(2)}) async-start(), calls=%async_computation.12 | async-start | bytes 2457600 | tf_op jit(solution)/shard_map/all_gather | solution.py:1160
  132.4 50.5 %collective-permute-start.26 = (bf16[4,256,768]{2,1,0:T(8,128)(2,1)}, bf16[4,256,768]{2,1,0:T(8,128)(2,1)}, u32[]{:S(2)}, u32[]{:S(2)}) collective-permute-start(bf16[4,256,768]{2,1,0:T(8,128)(2,1)} %bitcast.583), channel_id=1, source_target_pairs={{0,8},{4,12},{8,0},{12,4},{16,24},{20,28},{24,16},{28,20},{1,9},{5... | collective-permute-start | bytes 4718600 | tf_op jit(solution)/shard_map/ppermute | solution.py:977
  132.8 52.0 %collective-permute-start.27 = (bf16[4,256,768]{2,1,0:T(8,128)(2,1)}, bf16[4,256,768]{2,1,0:T(8,128)(2,1)}, u32[]{:S(2)}, u32[]{:S(2)}) collective-permute-start(bf16[4,256,768]{2,1,0:T(8,128)(2,1)} %bitcast.584), channel_id=1, source_target_pairs={{0,16},{4,20},{8,24},{12,28},{16,0},{20,4},{24,8},{28,12},{1,17},{... | collective-permute-start | bytes 4718600 | tf_op jit(solution)/shard_map/ppermute | solution.py:977
  137.9 40.6 %collective-permute-start.18 = (bf16[2,256,512]{2,1,0:T(8,128)(2,1)}, bf16[2,256,512]{2,1,0:T(8,128)(2,1)S(1)}, u32[]{:S(2)}, u32[]{:S(2)}) collective-permute-start(bf16[2,256,512]{2,1,0:T(8,128)(2,1)} %slice.903), channel_id=1, source_target_pairs={{0,16},{4,20},{8,24},{12,28},{16,0},{20,4},{24,8},{28,12},{1,17},{... | collective-permute-start | bytes 1572872 | tf_op jit(solution)/shard_map/ppermute | solution.py:977
  139.1 40.1 %collective-permute-start.19 = (bf16[2,256,512]{2,1,0:T(8,128)(2,1)}, bf16[2,256,512]{2,1,0:T(8,128)(2,1)}, u32[]{:S(2)}, u32[]{:S(2)}) collective-permute-start(bf16[2,256,512]{2,1,0:T(8,128)(2,1)} %slice.904), channel_id=1, source_target_pairs={{0,8},{4,12},{8,0},{12,4},{16,24},{20,28},{24,16},{28,20},{1,9},{5... | collective-permute-start | bytes 1572872 | tf_op jit(solution)/shard_map/ppermute | solution.py:977
  140.1 213.5 %all-gather.20.cloned.1.call-start = ((), (), s32[]{:S(2)}) async-start(), calls=%async_computation.13 | async-start | bytes 3932160 | tf_op jit(solution)/shard_map/all_gather | solution.py:1160
  230.1 49.1 %collective-permute-start.30 = (bf16[1280,1024]{1,0:T(8,128)(2,1)}, bf16[1280,1024]{1,0:T(8,128)(2,1)}, u32[]{:S(2)}, u32[]{:S(2)}) collective-permute-start(bf16[1280,1024]{1,0:T(8,128)(2,1)} %get-tuple-element.675), channel_id=1, source_target_pairs={{0,4},{4,0},{8,12},{12,8},{16,20},{20,16},{24,28},{28,24},{1,5},{5... | collective-permute-start | bytes 7864328 | tf_op jit(solution)/shard_map/ppermute | solution.py:972
  233.1 44.8 %collective-permute-start.34 = (bf16[4,384,640]{2,1,0:T(8,128)(2,1)}, bf16[4,384,640]{2,1,0:T(8,128)(2,1)S(1)}, u32[]{:S(2)}, u32[]{:S(2)}) collective-permute-start(bf16[4,384,640]{2,1,0:T(8,128)(2,1)} %bitcast.578), channel_id=1, source_target_pairs={{0,8},{4,12},{8,0},{12,4},{16,24},{20,28},{24,16},{28,20},{1,9},{5... | collective-permute-start | bytes 5898248 | tf_op jit(solution)/shard_map/ppermute | solution.py:977
  234.3 44.4 %collective-permute-start.35 = (bf16[4,384,640]{2,1,0:T(8,128)(2,1)}, bf16[4,384,640]{2,1,0:T(8,128)(2,1)}, u32[]{:S(2)}, u32[]{:S(2)}) collective-permute-start(bf16[4,384,640]{2,1,0:T(8,128)(2,1)} %bitcast.579), channel_id=1, source_target_pairs={{0,16},{4,20},{8,24},{12,28},{16,0},{20,4},{24,8},{28,12},{1,17},{... | collective-permute-start | bytes 5898248 | tf_op jit(solution)/shard_map/ppermute | solution.py:977
  278.7 114.4 %all-gather.22.cloned.1.call-start = ((), (), s32[]{:S(2)}) async-start(), calls=%async_computation.14 | async-start | bytes 1966080 | tf_op jit(solution)/shard_map/all_gather | solution.py:1160
  306.0 41.7 %collective-permute-start.36 = (bf16[2,384,640]{2,1,0:T(8,128)(2,1)}, bf16[2,384,640]{2,1,0:T(8,128)(2,1)}, u32[]{:S(2)}, u32[]{:S(2)}) collective-permute-start(bf16[2,384,640]{2,1,0:T(8,128)(2,1)} %slice.920), channel_id=1, source_target_pairs={{0,16},{4,20},{8,24},{12,28},{16,0},{20,4},{24,8},{28,12},{1,17},{... | collective-permute-start | bytes 2949128 | tf_op jit(solution)/shard_map/ppermute | solution.py:977
  308.7 39.0 %collective-permute-start.37 = (bf16[2,384,640]{2,1,0:T(8,128)(2,1)}, bf16[2,384,640]{2,1,0:T(8,128)(2,1)}, u32[]{:S(2)}, u32[]{:S(2)}) collective-permute-start(bf16[2,384,640]{2,1,0:T(8,128)(2,1)} %slice.921), channel_id=1, source_target_pairs={{0,8},{4,12},{8,0},{12,4},{16,24},{20,28},{24,16},{28,20},{1,9},{5... | collective-permute-start | bytes 2949128 | tf_op jit(solution)/shard_map/ppermute | solution.py:977
  353.6 67.8 %collective-permute-start.43 = (bf16[4,384,1024]{2,1,0:T(8,128)(2,1)}, bf16[4,384,1024]{2,1,0:T(8,128)(2,1)}, u32[]{:S(2)}, u32[]{:S(2)}) collective-permute-start(bf16[4,384,1024]{2,1,0:T(8,128)(2,1)} %bitcast.618), channel_id=1, source_target_pairs={{0,8},{4,12},{8,0},{12,4},{16,24},{20,28},{24,16},{28,20},{1,9},{5... | collective-permute-start | bytes 9437192 | tf_op jit(solution)/shard_map/ppermute | solution.py:977
  354.7 76.0 %collective-permute-start.44 = (bf16[4,384,1024]{2,1,0:T(8,128)(2,1)}, bf16[4,384,1024]{2,1,0:T(8,128)(2,1)}, u32[]{:S(2)}, u32[]{:S(2)}) collective-permute-start(bf16[4,384,1024]{2,1,0:T(8,128)(2,1)} %bitcast.619), channel_id=1, source_target_pairs={{0,16},{4,20},{8,24},{12,28},{16,0},{20,4},{24,8},{28,12},{1,17},{... | collective-permute-start | bytes 9437192 | tf_op jit(solution)/shard_map/ppermute | solution.py:977
  355.0 193.7 %all-gather.24.cloned.1.call-start = ((), (), s32[]{:S(2)}) async-start(), calls=%async_computation.15 | async-start | bytes 1966080 | tf_op jit(solution)/shard_map/all_gather | solution.py:1160
  395.0 60.0 %collective-permute-start.47 = (bf16[4,512,384]{2,1,0:T(8,128)(2,1)S(1)}, bf16[4,512,384]{2,1,0:T(8,128)(2,1)}, u32[]{:S(2)}, u32[]{:S(2)}) collective-permute-start(bf16[4,512,384]{2,1,0:T(8,128)(2,1)S(1)} %bitcast.564), channel_id=1, source_target_pairs={{0,8},{4,12},{8,0},{12,4},{16,24},{20,28},{24,16},{28,20},{1,9},{5... | collective-permute-start | bytes 4718600 | tf_op jit(solution)/shard_map/ppermute | solution.py:977
  396.3 61.8 %collective-permute-start.48 = (bf16[4,512,384]{2,1,0:T(8,128)(2,1)S(1)}, bf16[4,512,384]{2,1,0:T(8,128)(2,1)}, u32[]{:S(2)}, u32[]{:S(2)}) collective-permute-start(bf16[4,512,384]{2,1,0:T(8,128)(2,1)S(1)} %bitcast.565), channel_id=1, source_target_pairs={{0,16},{4,20},{8,24},{12,28},{16,0},{20,4},{24,8},{28,12},{1,17},{... | collective-permute-start | bytes 4718600 | tf_op jit(solution)/shard_map/ppermute | solution.py:977
  411.4 49.1 %collective-permute-start.42 = (bf16[320,1536]{1,0:T(8,128)(2,1)}, bf16[320,1536]{1,0:T(8,128)(2,1)}, u32[]{:S(2)}, u32[]{:S(2)}) collective-permute-start(bf16[320,1536]{1,0:T(8,128)(2,1)} %get-tuple-element.679), channel_id=1, source_target_pairs={{0,4},{4,0},{8,12},{12,8},{16,20},{20,16},{24,28},{28,24},{1,5},{5... | collective-permute-start | bytes 2949128 | tf_op jit(solution)/shard_map/ppermute | solution.py:972
  430.7 58.8 %collective-permute-start.45 = (bf16[2,384,1024]{2,1,0:T(8,128)(2,1)}, bf16[2,384,1024]{2,1,0:T(8,128)(2,1)}, u32[]{:S(2)}, u32[]{:S(2)}) collective-permute-start(bf16[2,384,1024]{2,1,0:T(8,128)(2,1)} %slice.925), channel_id=1, source_target_pairs={{0,16},{4,20},{8,24},{12,28},{16,0},{20,4},{24,8},{28,12},{1,17},{... | collective-permute-start | bytes 4718600 | tf_op jit(solution)/shard_map/ppermute | solution.py:977
  434.4 55.1 %collective-permute-start.46 = (bf16[2,384,1024]{2,1,0:T(8,128)(2,1)}, bf16[2,384,1024]{2,1,0:T(8,128)(2,1)}, u32[]{:S(2)}, u32[]{:S(2)}) collective-permute-start(bf16[2,384,1024]{2,1,0:T(8,128)(2,1)} %slice.926), channel_id=1, source_target_pairs={{0,8},{4,12},{8,0},{12,4},{16,24},{20,28},{24,16},{28,20},{1,9},{5... | collective-permute-start | bytes 4718600 | tf_op jit(solution)/shard_map/ppermute | solution.py:977
  457.1 49.3 %collective-permute-start.49 = (bf16[2,512,384]{2,1,0:T(8,128)(2,1)}, bf16[2,512,384]{2,1,0:T(8,128)(2,1)}, u32[]{:S(2)}, u32[]{:S(2)}) collective-permute-start(bf16[2,512,384]{2,1,0:T(8,128)(2,1)} %slice.927), channel_id=1, source_target_pairs={{0,16},{4,20},{8,24},{12,28},{16,0},{20,4},{24,8},{28,12},{1,17},{... | collective-permute-start | bytes 2359304 | tf_op jit(solution)/shard_map/ppermute | solution.py:977
  460.1 46.3 %collective-permute-start.50 = (bf16[2,512,384]{2,1,0:T(8,128)(2,1)}, bf16[2,512,384]{2,1,0:T(8,128)(2,1)}, u32[]{:S(2)}, u32[]{:S(2)}) collective-permute-start(bf16[2,512,384]{2,1,0:T(8,128)(2,1)} %slice.928), channel_id=1, source_target_pairs={{0,8},{4,12},{8,0},{12,4},{16,24},{20,28},{24,16},{28,20},{1,9},{5... | collective-permute-start | bytes 2359304 | tf_op jit(solution)/shard_map/ppermute | solution.py:977
  464.8 710.3 %reduce-scatter.5.cloned.1.call-start = ((), (), s32[]{:S(2)}) async-start(), calls=%async_computation.5 | async-start | bytes 1966080 | tf_op jit(solution)/shard_map/reduce_scatter | solution.py:1326
  674.7 107.1 %collective-permute-start.58 = (bf16[1280,1024]{1,0:T(8,128)(2,1)}, bf16[1280,1024]{1,0:T(8,128)(2,1)}, u32[]{:S(2)}, u32[]{:S(2)}) collective-permute-start(bf16[1280,1024]{1,0:T(8,128)(2,1)} %get-tuple-element.689), channel_id=1, source_target_pairs={{0,4},{4,0},{8,12},{12,8},{16,20},{20,16},{24,28},{28,24},{1,5},{5... | collective-permute-start | bytes 7864328 | tf_op jit(solution)/shard_map/ppermute | solution.py:972
  814.1 39.1 %collective-permute-start.62 = (bf16[640,256]{1,0:T(8,128)(2,1)}, bf16[640,256]{1,0:T(8,128)(2,1)}, u32[]{:S(2)}, u32[]{:S(2)}) collective-permute-start(bf16[640,256]{1,0:T(8,128)(2,1)} %get-tuple-element.375), channel_id=1, source_target_pairs={{0,3},{1,2},{2,1},{3,0},{4,7},{5,6},{6,5},{7,4},{8,11},{9,10},{10,... | collective-permute-start | bytes 983048 | tf_op jit(solution)/shard_map/ppermute | solution.py:984
  852.3 154.5 %collective-permute-start.76 = (bf16[1280,1024]{1,0:T(8,128)(2,1)}, bf16[1280,1024]{1,0:T(8,128)(2,1)}, u32[]{:S(2)}, u32[]{:S(2)}) collective-permute-start(bf16[1280,1024]{1,0:T(8,128)(2,1)} %get-tuple-element.695), channel_id=1, source_target_pairs={{0,4},{4,0},{8,12},{12,8},{16,20},{20,16},{24,28},{28,24},{1,5},{5... | collective-permute-start | bytes 7864328 | tf_op jit(solution)/shard_map/ppermute | solution.py:972
  855.9 44.6 %collective-permute-start.63 = (bf16[2,640,256]{2,1,0:T(8,128)(2,1)}, bf16[2,640,256]{2,1,0:T(8,128)(2,1)}, u32[]{:S(2)}, u32[]{:S(2)}) collective-permute-start(bf16[2,640,256]{2,1,0:T(8,128)(2,1)} %dynamic-slice_bitcast_fusion.1), channel_id=1, source_target_pairs={{0,4},{4,0},{8,12},{12,8},{16,20},{20,16},{24,28},{28,24},{1,5},{5... | collective-permute-start | bytes 1966088 | tf_op jit(solution)/shard_map/ppermute | solution.py:972
  875.7 56.2 %collective-permute-start.88 = (bf16[2,2,256,768]{3,2,1,0:T(8,128)(2,1)}, bf16[2,2,256,768]{3,2,1,0:T(8,128)(2,1)}, u32[]{:S(2)}, u32[]{:S(2)}) collective-permute-start(bf16[2,2,256,768]{3,2,1,0:T(8,128)(2,1)} %bitcast.145), channel_id=1, source_target_pairs={{0,8},{4,12},{8,0},{12,4},{16,24},{20,28},{24,16},{28,20},{1,9},{5... | collective-permute-start | bytes 4718600 | tf_op jit(solution)/shard_map/ppermute | solution.py:977
  876.7 59.1 %collective-permute-start.86 = (bf16[2,2,256,768]{3,2,1,0:T(8,128)(2,1)}, bf16[2,2,256,768]{3,2,1,0:T(8,128)(2,1)}, u32[]{:S(2)}, u32[]{:S(2)}) collective-permute-start(bf16[2,2,256,768]{3,2,1,0:T(8,128)(2,1)} %bitcast.142), channel_id=1, source_target_pairs={{0,16},{4,20},{8,24},{12,28},{16,0},{20,4},{24,8},{28,12},{1,17},{... | collective-permute-start | bytes 4718600 | tf_op jit(solution)/shard_map/ppermute | solution.py:977
  900.5 56.7 %collective-permute-start.84 = (bf16[2,2,512,384]{3,2,1,0:T(8,128)(2,1)S(1)}, bf16[2,2,512,384]{3,2,1,0:T(8,128)(2,1)}, u32[]{:S(2)}, u32[]{:S(2)}) collective-permute-start(bf16[2,2,512,384]{3,2,1,0:T(8,128)(2,1)S(1)} %bitcast.587), channel_id=1, source_target_pairs={{0,16},{4,20},{8,24},{12,28},{16,0},{20,4},{24,8},{28,12},{1,17},{... | collective-permute-start | bytes 4718600 | tf_op jit(solution)/shard_map/ppermute | solution.py:977
  903.7 56.3 %collective-permute-start.85 = (bf16[2,2,512,384]{3,2,1,0:T(8,128)(2,1)S(1)}, bf16[2,2,512,384]{3,2,1,0:T(8,128)(2,1)}, u32[]{:S(2)}, u32[]{:S(2)}) collective-permute-start(bf16[2,2,512,384]{3,2,1,0:T(8,128)(2,1)S(1)} %bitcast.586), channel_id=1, source_target_pairs={{0,8},{4,12},{8,0},{12,4},{16,24},{20,28},{24,16},{28,20},{1,9},{5... | collective-permute-start | bytes 4718600 | tf_op jit(solution)/shard_map/ppermute | solution.py:977
  931.9 60.6 %collective-permute-start.74 = (bf16[320,1536]{1,0:T(8,128)(2,1)}, bf16[320,1536]{1,0:T(8,128)(2,1)}, u32[]{:S(2)}, u32[]{:S(2)}) collective-permute-start(bf16[320,1536]{1,0:T(8,128)(2,1)} %get-tuple-element.693), channel_id=1, source_target_pairs={{0,4},{4,0},{8,12},{12,8},{16,20},{20,16},{24,28},{28,24},{1,5},{5... | collective-permute-start | bytes 2949128 | tf_op jit(solution)/shard_map/ppermute | solution.py:972
  960.0 206.1 %collective-permute-start.94 = (bf16[2,2,384,1024]{3,2,1,0:T(8,128)(2,1)}, bf16[2,2,384,1024]{3,2,1,0:T(8,128)(2,1)}, u32[]{:S(2)}, u32[]{:S(2)}) collective-permute-start(bf16[2,2,384,1024]{3,2,1,0:T(8,128)(2,1)} %bitcast.155), channel_id=1, source_target_pairs={{0,8},{4,12},{8,0},{12,4},{16,24},{20,28},{24,16},{28,20},{1,9},{5... | collective-permute-start | bytes 9437192 | tf_op jit(solution)/shard_map/ppermute | solution.py:977
  964.9 121.9 %collective-permute-start.99 = (bf16[1,2,512,384]{3,2,1,0:T(8,128)(2,1)}, bf16[1,2,512,384]{3,2,1,0:T(8,128)(2,1)}, u32[]{:S(2)}, u32[]{:S(2)}) collective-permute-start(bf16[1,2,512,384]{3,2,1,0:T(8,128)(2,1)} %slice.1248), channel_id=1, source_target_pairs={{0,16},{4,20},{8,24},{12,28},{16,0},{20,4},{24,8},{28,12},{1,17},{... | collective-permute-start | bytes 2359304 | tf_op jit(solution)/shard_map/ppermute | solution.py:977
  976.4 126.4 %collective-permute-start.98 = (bf16[1,2,512,384]{3,2,1,0:T(8,128)(2,1)}, bf16[1,2,512,384]{3,2,1,0:T(8,128)(2,1)}, u32[]{:S(2)}, u32[]{:S(2)}) collective-permute-start(bf16[1,2,512,384]{3,2,1,0:T(8,128)(2,1)} %slice.1249), channel_id=1, source_target_pairs={{0,8},{4,12},{8,0},{12,4},{16,24},{20,28},{24,16},{28,20},{1,9},{5... | collective-permute-start | bytes 2359304 | tf_op jit(solution)/shard_map/ppermute | solution.py:977
  979.0 224.9 %reduce-scatter.11.cloned.1.call-start = ((), (), s32[]{:S(2)}) async-start(), calls=%async_computation.9 | async-start | bytes 1966080 | tf_op jit(solution)/shard_map/reduce_scatter | solution.py:1326
  1003.1 81.3 %collective-permute-start.90 = (bf16[2,2,192,640]{3,2,1,0:T(8,128)(2,1)}, bf16[2,2,192,640]{3,2,1,0:T(8,128)(2,1)}, u32[]{:S(2)}, u32[]{:S(2)}) collective-permute-start(bf16[2,2,192,640]{3,2,1,0:T(8,128)(2,1)} %bitcast.148), channel_id=1, source_target_pairs={{0,16},{4,20},{8,24},{12,28},{16,0},{20,4},{24,8},{28,12},{1,17},{... | collective-permute-start | bytes 2949128 | tf_op jit(solution)/shard_map/ppermute | solution.py:977
  1020.5 61.2 %collective-permute-start.91 = (bf16[2,2,192,640]{3,2,1,0:T(8,128)(2,1)}, bf16[2,2,192,640]{3,2,1,0:T(8,128)(2,1)}, u32[]{:S(2)}, u32[]{:S(2)}) collective-permute-start(bf16[2,2,192,640]{3,2,1,0:T(8,128)(2,1)} %bitcast.150), channel_id=1, source_target_pairs={{0,8},{4,12},{8,0},{12,4},{16,24},{20,28},{24,16},{28,20},{1,9},{5... | collective-permute-start | bytes 2949128 | tf_op jit(solution)/shard_map/ppermute | solution.py:977
  1081.7 64.8 %collective-permute-start.78 = (f32[1280,256]{1,0:T(8,128)}, f32[1280,256]{1,0:T(8,128)}, u32[]{:S(2)}, u32[]{:S(2)}) collective-permute-start(f32[1280,256]{1,0:T(8,128)} %copy-done.76), channel_id=1, source_target_pairs={{0,4},{4,0},{8,12},{12,8},{16,20},{20,16},{24,28},{28,24},{1,5},{5... | collective-permute-start | bytes 3932168 | tf_op jit(solution)/shard_map/ppermute | solution.py:972
  1106.7 118.4 %reduce-scatter.7.cloned.1.call-start = ((), (), s32[]{:S(2)}) async-start(), calls=%async_computation.6 | async-start | bytes 2654208 | tf_op jit(solution)/shard_map/reduce_scatter | solution.py:1539
  1108.9 69.0 %collective-permute-start.92 = (bf16[2,2,384,1024]{3,2,1,0:T(8,128)(2,1)}, bf16[2,2,384,1024]{3,2,1,0:T(8,128)(2,1)}, u32[]{:S(2)}, u32[]{:S(2)}) collective-permute-start(bf16[2,2,384,1024]{3,2,1,0:T(8,128)(2,1)} %bitcast.621), channel_id=1, source_target_pairs={{0,16},{4,20},{8,24},{12,28},{16,0},{20,4},{24,8},{28,12},{1,17},{... | collective-permute-start | bytes 9437192 | tf_op jit(solution)/shard_map/ppermute | solution.py:977
  1158.9 50.0 %collective-permute-start.79 = (bf16[1280,1024]{1,0:T(8,128)(2,1)}, bf16[1280,1024]{1,0:T(8,128)(2,1)}, u32[]{:S(2)}, u32[]{:S(2)}) collective-permute-start(bf16[1280,1024]{1,0:T(8,128)(2,1)} %get-tuple-element.699), channel_id=1, source_target_pairs={{0,4},{4,0},{8,12},{12,8},{16,20},{20,16},{24,28},{28,24},{1,5},{5... | collective-permute-start | bytes 7864328 | tf_op jit(solution)/shard_map/ppermute | solution.py:972
  1164.1 321.4 %all-reduce.20.cloned.1.call-start = ((), (), s32[]{:S(2)}) async-start(), calls=%async_computation.4 | async-start | bytes 229376 | tf_op jit(solution)/shard_map/psum | solution.py:1793
  1174.7 46.3 %collective-permute-start.95 = (bf16[1,2,384,1024]{3,2,1,0:T(8,128)(2,1)}, bf16[1,2,384,1024]{3,2,1,0:T(8,128)(2,1)}, u32[]{:S(2)}, u32[]{:S(2)}) collective-permute-start(bf16[1,2,384,1024]{3,2,1,0:T(8,128)(2,1)} %slice.1240), channel_id=1, source_target_pairs={{0,16},{4,20},{8,24},{12,28},{16,0},{20,4},{24,8},{28,12},{1,17},{... | collective-permute-start | bytes 4718600 | tf_op jit(solution)/shard_map/ppermute | solution.py:977
  1185.2 43.0 %collective-permute-start.93 = (bf16[1,2,384,1024]{3,2,1,0:T(8,128)(2,1)}, bf16[1,2,384,1024]{3,2,1,0:T(8,128)(2,1)}, u32[]{:S(2)}, u32[]{:S(2)}) collective-permute-start(bf16[1,2,384,1024]{3,2,1,0:T(8,128)(2,1)} %slice.1241), channel_id=1, source_target_pairs={{0,8},{4,12},{8,0},{12,4},{16,24},{20,28},{24,16},{28,20},{1,9},{5... | collective-permute-start | bytes 4718600 | tf_op jit(solution)/shard_map/ppermute | solution.py:977
  1189.5 83.4 %collective-permute-start.102 = (bf16[2,2,384,640]{3,2,1,0:T(8,128)(2,1)}, bf16[2,2,384,640]{3,2,1,0:T(8,128)(2,1)}, u32[]{:S(2)}, u32[]{:S(2)}) collective-permute-start(bf16[2,2,384,640]{3,2,1,0:T(8,128)(2,1)} %bitcast.167), channel_id=1, source_target_pairs={{0,8},{4,12},{8,0},{12,4},{16,24},{20,28},{24,16},{28,20},{1,9},{5... | collective-permute-start | bytes 5898248 | tf_op jit(solution)/shard_map/ppermute | solution.py:977
  1201.1 74.9 %collective-permute-start.100 = (bf16[2,2,384,640]{3,2,1,0:T(8,128)(2,1)}, bf16[2,2,384,640]{3,2,1,0:T(8,128)(2,1)}, u32[]{:S(2)}, u32[]{:S(2)}) collective-permute-start(bf16[2,2,384,640]{3,2,1,0:T(8,128)(2,1)} %bitcast.164), channel_id=1, source_target_pairs={{0,16},{4,20},{8,24},{12,28},{16,0},{20,4},{24,8},{28,12},{1,17},{... | collective-permute-start | bytes 5898248 | tf_op jit(solution)/shard_map/ppermute | solution.py:977
  1219.1 266.5 %all-reduce.22.cloned.1.call-start = ((), (), s32[]{:S(2)}) async-start(), calls=%async_computation.7 | async-start | bytes 589824 | tf_op jit(solution)/shard_map/psum | solution.py:1539
  1225.1 304.0 %reduce-scatter.9.cloned.1.call-start = ((), (), s32[]{:S(2)}) async-start(), calls=%async_computation.8 | async-start | bytes 3932160 | tf_op jit(solution)/shard_map/reduce_scatter | solution.py:1326
  1239.3 48.1 %collective-permute-start.97 = (bf16[2,2,128,384]{3,2,1,0:T(8,128)(2,1)S(1)}, bf16[2,2,128,384]{3,2,1,0:T(8,128)(2,1)}, u32[]{:S(2)}, u32[]{:S(2)}) collective-permute-start(bf16[2,2,128,384]{3,2,1,0:T(8,128)(2,1)S(1)} %bitcast.592), channel_id=1, source_target_pairs={{0,8},{4,12},{8,0},{12,4},{16,24},{20,28},{24,16},{28,20},{1,9},{5... | collective-permute-start | bytes 1179656 | tf_op jit(solution)/shard_map/ppermute | solution.py:977
  1288.7 55.5 %collective-permute-start.116 = (bf16[2,2,256,256]{3,2,1,0:T(8,128)(2,1)S(1)}, bf16[2,2,256,256]{3,2,1,0:T(8,128)(2,1)S(1)}, u32[]{:S(2)}, u32[]{:S(2)}) collective-permute-start(bf16[2,2,256,256]{3,2,1,0:T(8,128)(2,1)S(1)} %bitcast.590), channel_id=1, source_target_pairs={{0,16},{4,20},{8,24},{12,28},{16,0},{20,4},{24,8},{28,12},{1,17},{... | collective-permute-start | bytes 1572872 | tf_op jit(solution)/shard_map/ppermute | solution.py:977
  1332.6 58.8 %collective-permute-start.103 = (bf16[1,2,384,640]{3,2,1,0:T(8,128)(2,1)}, bf16[1,2,384,640]{3,2,1,0:T(8,128)(2,1)S(1)}, u32[]{:S(2)}, u32[]{:S(2)}) collective-permute-start(bf16[1,2,384,640]{3,2,1,0:T(8,128)(2,1)} %slice.1242), channel_id=1, source_target_pairs={{0,16},{4,20},{8,24},{12,28},{16,0},{20,4},{24,8},{28,12},{1,17},{... | collective-permute-start | bytes 2949128 | tf_op jit(solution)/shard_map/ppermute | solution.py:977
  1342.8 48.9 %collective-permute-start.101 = (bf16[1,2,384,640]{3,2,1,0:T(8,128)(2,1)}, bf16[1,2,384,640]{3,2,1,0:T(8,128)(2,1)S(1)}, u32[]{:S(2)}, u32[]{:S(2)}) collective-permute-start(bf16[1,2,384,640]{3,2,1,0:T(8,128)(2,1)} %slice.1243), channel_id=1, source_target_pairs={{0,8},{4,12},{8,0},{12,4},{16,24},{20,28},{24,16},{28,20},{1,9},{5... | collective-permute-start | bytes 2949128 | tf_op jit(solution)/shard_map/ppermute | solution.py:977
  1378.4 42.5 %collective-permute-start.83 = (bf16[2,640,256]{2,1,0:T(8,128)(2,1)S(1)}, bf16[2,640,256]{2,1,0:T(8,128)(2,1)}, u32[]{:S(2)}, u32[]{:S(2)}) collective-permute-start(bf16[2,640,256]{2,1,0:T(8,128)(2,1)S(1)} %dynamic-slice_bitcast_fusion), channel_id=1, source_target_pairs={{0,4},{4,0},{8,12},{12,8},{16,20},{20,16},{24,28},{28,24},{1,5},{5... | collective-permute-start | bytes 1966088 | tf_op jit(solution)/shard_map/ppermute | solution.py:972
  1393.3 60.6 %collective-permute-start.133 = (bf16[384,640]{1,0:T(8,128)(2,1)}, bf16[384,640]{1,0:T(8,128)(2,1)}, u32[]{:S(2)}, u32[]{:S(2)}) collective-permute-start(bf16[384,640]{1,0:T(8,128)(2,1)} %get-tuple-element.364), channel_id=1, source_target_pairs={{0,2},{1,3},{2,0},{3,1},{4,6},{5,7},{6,4},{7,5},{8,10},{9,11},{10,... | collective-permute-start | bytes 1474568 | tf_op jit(solution)/shard_map/ppermute | solution.py:984
  1393.5 60.3 %collective-permute-start.132 = (bf16[384,640]{1,0:T(8,128)(2,1)S(1)}, bf16[384,640]{1,0:T(8,128)(2,1)}, u32[]{:S(2)}, u32[]{:S(2)}) collective-permute-start(bf16[384,640]{1,0:T(8,128)(2,1)S(1)} %get-tuple-element.363), channel_id=1, source_target_pairs={{0,1},{1,0},{2,3},{3,2},{4,5},{5,4},{6,7},{7,6},{8,9},{9,8},{10,11... | collective-permute-start | bytes 1474568 | tf_op jit(solution)/shard_map/ppermute | solution.py:984
  1420.8 39.6 %collective-permute-start.106 = (bf16[2,2,256,768]{3,2,1,0:T(8,128)(2,1)S(1)}, bf16[2,2,256,768]{3,2,1,0:T(8,128)(2,1)S(1)}, u32[]{:S(2)}, u32[]{:S(2)}) collective-permute-start(bf16[2,2,256,768]{3,2,1,0:T(8,128)(2,1)S(1)} %bitcast.582), channel_id=1, source_target_pairs={{0,8},{4,12},{8,0},{12,4},{16,24},{20,28},{24,16},{28,20},{1,9},{5... | collective-permute-start | bytes 4718600 | tf_op jit(solution)/shard_map/ppermute | solution.py:977
  1484.5 41.6 %collective-permute-start.109 = (bf16[256,768]{1,0:T(8,128)(2,1)}, bf16[256,768]{1,0:T(8,128)(2,1)}, u32[]{:S(2)}, u32[]{:S(2)}) collective-permute-start(bf16[256,768]{1,0:T(8,128)(2,1)} %get-tuple-element.367), channel_id=1, source_target_pairs={{0,2},{1,3},{2,0},{3,1},{4,6},{5,7},{6,4},{7,5},{8,10},{9,11},{10,... | collective-permute-start | bytes 1179656 | tf_op jit(solution)/shard_map/ppermute | solution.py:984
  1484.5 41.6 %collective-permute-start.108 = (bf16[256,768]{1,0:T(8,128)(2,1)}, bf16[256,768]{1,0:T(8,128)(2,1)}, u32[]{:S(2)}, u32[]{:S(2)}) collective-permute-start(bf16[256,768]{1,0:T(8,128)(2,1)} %get-tuple-element.366), channel_id=1, source_target_pairs={{0,1},{1,0},{2,3},{3,2},{4,5},{5,4},{6,7},{7,6},{8,9},{9,8},{10,11... | collective-permute-start | bytes 1179656 | tf_op jit(solution)/shard_map/ppermute | solution.py:984
  (410 other events, 5335.2 us)
Sparse Core Ops, SparseCore 0:
  28.6 30.7 all-gather.13
  96.8 35.5 all-gather.15
  140.2 43.6 all-gather.17
  278.9 62.7 all-gather.19
  355.1 38.0 all-gather.21
  464.9 41.6 all-gather.23
  979.1 35.2 reduce-scatter.4
  1106.8 40.5 reduce-scatter.10
  1164.2 50.6 reduce-scatter.6
  1221.9 149.1 all-reduce.19
  1373.6 53.1 all-reduce.21
  1429.0 77.7 reduce-scatter.8
